TPU v7x, 32 devices: a whole 2x2x4 slice. The times are simulated.
32 devices in a mesh: seq: 8 (over z, y), head: 4 (over x, core).
Axes of the slice: x: 2, y: 2, z: 4, core: 2. Of those that a mesh axis runs over, the one named last changes fastest.
Arguments:
- query: bfloat16 [4096, 2048], P('seq', 'head'), may hold values from -6 to 6
- keys: bfloat16 [4096, 2048], P('seq', 'head'), may hold values from -6 to 6
- values: bfloat16 [4096, 4096], P('seq', 'head'), may hold values from -6 to 6
- gate_logit: float32 [4096, 32], P('seq', 'head'), may hold values from -17 to 1.5
- beta_logit: float32 [4096, 32], P('seq', 'head'), may hold values from -9 to 6
- decay_rate: float32 [32], P('head'), may hold values from 0.5 to 8
- norm_gain: float32 [128], replicated, may hold values from 0.1 to 1.9
- gate_z: bfloat16 [4096, 4096], P('seq', 'head'), may hold values from -6 to 6
- out_weight: bfloat16 [4096, 2048], P('head'), may hold values from -0.09375 to 0.09375
Outputs:
- mixed: bfloat16 [4096, 2048], P(('seq', 'head'))
All inputs are finite; a program needn't handle non-finite values.
Results may differ from a plain program's by a relative error of at most 0.014.
Values may be sent and summed in bfloat16 or wider, within the bound.
No kernel may reach another device: no remote copies, remote signals or barrier semaphores. Data moves between devices by JAX's collectives and lax.ppermute only.
A program may use at most 128 MiB of HBM per device.

v0:
```python
import jax
import jax.numpy as jnp
from jax import lax
from jax.sharding import PartitionSpec as P

DK = 128
DV = 128
SPAN = 64


def passed_along(shard, axis, by):
    size = lax.axis_size(axis)
    pairs = [(i, i + by) for i in range(size) if 0 <= i + by < size]
    return lax.ppermute(shard, axis, pairs)


def unit_norm(values_in):
    return values_in * lax.rsqrt(jnp.sum(values_in * values_in, axis=-1, keepdims=True) + 1e-06)


def block_terms(query, keys, values, logdecay, beta):
    highest = lax.Precision.HIGHEST
    size = logdecay.shape[-1]
    width = keys.shape[-1]
    cumul = jnp.cumsum(logdecay, axis=-1)
    differ = cumul[..., :, None] - cumul[..., None, :]
    row_ids = lax.broadcasted_iota(jnp.int32, (size, size), 0)
    col_ids = lax.broadcasted_iota(jnp.int32, (size, size), 1)
    inclusive = col_ids <= row_ids
    strict = col_ids < row_ids
    ratio = jnp.where(inclusive, jnp.exp(jnp.where(inclusive, differ, 0.0)), 0.0)
    key_key = jnp.einsum("...te,...se->...ts", keys, keys, precision=highest)
    query_key = jnp.einsum("...te,...se->...ts", query, keys, precision=highest)
    lower = jnp.where(strict, beta[..., :, None] * ratio * key_key, 0.0) + jnp.eye(
        size, dtype=jnp.float32
    )
    rhs_values = beta[..., None] * values
    rhs_keys = (beta * jnp.exp(cumul))[..., None] * keys
    update = lax.linalg.triangular_solve(
        lower, rhs_values, left_side=True, lower=True, unit_diagonal=True
    )
    weights = lax.linalg.triangular_solve(
        lower, rhs_keys, left_side=True, lower=True, unit_diagonal=True
    )
    mixing = ratio * query_key
    decayed_query = jnp.exp(cumul)[..., None] * query
    key_end = jnp.exp(cumul[..., -1:] - cumul)[..., None] * keys
    transit = jnp.exp(cumul[..., -1])[..., None, None] * jnp.eye(width, dtype=jnp.float32)
    transit = transit - jnp.einsum("...se,...sf->...ef", key_end, weights, precision=highest)
    inject = jnp.einsum("...se,...sf->...ef", key_end, update, precision=highest)
    return (update, weights, mixing, decayed_query, transit, inject)


def run_blocks(terms, start):
    highest = lax.Precision.HIGHEST

    def advance(state, item):
        update, weights, mixing, decayed_query, transit, inject = item
        resid = update - jnp.einsum("...ce,...ef->...cf", weights, state, precision=highest)
        result = jnp.einsum("...ce,...ef->...cf", decayed_query, state, precision=highest)
        result = result + jnp.einsum("...ts,...sf->...tf", mixing, resid, precision=highest)
        state = jnp.einsum("...ef,...fg->...eg", transit, state, precision=highest) + inject
        return (state, result)

    return lax.scan(advance, start, terms)


def matmul_heads(left, right):
    return jnp.einsum("hef,hfg->heg", left, right, precision=lax.Precision.HIGHEST)


def on_device(
    query, keys, values, gate_logit, beta_logit, decay_rate, norm_gain, gate_z, out_weight
):
    tok_rows = query.shape[0]
    local_heads = values.shape[1] // DV
    key_heads = query.shape[1] // DK
    blocks = tok_rows // SPAN

    def to_blocks(array, width):
        return array.reshape(blocks, SPAN, local_heads, width).transpose(0, 2, 1, 3)

    qn = jnp.repeat(
        unit_norm(query.astype(jnp.float32).reshape(tok_rows, key_heads, DK)), 2, axis=1
    )
    kn = jnp.repeat(unit_norm(keys.astype(jnp.float32).reshape(tok_rows, key_heads, DK)), 2, axis=1)
    vals = values.astype(jnp.float32).reshape(tok_rows, local_heads, DV)
    logdecay = -decay_rate[None, :] * jax.nn.softplus(gate_logit)
    beta = jax.nn.sigmoid(beta_logit)
    terms = block_terms(
        to_blocks(qn, DK),
        to_blocks(kn, DK),
        to_blocks(vals, DV),
        logdecay.reshape(blocks, SPAN, local_heads).transpose(0, 2, 1),
        beta.reshape(blocks, SPAN, local_heads).transpose(0, 2, 1),
    )
    ident = jnp.broadcast_to(jnp.eye(DK, dtype=jnp.float32), (local_heads, DK, DK))
    zeros = jnp.zeros((local_heads, DK, DV), jnp.float32)

    def compose(carry, item):
        transit, inject = item
        return ((matmul_heads(transit, carry[0]), matmul_heads(transit, carry[1]) + inject), None)

    (shard_transit, shard_inject), unused = lax.scan(compose, (ident, zeros), (terms[4], terms[5]))

    def relay(step, carry):
        ending = matmul_heads(shard_transit, carry) + shard_inject
        return passed_along(ending, "seq", 1)

    start = lax.fori_loop(0, lax.axis_size("seq") - 1, relay, zeros)
    final, outs = run_blocks(terms, start)
    core = outs.transpose(0, 2, 1, 3).reshape(tok_rows, local_heads, DV)
    gate = jax.nn.silu(gate_z.astype(jnp.float32).reshape(tok_rows, local_heads, DV))
    scale = lax.rsqrt(jnp.mean(core * core, axis=-1, keepdims=True) + 1e-06)
    gated = (
        (core * scale * norm_gain * gate).astype(jnp.bfloat16).reshape(tok_rows, local_heads * DV)
    )
    rows = lax.all_to_all(gated, "head", split_axis=0, concat_axis=1, tiled=True)
    mixed = jnp.dot(
        rows,
        lax.all_gather(out_weight, "head", axis=0, tiled=True),
        preferred_element_type=jnp.float32,
    )
    return mixed.astype(jnp.bfloat16)


def solution(mesh):
    return jax.shard_map(
        on_device,
        mesh=mesh,
        in_specs=(
            P("seq", "head"),
            P("seq", "head"),
            P("seq", "head"),
            P("seq", "head"),
            P("seq", "head"),
            P("head"),
            P(),
            P("seq", "head"),
            P("head", None),
        ),
        out_specs=P(("seq", "head"), None),
        check_vma=False,
    )
```

profile of v0, /device:TPU:0, one launch (start us, length us, event | category | flops | bytes accessed | tf_op | source)
XLA Modules:
  0.0 600.9 jit_solution(1133894775231314642)
XLA Ops:
  7.6 1.8 reduce_window_sum.11
  11.6 4.9 add_bitcast_fusion
  16.6 316.0 %custom-call.5 = f32[8,8,1,64,64]{3,4,2,1,0:T(8,128)} custom-call(f32[8,8,1,64,64]{4,3,2,1,0:T(8,128)} %add_bitcast_fusion), custom_call_target="InvertDiagBlocksLowerTriangular" | custom-call | tf_op jit(solution)/shard_map/triangular_solve/custom-call.1 | solution.py:42
  334.0 1.8 copy.85
  337.1 1.9 multiply_reduce_fusion.1
  340.0 2.0 broadcast_multiply_fusion
  343.5 3.6 fusion.33
  347.2 4.1 fusion.31
  351.3 4.8 fusion.39
  356.1 8.5 %fusion.41 = f32[8,8,128,128]{3,2,1,0:T(8,128)} fusion(f32[8,8,64,128]{3,2,1,0:T(8,128)S(1)} %fusion.31, f32[8,8,64,128]{3,2,0,1:T(8,128)S(1)} %get-tuple-element.188), kind=kOutput, calls=%fused_computation.56 | convolution fusion | flops 805306368 | bytes 8388608 | tf_op jit(solution)/shard_map/...se,...sf->...ef/dot_general | solution.py:50
  364.6 8.7 %multiply_subtract_fusion = f32[8,8,128,128]{3,2,1,0:T(8,128)} fusion(f32[8,8,64,128]{3,2,1,0:T(8,128)S(1)} %fusion.33, f32[128,128]{1,0:T(8,128)S(1)} %fusion.54, f32[8,8]{1,0:T(8,128)S(1)} %exp.38, f32[8,8,64,128]{3,2,0,1:T(8,128)S(1)} %get-tuple-element.188), kind=kOutput, calls=%fused_computation.31 | convolution fusion | flops 807403520 | bytes 8454400 | tf_op jit(solution)/shard_map/...se,...sf->...ef/dot_general | solution.py:49
  373.4 29.6 %while.37 = (s32[]{:T(128)}, f32[8,128,128]{2,1,0:T(8,128)S(1)}, f32[8,128,128]{2,1,0:T(8,128)S(1)}, f32[8,8,128,128]{3,2,1,0:T(8,128)}, f32[8,8,128,128]{3,2,1,0:T(8,128)}, /*index=5*/s32[]{:T(128)}, s32[]{:T(128)}) while((s32[]{:T(128)}, f32[8,128,128]{2,1,0:T(8,128)S(1)}, f32[8,128,128]{2,1,0:T(8,128)S(1)}, ...), condition=%wide.region_3.5_spmd.clone, body=%wide.region_2.0_spmd.clone.sunk | while | flops 402915328 | bytes 5768791 | solution.py:104
  373.4 1.9 convolution_add_fusion.9
  375.3 1.7 fusion.104
  377.1 1.9 convolution_add_fusion.9
  379.0 1.7 fusion.104
  380.8 1.9 convolution_add_fusion.9
  382.7 1.7 fusion.104
  384.5 1.9 convolution_add_fusion.9
  386.4 1.7 fusion.104
  388.2 1.9 convolution_add_fusion.9
  390.2 1.7 fusion.104
  391.9 1.9 convolution_add_fusion.9
  393.9 1.7 fusion.104
  395.6 1.9 convolution_add_fusion.9
  397.6 1.7 fusion.104
  399.3 1.9 convolution_add_fusion.9
  401.3 1.7 fusion.104
  403.0 99.6 %while.35 = (s32[]{:T(128)}, f32[8,128,128]{2,1,0:T(8,128)S(1)}, f32[8,128,128]{2,1,0:T(8,128)S(1)}, f32[8,128,128]{2,1,0:T(8,128)S(1)}, s32[]{:T(128)}) while((s32[]{:T(128)}, f32[8,128,128]{2,1,0:T(8,128)S(1)}, f32[8,128,128]{2,1,0:T(8,128)S(1)}, f32[8,128,128]{2,1,0:T(8,128)S(1)}, s32[]{:T(128)}) %tuple.60), condition=%wide.region_5.7_spmd, body=%wide.region_4.6_spmd.sunk | while | flops 201457664 | bytes 4194405 | solution.py:110
  403.7 4.9 collective-permute-start
  408.6 11.1 %collective-permute-done = f32[8,128,128]{2,1,0:T(8,128)S(1)} collective-permute-done((f32[8,128,128]{2,1,0:T(8,128)S(1)}, f32[8,128,128]{2,1,0:T(8,128)S(1)}, u32[]{:S(2)}, u32[]{:S(2)}) %collective-permute-start) | collective-permute-done | bytes 524320 | tf_op jit(solution)/shard_map/while/body/eval_jaxpr/ppermute | solution.py:14
  420.4 4.4 collective-permute-start
  424.9 10.3 %collective-permute-done = f32[8,128,128]{2,1,0:T(8,128)S(1)} collective-permute-done((f32[8,128,128]{2,1,0:T(8,128)S(1)}, f32[8,128,128]{2,1,0:T(8,128)S(1)}, u32[]{:S(2)}, u32[]{:S(2)}) %collective-permute-start) | collective-permute-done | bytes 524320 | tf_op jit(solution)/shard_map/while/body/eval_jaxpr/ppermute | solution.py:14
  435.8 4.4 collective-permute-start
  440.2 9.3 %collective-permute-done = f32[8,128,128]{2,1,0:T(8,128)S(1)} collective-permute-done((f32[8,128,128]{2,1,0:T(8,128)S(1)}, f32[8,128,128]{2,1,0:T(8,128)S(1)}, u32[]{:S(2)}, u32[]{:S(2)}) %collective-permute-start) | collective-permute-done | bytes 524320 | tf_op jit(solution)/shard_map/while/body/eval_jaxpr/ppermute | solution.py:14
  450.2 5.2 collective-permute-start
  455.5 8.4 %collective-permute-done = f32[8,128,128]{2,1,0:T(8,128)S(1)} collective-permute-done((f32[8,128,128]{2,1,0:T(8,128)S(1)}, f32[8,128,128]{2,1,0:T(8,128)S(1)}, u32[]{:S(2)}, u32[]{:S(2)}) %collective-permute-start) | collective-permute-done | bytes 524320 | tf_op jit(solution)/shard_map/while/body/eval_jaxpr/ppermute | solution.py:14
  464.6 5.3 collective-permute-start
  469.9 7.5 %collective-permute-done = f32[8,128,128]{2,1,0:T(8,128)S(1)} collective-permute-done((f32[8,128,128]{2,1,0:T(8,128)S(1)}, f32[8,128,128]{2,1,0:T(8,128)S(1)}, u32[]{:S(2)}, u32[]{:S(2)}) %collective-permute-start) | collective-permute-done | bytes 524320 | tf_op jit(solution)/shard_map/while/body/eval_jaxpr/ppermute | solution.py:14
  478.0 5.3 collective-permute-start
  483.4 6.6 %collective-permute-done = f32[8,128,128]{2,1,0:T(8,128)S(1)} collective-permute-done((f32[8,128,128]{2,1,0:T(8,128)S(1)}, f32[8,128,128]{2,1,0:T(8,128)S(1)}, u32[]{:S(2)}, u32[]{:S(2)}) %collective-permute-start) | collective-permute-done | bytes 524320 | tf_op jit(solution)/shard_map/while/body/eval_jaxpr/ppermute | solution.py:14
  490.7 5.3 collective-permute-start
  496.0 6.6 %collective-permute-done = f32[8,128,128]{2,1,0:T(8,128)S(1)} collective-permute-done((f32[8,128,128]{2,1,0:T(8,128)S(1)}, f32[8,128,128]{2,1,0:T(8,128)S(1)}, u32[]{:S(2)}, u32[]{:S(2)}) %collective-permute-start) | collective-permute-done | bytes 524320 | tf_op jit(solution)/shard_map/while/body/eval_jaxpr/ppermute | solution.py:14
  502.7 58.1 %while.36 = (s32[]{:T(128)}, f32[8,128,128]{2,1,0:T(8,128)S(1)}, f32[8,8,64,128]{3,2,1,0:T(8,128)}, f32[8,8,128,128]{3,2,1,0:T(8,128)}, f32[8,8,128,128]{3,2,1,0...) while((s32[]{:T(128)}, f32[8,128,128]{2,1,0:T(8,128)S(1)}, ...), condition=%wide.region_8.10_spmd, body=%wide.region_7.9_spmd.sunk | while | flops 453246976 | bytes 6557285 | solution.py:65
  505.9 2.1 fusion.99
  508.0 1.9 convolution_add_fusion.8
  513.2 2.1 fusion.99
  515.2 1.9 convolution_add_fusion.8
  517.2 1.6 convolution_subtract_fusion.2
  520.4 2.1 fusion.99
  522.5 1.9 convolution_add_fusion.8
  527.6 2.0 fusion.99
  529.7 1.9 convolution_add_fusion.8
  534.9 2.1 fusion.99
  536.9 1.9 convolution_add_fusion.8
  542.1 2.0 fusion.99
  544.1 1.9 convolution_add_fusion.8
  549.3 2.0 fusion.99
  551.4 1.9 convolution_add_fusion.8
  556.5 2.1 fusion.99
  558.6 1.9 convolution_add_fusion.8
  560.8 2.4 multiply_reduce_fusion
  567.7 17.0 %all_to_all.19 = bf16[4,128,1024]{1,2,0:T(8,128)(2,1)S(1)} all-to-all(bf16[4,128,1024]{1,2,0:T(8,128)(2,1)S(1)} %copy.79), channel_id=1, replica_groups=mesh['seq'=8,'head'=4] {'head'}, dimensions={0} | all-to-all | bytes 2097152 | tf_op jit(solution)/shard_map/all_to_all | solution.py:118
  584.7 9.0 %convolution_convert_fusion = bf16[128,2048]{1,0:T(8,128)(2,1)} fusion(bf16[128,4096]{0,1:T(8,128)(2,1)S(1)} %bitcast.143, bf16[4096,2048]{1,0:T(8,128)(2,1)} %all-gather.2.cloned.1.call-done), kind=kOutput, calls=%fused_computation.34 | convolution fusion | flops 2147745792 | bytes 18350080 | tf_op jit(solution)/shard_map/dot_general | solution.py:119
  (117 shorter events, 42.5 us)
Async XLA Ops:
  6.5 557.9 %copy-start = (f32[128]{0:T(128)S(1)}, f32[128]{0:T(128)}, u32[]{:S(2)}) copy-start(f32[128]{0:T(128)} %param.23) | copy-start | bytes 1540
  6.5 0.8 copy-start.12
  6.5 0.8 copy-start.10
  6.5 1.0 copy-start.11
  6.5 3.1 copy-start.8
  6.5 578.1 %all-gather.2.cloned.1.call-start = ((), (), s32[]{:S(2)}) async-start(), calls=%async_computation.1 | async-start | bytes 20971520 | tf_op jit(solution)/shard_map/all_gather | solution.py:121
  334.0 1.8 copy-start.9
  337.1 2.0 copy-start.3
  341.9 1.6 copy-start.4
  343.5 3.6 copy-start.5
  347.2 17.4 %copy-start.1 = (f32[8,8,64,128]{3,2,1,0:T(8,128)}, f32[8,8,64,128]{3,2,1,0:T(8,128)S(1)}, u32[]{:S(2)}) copy-start(f32[8,8,64,128]{3,2,1,0:T(8,128)S(1)} %fusion.33) | copy-start | bytes 6291460
  351.2 4.8 copy-start.2
  403.7 16.0 %collective-permute-start = (f32[8,128,128]{2,1,0:T(8,128)S(1)}, f32[8,128,128]{2,1,0:T(8,128)S(1)}, u32[]{:S(2)}, u32[]{:S(2)}) collective-permute-start(f32[8,128,128]{2,1,0:T(8,128)S(1)} %convolution_add_fusion.7), channel_id=1, source_target_pairs={{0,4},{4,8},{8,12},{12,16},{16,20},{20,24},{24,28},{1,5},{5,9},{9,... | collective-permute-start | bytes 1572872 | tf_op jit(solution)/shard_map/while/body/eval_jaxpr/ppermute | solution.py:14
  420.4 14.7 %collective-permute-start = (f32[8,128,128]{2,1,0:T(8,128)S(1)}, f32[8,128,128]{2,1,0:T(8,128)S(1)}, u32[]{:S(2)}, u32[]{:S(2)}) collective-permute-start(f32[8,128,128]{2,1,0:T(8,128)S(1)} %convolution_add_fusion.7), channel_id=1, source_target_pairs={{0,4},{4,8},{8,12},{12,16},{16,20},{20,24},{24,28},{1,5},{5,9},{9,... | collective-permute-start | bytes 1572872 | tf_op jit(solution)/shard_map/while/body/eval_jaxpr/ppermute | solution.py:14
  435.8 13.8 %collective-permute-start = (f32[8,128,128]{2,1,0:T(8,128)S(1)}, f32[8,128,128]{2,1,0:T(8,128)S(1)}, u32[]{:S(2)}, u32[]{:S(2)}) collective-permute-start(f32[8,128,128]{2,1,0:T(8,128)S(1)} %convolution_add_fusion.7), channel_id=1, source_target_pairs={{0,4},{4,8},{8,12},{12,16},{16,20},{20,24},{24,28},{1,5},{5,9},{9,... | collective-permute-start | bytes 1572872 | tf_op jit(solution)/shard_map/while/body/eval_jaxpr/ppermute | solution.py:14
  450.2 13.7 %collective-permute-start = (f32[8,128,128]{2,1,0:T(8,128)S(1)}, f32[8,128,128]{2,1,0:T(8,128)S(1)}, u32[]{:S(2)}, u32[]{:S(2)}) collective-permute-start(f32[8,128,128]{2,1,0:T(8,128)S(1)} %convolution_add_fusion.7), channel_id=1, source_target_pairs={{0,4},{4,8},{8,12},{12,16},{16,20},{20,24},{24,28},{1,5},{5,9},{9,... | collective-permute-start | bytes 1572872 | tf_op jit(solution)/shard_map/while/body/eval_jaxpr/ppermute | solution.py:14
  464.6 12.8 %collective-permute-start = (f32[8,128,128]{2,1,0:T(8,128)S(1)}, f32[8,128,128]{2,1,0:T(8,128)S(1)}, u32[]{:S(2)}, u32[]{:S(2)}) collective-permute-start(f32[8,128,128]{2,1,0:T(8,128)S(1)} %convolution_add_fusion.7), channel_id=1, source_target_pairs={{0,4},{4,8},{8,12},{12,16},{16,20},{20,24},{24,28},{1,5},{5,9},{9,... | collective-permute-start | bytes 1572872 | tf_op jit(solution)/shard_map/while/body/eval_jaxpr/ppermute | solution.py:14
  478.0 12.0 %collective-permute-start = (f32[8,128,128]{2,1,0:T(8,128)S(1)}, f32[8,128,128]{2,1,0:T(8,128)S(1)}, u32[]{:S(2)}, u32[]{:S(2)}) collective-permute-start(f32[8,128,128]{2,1,0:T(8,128)S(1)} %convolution_add_fusion.7), channel_id=1, source_target_pairs={{0,4},{4,8},{8,12},{12,16},{16,20},{20,24},{24,28},{1,5},{5,9},{9,... | collective-permute-start | bytes 1572872 | tf_op jit(solution)/shard_map/while/body/eval_jaxpr/ppermute | solution.py:14
  490.7 12.0 %collective-permute-start = (f32[8,128,128]{2,1,0:T(8,128)S(1)}, f32[8,128,128]{2,1,0:T(8,128)S(1)}, u32[]{:S(2)}, u32[]{:S(2)}) collective-permute-start(f32[8,128,128]{2,1,0:T(8,128)S(1)} %convolution_add_fusion.7), channel_id=1, source_target_pairs={{0,4},{4,8},{8,12},{12,16},{16,20},{20,24},{24,28},{1,5},{5,9},{9,... | collective-permute-start | bytes 1572872 | tf_op jit(solution)/shard_map/while/body/eval_jaxpr/ppermute | solution.py:14
  560.8 2.5 copy-start.6
  564.5 1.2 copy-start.7
Sparse Core Ops, SparseCore 0:
  8.9 108.7 all-gather.1
where the time goes:
time: 611 us; the launch traced here: 601 us
  other arithmetic  330 us (54%)
  matrix products  134 us (22%)
  waiting for transfers between devices  60.6 us (10%)
  starting transfers between devices  35 us (6%)
  blocking collectives  17 us (3%)
  between operations  14.2 us (2%)
  local copies, waits for them, and re-layouts  8.51 us (1%)
    another operation x4, other arithmetic, block_terms(): lax.linalg.triangular_solve(lower, rhs_keys, left_side=True, lower=True,...  316 us
    ppermute x7, waiting for transfers between devices, passed_along(): return lax.ppermute(shard, axis, pairs)  59.9 us
    ppermute x7, starting transfers between devices, passed_along(): return lax.ppermute(shard, axis, pairs)  34.9 us
    dot_general x23, matrix products, matmul_heads(): jnp.einsum('hef,hfg->heg', left, right, precision=lax.Precision.HIGHEST)  33.3 us
    all_to_all x1, blocking collectives, on_device(): lax.all_to_all(gated, 'head', split_axis=0, concat_axis=1, tiled=True)  17 us
    dot_general x8, matrix products, advance(): jnp.einsum('...ts,...sf->...tf', mixing, resid, precision=highest)  16.4 us
    dot_general x8, matrix products, advance(): jnp.einsum('...ef,...fg->...eg', transit, state, precision=highest) + inject  15.1 us
    dot_general x8, matrix products, advance(): jnp.einsum('...ce,...ef->...cf', weights, state, precision=highest)  13.2 us
  transfers between devices with their start and end apart: 8, of which 7 were waited for; matrix products, arithmetic and copies ran while one was open for 77% of the time, Pallas kernels for 0%

commit v1 on v0

v1 whole, which is shorter than its diff:
```python
import functools

import jax
import jax.numpy as jnp
from jax import lax
from jax.experimental import pallas as pl
from jax.experimental.pallas import tpu as pltpu
from jax.sharding import PartitionSpec as P

DK = 128
DV = 128
CHUNK = 256
F32 = jnp.float32
BF16 = jnp.bfloat16
NEG = -1e30
VMEM_BYTES = 56 * 1024 * 1024


def mm(left, right):
    return lax.dot_general(left, right, (((1,), (0,)), ((), ())), preferred_element_type=F32)


def mm_nt(left, right):
    return lax.dot_general(left, right, (((1,), (1,)), ((), ())), preferred_element_type=F32)


def iota(shape, dim):
    return lax.broadcasted_iota(jnp.int32, shape, dim)


def split3(x):
    hi = x.astype(BF16).astype(F32)
    mid = (x - hi).astype(BF16).astype(F32)
    return hi, mid, x - hi - mid


def softplus(x):
    small = jnp.exp(-jnp.abs(x))
    one = 1.0 + small
    log1p = jnp.where(one == 1.0, small, jnp.log(one) * (small / jnp.where(one == 1.0, 1.0, one - 1.0)))
    return jnp.maximum(x, 0.0) + log1p


def rows_of(pick, array):
    total = None
    for part in split3(array):
        term = mm_nt(pick, part.astype(BF16))
        total = term if total is None else total + term
    return total


def log_inverse_norm(x):
    square = x.astype(F32) * x.astype(F32)
    high = square.astype(BF16)
    low = (square - high.astype(F32)).astype(BF16)
    ones = jnp.ones((8, x.shape[1]), BF16)
    return -0.5 * jnp.log(mm_nt(ones, high) + mm_nt(ones, low) + 1e-6)


def odd_rows(x, n):
    return jnp.concatenate([x[i + n : i + 2 * n] for i in range(0, x.shape[0], 2 * n)], axis=0)


def weave(x, odd, n):
    parts = []
    for at in range(0, odd.shape[0], n):
        parts.append(x[2 * at : 2 * at + n])
        parts.append(odd[at : at + n])
    return jnp.concatenate(parts, axis=0)


def unit_lower_inverse(lower):
    size = lower.shape[0]
    half = size // 2
    row, col = iota((size, size), 0), iota((size, size), 1)
    crow, ccol = iota((half, size), 0), iota((half, size), 1)
    zeros = jnp.zeros((size, size), F32)
    pair = (row // 2 == col // 2)
    x = jnp.where(row == col, 1.0, jnp.where(pair, -lower, 0.0))
    n = 2
    while n < size:
        xb = x.astype(BF16)
        if n < 8:
            below = (row // n == col // n + 1) & (row // (2 * n) == col // (2 * n))
            b = jnp.where(below, lower, 0.0).astype(BF16)
            x = x - mm(xb, mm(b, xb).astype(BF16))
        elif n < half:
            b = jnp.where(ccol // n == 2 * (crow // n), odd_rows(lower, n), 0.0).astype(BF16)
            y = mm(b, xb)
            x_odd = odd_rows(x, n)
            z = mm(x_odd.astype(BF16), weave(zeros, y, n).astype(BF16))
            x = weave(x, x_odd - z, n)
        else:
            y = mm(lower[half:, :half].astype(BF16), xb[:half, :half])
            z = mm(xb[half:, half:], y.astype(BF16))
            low = jnp.concatenate([-z, x[half:, half:]], axis=1)
            x = jnp.concatenate([x[:half], low], axis=0)
        n *= 2
    return x


def local_kernel(first_ref, q_ref, k_ref, v_ref, gate_ref, beta_ref, rate_ref, *rest):
    ends_ref, out_ref, gain_ref = rest[-3:]
    tokens = q_ref.shape[0]
    heads = gate_ref.shape[1]
    key_head = first_ref[0] + pl.program_id(0)
    q_all, k_all = q_ref[...], k_ref[...]

    pick = iota((8, heads), 1) == 2 * key_head + iota((8, heads), 0)
    rate = jnp.sum(jnp.where(pick, rate_ref[...], 0.0), axis=1, keepdims=True)
    pick = jnp.where(pick, 1.0, 0.0).astype(BF16)
    decay = -rate * softplus(rows_of(pick, gate_ref[...]))
    log_beta = -softplus(-rows_of(pick, beta_ref[...]))
    log_k, log_q = log_inverse_norm(k_all), log_inverse_norm(q_all)

    row, col = iota((CHUNK, CHUNK), 0), iota((CHUNK, CHUNK), 1)
    upto = jnp.where(row <= col, 1.0, 0.0).astype(BF16)
    state = [None, None]
    for at in range(0, tokens, CHUNK):
        here = slice(at, at + CHUNK)
        q, k, v = q_all[here], k_all[here], v_ref[here, :]
        parts = mm(jnp.concatenate(split3(decay[:, here]), axis=0).astype(BF16), upto)
        cumul = parts[:8] + parts[8:16] + parts[16:]
        end = cumul[:, CHUNK - 1 :]
        lb, lk, lq = log_beta[:, here], log_k[:, here], log_q[:, here]
        col_log = cumul - lk
        row_lower = cumul + lb + lk
        row_mix = cumul + lq
        key_end = jnp.exp(end - cumul + lk)
        columns = jnp.concatenate(
            [row_lower, row_mix, jnp.exp(lb), jnp.exp(row_lower), jnp.exp(row_mix)], axis=0
        ).T
        turned = k.astype(F32).T
        turned_b = turned.astype(BF16)
        key_key = mm(k, turned_b)
        query_key = mm(q, turned_b)
        k32, q32 = k.astype(F32), q.astype(F32)
        for r in range(2):
            c_lower, c_mix, c_beta, c_weight, c_query = (
                columns[:, 8 * i + r : 8 * i + r + 1] for i in range(5)
            )
            b_row = col_log[r : r + 1]
            lower = jnp.exp(jnp.where(col < row, c_lower - b_row, NEG)) * key_key
            mixing = (jnp.exp(jnp.where(col <= row, c_mix - b_row, NEG)) * query_key).astype(BF16)
            inverse = unit_lower_inverse(lower).astype(BF16)
            v32 = v[:, r * DV : (r + 1) * DV].astype(F32)
            rhs = jnp.concatenate([c_beta * v32, c_weight * k32], axis=1).astype(BF16)
            solved = mm(inverse, rhs)
            update, weights = solved[:, :DV], solved[:, DV:]
            q_decayed = c_query * q32
            k_ended = (turned * key_end[r : r + 1]).astype(BF16)
            e = jnp.exp(end[r : r + 1])
            if state[r] is None:
                resid = jnp.concatenate([update, -weights], axis=1).astype(BF16)
                result = mm(mixing, resid)
                result = jnp.concatenate([result[:, :DV], result[:, DV:] + q_decayed], axis=1)
                eye = jnp.where(iota((DK, DV + DK), 1) == iota((DK, DV + DK), 0) + DV, e, 0.0)
                state[r] = eye + mm(k_ended, resid)
            else:
                held = state[r].astype(BF16)
                moved = mm(weights.astype(BF16), held)
                resid = jnp.concatenate([update - moved[:, :DV], -moved[:, DV:]], axis=1).astype(BF16)
                result = mm(q_decayed.astype(BF16), held) + mm(mixing, resid)
                state[r] = e * state[r] + mm(k_ended, resid)
            out_ref[here, r * DV : (r + 1) * DV] = result[:, :DV]
            gain_ref[here, r * DK : (r + 1) * DK] = result[:, DV:].astype(BF16)
    for r in range(2):
        ends_ref[r] = state[r].astype(BF16)


def local_part(first, groups, query, keys, values, gate_logit, beta_logit, rate, earlier):
    tokens, heads = gate_logit.shape
    whole = lambda i, first: (0, 0)
    mine = lambda i, first: (0, first[0] + i)
    in_specs = [
        pl.BlockSpec((tokens, DK), mine),
        pl.BlockSpec((tokens, DK), mine),
        pl.BlockSpec((tokens, 2 * DV), mine),
        pl.BlockSpec((tokens, heads), whole),
        pl.BlockSpec((tokens, heads), whole),
        pl.BlockSpec((1, heads), whole),
    ]
    args = [first, query, keys, values, gate_logit, beta_logit, rate]
    aliases = {}
    if earlier is not None:
        in_specs += [pl.BlockSpec(memory_space=pl.ANY)] * 2
        aliases = {len(args): 1, len(args) + 1: 2}
        args += list(earlier)
    return pl.pallas_call(
        local_kernel,
        grid_spec=pltpu.PrefetchScalarGridSpec(
            num_scalar_prefetch=1,
            grid=(groups,),
            in_specs=in_specs,
            out_specs=[
                pl.BlockSpec((2, DK, DV + DK), lambda i, first: (i, 0, 0)),
                pl.BlockSpec((tokens, 2 * DV), mine),
                pl.BlockSpec((tokens, 2 * DK), mine),
            ],
        ),
        out_shape=[
            jax.ShapeDtypeStruct((2 * groups, DK, DV + DK), BF16),
            jax.ShapeDtypeStruct((tokens, heads * DV), F32),
            jax.ShapeDtypeStruct((tokens, heads * DK), BF16),
        ],
        input_output_aliases=aliases,
        compiler_params=pltpu.CompilerParams(vmem_limit_bytes=VMEM_BYTES),
        cost_estimate=pl.CostEstimate(
            flops=groups * 4 * 14 * 2 * CHUNK**3, bytes_accessed=groups * 2**20, transcendentals=0
        ),
        name="local_part",
    )(*args)


def small_call(kernel, flag, arrays, out_shapes, flops):
    return pl.pallas_call(
        kernel,
        in_specs=[pl.BlockSpec(memory_space=pltpu.SMEM)]
        + [pl.BlockSpec(memory_space=pltpu.VMEM)] * len(arrays),
        out_specs=[pl.BlockSpec(memory_space=pltpu.VMEM)] * len(out_shapes),
        out_shape=[jax.ShapeDtypeStruct(s, BF16) for s in out_shapes],
        cost_estimate=pl.CostEstimate(flops=flops, bytes_accessed=2**18, transcendentals=0),
        name=kernel.__name__.strip("_"),
    )(flag, *arrays)


def pair_kernel(upper_ref, own_ref, other_ref, pair_ref):
    upper = upper_ref[0] == 1
    for h in range(own_ref.shape[0]):
        own, other = own_ref[h].astype(F32), other_ref[h].astype(F32)
        one = jnp.where(upper, other, own)
        two = jnp.where(upper, own, other)
        both = mm(two[:, DV:].astype(BF16), one.astype(BF16))
        pair_ref[h] = jnp.concatenate([both[:, :DV] + two[:, :DV], both[:, DV:]], axis=1).astype(BF16)


def hop_kernel(upper_ref, pair_ref, held_ref, came_ref, sum_ref, out_ref):
    for h in range(pair_ref.shape[0]):
        start = held_ref[h] + came_ref[h]
        sum_ref[h] = start
        pair = pair_ref[h]
        out_ref[h] = (mm(pair[:, DV:], start) + pair[:, :DV].astype(F32)).astype(BF16)


def middle_kernel(upper_ref, own_ref, other_ref, held_ref, came_ref, keep_ref, send_ref):
    upper = upper_ref[0] == 1
    for h in range(own_ref.shape[0]):
        start = held_ref[h] + came_ref[h]
        one = jnp.where(upper, other_ref[h].astype(F32), own_ref[h].astype(F32))
        middle = mm(one[:, DV:].astype(BF16), start) + one[:, :DV]
        start = start.astype(F32)
        keep_ref[h] = jnp.where(upper, middle, start).astype(BF16)
        send_ref[h] = jnp.where(upper, start, middle).astype(BF16)


def project_kernel(
    place_ref, out_ref, gain_ref, z_ref, keep_ref, came_ref, norm_ref, w_ref, send_ref, stay_ref, gated_ref
):
    heads = z_ref.shape[1] // DV
    half = heads // 2
    upper = place_ref[2]
    ones = jnp.full((DV, DV), 1.0 / DV, BF16)
    for h in range(heads):
        at = slice(h * DV, (h + 1) * DV)
        kept = keep_ref[h % half].astype(F32)
        came = came_ref[h % half].astype(F32)
        start = jnp.where(upper == h // half, kept, came).astype(BF16)
        core = out_ref[:, at] + mm(gain_ref[:, at], start)
        square = core * core
        high = square.astype(BF16)
        low = (square - high.astype(F32)).astype(BF16)
        mean = mm(high, ones) + mm(low, ones)
        z = z_ref[:, at].astype(F32)
        gate = z / (1.0 + jnp.exp(-z))
        gated_ref[:, at] = (core * lax.rsqrt(mean + 1e-6) * norm_ref[...] * gate).astype(BF16)
    partial = mm(gated_ref[...], w_ref[...])

    @pl.when(pl.program_id(0) == 0)
    def _():
        send_ref[...] = partial.astype(BF16)

    @pl.when(pl.program_id(0) == 1)
    def _():
        stay_ref[...] = partial


def project_part(place, rows, out, gain, z, keep, came, norm_gain, weight):
    width = z.shape[1]
    wide = weight.shape[1]
    half = keep.shape[0]

    def block(i, place):
        return (2 * place[0] + jnp.where(i == 0, 1 - place[1], place[1]), 0)

    fixed = lambda i, place: (0, 0)
    return pl.pallas_call(
        project_kernel,
        grid_spec=pltpu.PrefetchScalarGridSpec(
            num_scalar_prefetch=1,
            grid=(2,),
            in_specs=[
                pl.BlockSpec((rows, width), block),
                pl.BlockSpec((rows, width), block),
                pl.BlockSpec((rows, width), block),
                pl.BlockSpec((half, DK, DV), lambda i, place: (0, 0, 0)),
                pl.BlockSpec((half, DK, DV), lambda i, place: (0, 0, 0)),
                pl.BlockSpec((1, DV), fixed),
                pl.BlockSpec(weight.shape, fixed),
            ],
            out_specs=[pl.BlockSpec((rows, wide), fixed)] * 2,
            scratch_shapes=[pltpu.VMEM((rows, width), BF16)],
        ),
        out_shape=[
            jax.ShapeDtypeStruct((rows, wide), BF16),
            jax.ShapeDtypeStruct((rows, wide), F32),
        ],
        compiler_params=pltpu.CompilerParams(vmem_limit_bytes=VMEM_BYTES),
        cost_estimate=pl.CostEstimate(
            flops=2 * rows * 2 * width * wide, bytes_accessed=2 * weight.size, transcendentals=0
        ),
        name="project_part",
    )(place, out, gain, z, keep, came, norm_gain, weight)


def on_device(
    query, keys, values, gate_logit, beta_logit, decay_rate, norm_gain, gate_z, out_weight
):
    shards, cores = lax.axis_size("seq"), lax.axis_size("head")
    seq, head = lax.axis_index("seq"), lax.axis_index("head")
    key_heads = query.shape[1] // DK
    groups = key_heads // 2
    half = 2 * groups
    upper = lax.rem(seq, 2)
    flag = upper.reshape(1)
    rate = decay_rate.reshape(1, -1)
    arrays = (query, keys, values, gate_logit, beta_logit, rate)

    away, out, gain = local_part(((1 - upper) * groups).reshape(1), groups, *arrays, None)
    other = lax.ppermute(away, "seq", [(s, s ^ 1) for s in range(shards)])
    own, out, gain = local_part((upper * groups).reshape(1), groups, *arrays, (out, gain))

    state = (half, DK, DV)
    pair = small_call(pair_kernel, flag, (own, other), [own.shape], half * 2**23)[0]
    held = jnp.zeros(state, BF16)
    ending = pair[:, :, :DV]
    came = None
    for step in range(shards // 2 - 1):
        if step:
            held, ending = small_call(hop_kernel, flag, (pair, held, came), [state] * 2, half * 2**22)
        came = lax.ppermute(
            ending, "seq", [(2 * step + i, 2 * step + 2 + i) for i in range(2)]
        )
    keep, send = small_call(middle_kernel, flag, (own, other, held, came), [state] * 2, half * 2**22)
    back = lax.ppermute(send, "seq", [(s, s ^ 1) for s in range(shards)])

    chips = cores // 2
    chip, core = head // 2, lax.rem(head, 2)
    rows = query.shape[0] // cores
    norm_gain = norm_gain.reshape(1, -1)
    swap = [(i, i ^ 1) for i in range(cores)]
    arrived = []
    for by in list(range(1, chips)) + [0]:
        target = lax.rem(chip + by, chips)
        place = jnp.stack([target, core, upper])
        give, stay = project_part(
            place, rows, out, gain, gate_z, keep, back, norm_gain, out_weight
        )
        both = stay + lax.ppermute(give, "head", swap).astype(F32)
        if by:
            moves = [(i, (i + 2 * by) % cores) for i in range(cores)]
            arrived.append(lax.ppermute(both.astype(BF16), "head", moves))
    for part in arrived:
        both = both + part.astype(F32)
    return both.astype(BF16)


def solution(mesh):
    return jax.shard_map(
        on_device,
        mesh=mesh,
        in_specs=(
            P("seq", "head"),
            P("seq", "head"),
            P("seq", "head"),
            P("seq", "head"),
            P("seq", "head"),
            P("head"),
            P(),
            P("seq", "head"),
            P("head", None),
        ),
        out_specs=P(("seq", "head"), None),
        check_vma=False,
    )
```

time: 611 us -> 120 us (0.20)
  the two profiles are of different devices: /device:TPU:0 before, /device:TPU:26 now
where the time goes in v1:
time: 120 us; the launch traced here: 119 us
  Pallas kernels  73.2 us (61%)
  waiting for transfers between devices  31.2 us (26%)
  local copies, waits for them, and re-layouts  7.36 us (6%)
  starting transfers between devices  5.88 us (5%)
  other arithmetic  1.7 us (1%)
    pallas_call x2, Pallas kernels, local_part(): pl.pallas_call(local_kernel, grid_spec=pltpu.PrefetchScalarGridSpec(num_s...  49.9 us
    pallas_call x2, Pallas kernels, project_part(): pl.pallas_call(project_kernel, grid_spec=pltpu.PrefetchScalarGridSpec(num...  15.5 us
    ppermute x3, waiting for transfers between devices, on_device(): lax.ppermute(ending, 'seq', [(2 * step + i, 2 * step + 2 + i) for i in ra...  13.8 us
    ppermute x1, waiting for transfers between devices, on_device(): arrived.append(lax.ppermute(both.astype(BF16), 'head', moves))  12.3 us
    pallas_call x4, Pallas kernels, small_call(): pl.pallas_call(kernel, in_specs=[pl.BlockSpec(memory_space=pltpu.SMEM)] +...  7.77 us
    unnamed x16, local copies, waits for them, and re-layouts  5.74 us
    ppermute x1, waiting for transfers between devices, on_device(): back = lax.ppermute(send, 'seq', [(s, s ^ 1) for s in range(shards)])  4.1 us
    ppermute x3, starting transfers between devices, on_device(): lax.ppermute(ending, 'seq', [(2 * step + i, 2 * step + 2 + i) for i in ra...  2.79 us
  transfers between devices with their start and end apart: 8, of which 4 were waited for; matrix products, arithmetic and copies ran while one was open for 1% of the time, Pallas kernels for 27%

profile of v1, /device:TPU:26, one launch (start us, length us, event | category | flops | bytes accessed | tf_op | source)
XLA Modules:
  0.0 119.5 jit_solution(11520083004567177935)
XLA Ops:
  0.0 1.6 %copy.14.gate_ref = f32[512,8]{1,0:T(8,128)} copy(f32[512,8]{0,1:T(8,128)} %param.12) | data formatting | bytes 32768 | tf_op args[3]
  1.6 1.6 %copy.15.beta_ref = f32[512,8]{1,0:T(8,128)} copy(f32[512,8]{0,1:T(8,128)} %param.13) | data formatting | bytes 32768 | tf_op args[4]
  3.1 24.9 %local_part.2 = (bf16[4,128,256]{2,1,0:T(8,128)(2,1)}, f32[512,1024]{1,0:T(8,128)}, bf16[512,1024]{1,0:T(8,128)(2,1)}) custom-call(s32[1]{0:T(128)} %bitcast.5.first_ref, bf16[512,512]{1,0:T(8,128)(2,1)} %q_ref.3, bf16[512,512]{1,0:T(8,128)(2,1)} %k_ref.3, bf16[512,1024]{1,0:T(8,128)(2,1)} %v_ref.3, f32[512,8]{1,0:T(8,128)} %copy.14.gate_ref, ...), custom_call_target="tpu_custom_call" | custom-call | flops 3758096384 | bytes 2097152 | tf_op jit(solution)/shard_map/local_part/pallas_call | solution.py:189
  28.1 1.5 %collective-permute-start = (bf16[4,128,256]{2,1,0:T(8,128)(2,1)}, bf16[4,128,256]{2,1,0:T(8,128)(2,1)S(1)}, u32[]{:S(2)}, u32[]{:S(2)}) collective-permute-start(bf16[4,128,256]{2,1,0:T(8,128)(2,1)} %get-tuple-element.26), channel_id=1, source_target_pairs={{0,4},{4,0},{8,12},{12,8},{16,20},{20,16},{24,28},{28,24},{1,5},{5... | collective-permute-start | bytes 786440 | tf_op jit(solution)/shard_map/ppermute | solution.py:339
  29.6 25.0 %local_part.3 = (bf16[4,128,256]{2,1,0:T(8,128)(2,1)}, f32[512,1024]{1,0:T(8,128)}, bf16[512,1024]{1,0:T(8,128)(2,1)}) custom-call(s32[1]{0:T(128)} %bitcast.3.first_ref, bf16[512,512]{1,0:T(8,128)(2,1)} %q_ref.3, bf16[512,512]{1,0:T(8,128)(2,1)} %k_ref.3, bf16[512,1024]{1,0:T(8,128)(2,1)} %v_ref.3, ...), custom_call_target="tpu_custom_call", output_to_operand_aliasing={{1}: (7, {}), {2}: (8, {})} | custom-call | flops 3758096384 | bytes 2097152 | tf_op jit(solution)/shard_map/local_part/pallas_call | solution.py:189
  54.6 0.0 collective-permute-done.other_ref
  54.6 0.0 copy-start.2
  54.6 0.7 copy-done.2
  55.3 2.0 %pair_kernel.1.pair_ref = bf16[4,128,256]{2,1,0:T(8,128)(2,1)} custom-call(s32[1]{0:T(128)} %bitcast.2.upper_ref, bf16[4,128,256]{2,1,0:T(8,128)(2,1)} %get-tuple-element.25.own_ref, bf16[4,128,256]{2,1,0:T(8,128)(2,1)} %copy-done.2), custom_call_target="tpu_custom_call" | custom-call | flops 33554432 | bytes 262144 | tf_op jit(solution)/shard_map/pair_kernel/pallas_call | solution.py:216
  57.2 0.9 slice.4
  58.2 0.7 collective-permute-start.1
  58.8 0.0 collective-permute-done.1.came_ref
  58.8 0.0 copy-start.5
  58.9 0.7 broadcast_in_dim.3.held_ref
  59.6 0.0 copy-done.5
  59.6 1.9 %hop_kernel.2 = (bf16[4,128,128]{2,1,0:T(8,128)(2,1)}, bf16[4,128,128]{2,1,0:T(8,128)(2,1)}) custom-call(s32[1]{0:T(128)} %bitcast.2.upper_ref, bf16[4,128,256]{2,1,0:T(8,128)(2,1)} %pair_kernel.1.pair_ref, bf16[4,128,128]{2,1,0:T(8,128)(2,1)} %broadcast_in_dim.3.held_ref, bf16[4,128,128]{2,1,0:T(8,128)(2,1)} %copy-done.5), custom_call_target="tpu_custom_call" | custom-call | flops 16777216 | bytes 262144 | tf_op jit(solution)/shard_map/hop_kernel/pallas_call | solution.py:216
  61.5 0.7 collective-permute-start.2
  62.1 0.0 collective-permute-done.2.came_ref
  62.1 0.0 copy-start.4
  62.1 0.6 copy-done.4
  62.8 1.9 %hop_kernel.3 = (bf16[4,128,128]{2,1,0:T(8,128)(2,1)}, bf16[4,128,128]{2,1,0:T(8,128)(2,1)}) custom-call(s32[1]{0:T(128)} %bitcast.2.upper_ref, bf16[4,128,256]{2,1,0:T(8,128)(2,1)} %pair_kernel.1.pair_ref, bf16[4,128,128]{2,1,0:T(8,128)(2,1)} %get-tuple-element.27.held_ref, bf16[4,128,128]{2,1,0:T(8,128)(2,1)} %copy-done.4), custom_call_target="tpu_custom_call" | custom-call | flops 16777216 | bytes 262144 | tf_op jit(solution)/shard_map/hop_kernel/pallas_call | solution.py:216
  64.7 1.5 %collective-permute-start.3 = (bf16[4,128,128]{2,1,0:T(8,128)(2,1)}, bf16[4,128,128]{2,1,0:T(8,128)(2,1)S(1)}, u32[]{:S(2)}, u32[]{:S(2)}) collective-permute-start(bf16[4,128,128]{2,1,0:T(8,128)(2,1)} %get-tuple-element.30), channel_id=1, source_target_pairs={{16,24},{20,28},{17,25},{21,29},{18,26},{22,30},{19,27},{23,31}} | collective-permute-start | bytes 393224 | tf_op jit(solution)/shard_map/ppermute | solution.py:350
  66.1 13.8 %collective-permute-done.3.came_ref = bf16[4,128,128]{2,1,0:T(8,128)(2,1)S(1)} collective-permute-done((bf16[4,128,128]{2,1,0:T(8,128)(2,1)}, bf16[4,128,128]{2,1,0:T(8,128)(2,1)S(1)}, u32[]{:S(2)}, u32[]{:S(2)}) %collective-permute-start.3) | collective-permute-done | bytes 131104 | tf_op jit(solution)/shard_map/ppermute | solution.py:350
  79.9 0.0 copy-start.6
  79.9 0.6 copy-done.6
  80.5 2.0 %middle_kernel.1 = (bf16[4,128,128]{2,1,0:T(8,128)(2,1)}, bf16[4,128,128]{2,1,0:T(8,128)(2,1)}) custom-call(s32[1]{0:T(128)} %bitcast.2.upper_ref, bf16[4,128,256]{2,1,0:T(8,128)(2,1)} %get-tuple-element.25.own_ref, bf16[4,128,256]{2,1,0:T(8,128)(2,1)} %copy-done.2, bf16[4,128,128]{2,1,0:T(8,128)(2,1)} %get-tuple-element.29.held_ref, ...), custom_call_target="tpu_custom_call" | custom-call | flops 16777216 | bytes 262144 | tf_op jit(solution)/shard_map/middle_kernel/pallas_call | solution.py:216
  82.6 0.5 collective-permute-start.4
  83.0 0.6 add_add_fusion
  83.7 4.1 %collective-permute-done.4.came_ref = bf16[4,128,128]{2,1,0:T(8,128)(2,1)S(1)} collective-permute-done((bf16[4,128,128]{2,1,0:T(8,128)(2,1)}, bf16[4,128,128]{2,1,0:T(8,128)(2,1)S(1)}, u32[]{:S(2)}, u32[]{:S(2)}) %collective-permute-start.4) | collective-permute-done | bytes 131104 | tf_op jit(solution)/shard_map/ppermute | solution.py:354
  87.8 0.0 copy-start.3
  87.8 0.6 copy-done.3
  88.4 7.7 %project_part.3 = (bf16[128,2048]{1,0:T(8,128)(2,1)}, f32[128,2048]{1,0:T(8,128)}) custom-call(s32[3]{0:T(128)} %get-tuple-element.38.place_ref, f32[512,1024]{1,0:T(8,128)} %get-tuple-element.23.out_ref, bf16[512,1024]{1,0:T(8,128)(2,1)} %get-tuple-element.24.gain_ref, bf16[512,1024]{1,0:T(8,128)(2,1)} %z_ref.3, ...), custom_call_target="tpu_custom_call" | custom-call | flops 1073741824 | bytes 4194304 | tf_op jit(solution)/shard_map/project_part/pallas_call | solution.py:296
  96.1 0.0 collective-permute-start.6
  96.1 0.0 copy-start.1
  96.1 7.8 %project_part.2 = (bf16[128,2048]{1,0:T(8,128)(2,1)}, f32[128,2048]{1,0:T(8,128)}) custom-call(s32[3]{0:T(128)} %get-tuple-element.37.place_ref, f32[512,1024]{1,0:T(8,128)} %get-tuple-element.23.out_ref, bf16[512,1024]{1,0:T(8,128)(2,1)} %get-tuple-element.24.gain_ref, bf16[512,1024]{1,0:T(8,128)(2,1)} %z_ref.3, ...), custom_call_target="tpu_custom_call" | custom-call | flops 1073741824 | bytes 4194304 | tf_op jit(solution)/shard_map/project_part/pallas_call | solution.py:296
  103.9 0.0 copy-start
  103.9 0.5 collective-permute-start.5
  104.4 0.0 collective-permute-done.6
  104.4 0.0 copy-done.1
  104.4 0.1 add_convert_fusion.1
  104.6 0.6 collective-permute-start.7
  105.2 1.0 collective-permute-done.5
  106.2 12.3 %collective-permute-done.7 = bf16[128,2048]{1,0:T(8,128)(2,1)S(1)} collective-permute-done((bf16[128,2048]{1,0:T(8,128)(2,1)S(1)}, bf16[128,2048]{1,0:T(8,128)(2,1)S(1)}, u32[]{:S(2)}, u32[]{:S(2)}) %collective-permute-start.7) | collective-permute-done | bytes 524320 | tf_op jit(solution)/shard_map/ppermute | solution.py:371
  118.5 0.0 copy-done
  118.5 1.0 add_convert_fusion
Async XLA Ops:
  28.1 26.5 %collective-permute-start = (bf16[4,128,256]{2,1,0:T(8,128)(2,1)}, bf16[4,128,256]{2,1,0:T(8,128)(2,1)S(1)}, u32[]{:S(2)}, u32[]{:S(2)}) collective-permute-start(bf16[4,128,256]{2,1,0:T(8,128)(2,1)} %get-tuple-element.26), channel_id=1, source_target_pairs={{0,4},{4,0},{8,12},{12,8},{16,20},{20,16},{24,28},{28,24},{1,5},{5... | collective-permute-start | bytes 786440 | tf_op jit(solution)/shard_map/ppermute | solution.py:339
  54.6 0.7 copy-start.2
  58.2 0.7 collective-permute-start.1
  58.8 0.7 copy-start.5
  61.5 0.7 collective-permute-start.2
  62.1 0.6 copy-start.4
  64.7 15.2 %collective-permute-start.3 = (bf16[4,128,128]{2,1,0:T(8,128)(2,1)}, bf16[4,128,128]{2,1,0:T(8,128)(2,1)S(1)}, u32[]{:S(2)}, u32[]{:S(2)}) collective-permute-start(bf16[4,128,128]{2,1,0:T(8,128)(2,1)} %get-tuple-element.30), channel_id=1, source_target_pairs={{16,24},{20,28},{17,25},{21,29},{18,26},{22,30},{19,27},{23,31}} | collective-permute-start | bytes 393224 | tf_op jit(solution)/shard_map/ppermute | solution.py:350
  79.9 0.6 copy-start.6
  82.6 5.2 %collective-permute-start.4 = (bf16[4,128,128]{2,1,0:T(8,128)(2,1)}, bf16[4,128,128]{2,1,0:T(8,128)(2,1)S(1)}, u32[]{:S(2)}, u32[]{:S(2)}) collective-permute-start(bf16[4,128,128]{2,1,0:T(8,128)(2,1)} %get-tuple-element.32), channel_id=1, source_target_pairs={{0,4},{4,0},{8,12},{12,8},{16,20},{20,16},{24,28},{28,24},{1,5},{5... | collective-permute-start | bytes 393224 | tf_op jit(solution)/shard_map/ppermute | solution.py:354
  87.8 0.6 copy-start.3
  96.1 8.4 %collective-permute-start.6 = (bf16[128,2048]{1,0:T(8,128)(2,1)}, bf16[128,2048]{1,0:T(8,128)(2,1)S(1)}, u32[]{:S(2)}, u32[]{:S(2)}) collective-permute-start(bf16[128,2048]{1,0:T(8,128)(2,1)} %get-tuple-element.36), channel_id=1, source_target_pairs={{0,1},{1,0},{2,3},{3,2},{4,5},{5,4},{6,7},{7,6},{8,9},{9,8},{10,11... | collective-permute-start | bytes 1572872 | tf_op jit(solution)/shard_map/ppermute | solution.py:368
  96.1 8.4 %copy-start.1 = (f32[128,2048]{1,0:T(8,128)S(1)}, f32[128,2048]{1,0:T(8,128)}, u32[]{:S(2)}) copy-start(f32[128,2048]{1,0:T(8,128)} %get-tuple-element.35) | copy-start | bytes 3145732
  103.9 14.5 %copy-start = (f32[128,2048]{1,0:T(8,128)S(1)}, f32[128,2048]{1,0:T(8,128)}, u32[]{:S(2)}) copy-start(f32[128,2048]{1,0:T(8,128)} %get-tuple-element.33) | copy-start | bytes 3145732
  103.9 2.2 %collective-permute-start.5 = (bf16[128,2048]{1,0:T(8,128)(2,1)}, bf16[128,2048]{1,0:T(8,128)(2,1)S(1)}, u32[]{:S(2)}, u32[]{:S(2)}) collective-permute-start(bf16[128,2048]{1,0:T(8,128)(2,1)} %get-tuple-element.34), channel_id=1, source_target_pairs={{0,1},{1,0},{2,3},{3,2},{4,5},{5,4},{6,7},{7,6},{8,9},{9,8},{10,11... | collective-permute-start | bytes 1572872 | tf_op jit(solution)/shard_map/ppermute | solution.py:368
  104.6 13.9 %collective-permute-start.7 = (bf16[128,2048]{1,0:T(8,128)(2,1)S(1)}, bf16[128,2048]{1,0:T(8,128)(2,1)S(1)}, u32[]{:S(2)}, u32[]{:S(2)}) collective-permute-start(bf16[128,2048]{1,0:T(8,128)(2,1)S(1)} %add_convert_fusion.1), channel_id=1, source_target_pairs={{0,2},{1,3},{2,0},{3,1},{4,6},{5,7},{6,4},{7,5},{8,10},{9,11},{10,... | collective-permute-start | bytes 1572872 | tf_op jit(solution)/shard_map/ppermute | solution.py:371

commit v2 on v1

v2 whole, which is shorter than its diff:
```python
import functools

import jax
import jax.numpy as jnp
from jax import lax
from jax.experimental import pallas as pl
from jax.experimental.pallas import tpu as pltpu
from jax.sharding import PartitionSpec as P

DK = 128
DV = 128
CHUNK = 256
F32 = jnp.float32
BF16 = jnp.bfloat16
NEG = -1e30
LOCAL_VMEM = 60 * 1024 * 1024
PROJECT_VMEM = 32 * 1024 * 1024


def mm(left, right):
    return lax.dot_general(left, right, (((1,), (0,)), ((), ())), preferred_element_type=F32)


def mm_nt(left, right):
    return lax.dot_general(left, right, (((1,), (1,)), ((), ())), preferred_element_type=F32)


def iota(shape, dim):
    return lax.broadcasted_iota(jnp.int32, shape, dim)


def split3(x):
    hi = x.astype(BF16).astype(F32)
    mid = (x - hi).astype(BF16).astype(F32)
    return hi, mid, x - hi - mid


def softplus(x):
    small = jnp.exp(-jnp.abs(x))
    one = 1.0 + small
    log1p = jnp.where(one == 1.0, small, jnp.log(one) * (small / jnp.where(one == 1.0, 1.0, one - 1.0)))
    return jnp.maximum(x, 0.0) + log1p


def log_inverse_norm(x, rows):
    square = x.astype(F32) * x.astype(F32)
    high = square.astype(BF16)
    low = (square - high.astype(F32)).astype(BF16)
    ones = jnp.ones((rows, x.shape[1]), BF16)
    return -0.5 * jnp.log(mm_nt(ones, high) + mm_nt(ones, low) + 1e-6)


def odd_rows(x, n):
    return jnp.concatenate([x[i + n : i + 2 * n] for i in range(0, x.shape[0], 2 * n)], axis=0)


def weave(even, odd, n):
    parts = []
    for at in range(0, odd.shape[0], n):
        parts.append(even[2 * at : 2 * at + n])
        parts.append(odd[at : at + n])
    return jnp.concatenate(parts, axis=0)


def as_mask(where):
    return jnp.where(where, 1.0, 0.0).astype(BF16)


def unit_lower_inverses(lowers):
    size = lowers[0].shape[0]
    half = size // 2
    row, col = iota((size, size), 0), iota((size, size), 1)
    crow, ccol = iota((half, size), 0), iota((half, size), 1)
    zeros = jnp.zeros((size, size), BF16)
    eye, pair = as_mask(row == col), as_mask(row // 2 == col // 2)
    xs = [eye - lower * pair for lower in lowers]
    n = 2
    while n < size:
        if n < 16:
            mask = as_mask((row // n == col // n + 1) & (row // (2 * n) == col // (2 * n)))
            ys = [mm(lower * mask, x).astype(BF16) for lower, x in zip(lowers, xs)]
            zs = [mm(x, y).astype(BF16) for x, y in zip(xs, ys)]
            xs = [x - z for x, z in zip(xs, zs)]
        elif n < half:
            mask = as_mask(ccol // n == 2 * (crow // n))
            ys = [mm(odd_rows(lower, n) * mask, x).astype(BF16) for lower, x in zip(lowers, xs)]
            odds = [odd_rows(x, n) for x in xs]
            zs = [mm(odd, weave(zeros, y, n)).astype(BF16) for odd, y in zip(odds, ys)]
            xs = [weave(x, odd - z, n) for x, odd, z in zip(xs, odds, zs)]
        else:
            ys = [mm(lower[half:, :half], x[:half, :half]).astype(BF16) for lower, x in zip(lowers, xs)]
            zs = [mm(x[half:, half:], y).astype(BF16) for x, y in zip(xs, ys)]
            xs = [
                jnp.concatenate([x[:half], jnp.concatenate([-z, x[half:, half:]], axis=1)], axis=0)
                for x, z in zip(xs, zs)
            ]
        n *= 2
    return xs


def decayed(c, b, product, mask):
    h = CHUNK // 2

    def quarter(i, j):
        arg = c[i * h : (i + 1) * h] - b[:, j * h : (j + 1) * h]
        if i == j:
            arg = jnp.where(mask, arg, NEG)
        return (jnp.exp(arg) * product[i * h : (i + 1) * h, j * h : (j + 1) * h]).astype(BF16)

    top = jnp.concatenate([quarter(0, 0), jnp.zeros((h, h), BF16)], axis=1)
    return jnp.concatenate([top, jnp.concatenate([quarter(1, 0), quarter(1, 1)], axis=1)], axis=0)


def local_kernel(place_ref, q_ref, k_ref, v_ref, gate_ref, beta_ref, rate_ref, *rest):
    ends_ref, out_ref, gain_ref = rest[-3:]
    tokens = q_ref.shape[0]
    heads = gate_ref.shape[0]
    groups = q_ref.shape[1] // DK
    half = heads // 2
    second = place_ref[0] == 1
    chunks = [slice(at, at + CHUNK) for at in range(0, tokens, CHUNK)]
    members = [(g, r) for g in range(groups) for r in range(2)]

    def chosen(x):
        return jnp.where(second, jnp.concatenate([x[half:], x[:half]], axis=0), x)

    decay = -chosen(rate_ref[...]) * softplus(chosen(gate_ref[...]))
    log_beta = -softplus(-chosen(beta_ref[...]))
    head_row = iota((heads, tokens), 0)

    def per_head(ref):
        total = log_inverse_norm(ref[:, :DK], heads)
        for g in range(1, groups):
            more = log_inverse_norm(ref[:, g * DK : (g + 1) * DK], heads)
            total = jnp.where(head_row < 2 * g, total, more)
        return total

    log_k, log_q = per_head(k_ref), per_head(q_ref)

    row, col = iota((CHUNK, CHUNK), 0), iota((CHUNK, CHUNK), 1)
    upto = jnp.where(row <= col, 1.0, 0.0).astype(BF16)
    sums = mm(
        jnp.concatenate([p for here in chunks for p in split3(decay[:, here])], axis=0).astype(BF16), upto
    )
    square = CHUNK // 2
    strict = iota((square, square), 1) < iota((square, square), 0)
    inclusive = iota((square, square), 1) <= iota((square, square), 0)

    lowers, mixings, rights, queries, ended, decays = {}, {}, {}, {}, {}, {}
    for c, here in enumerate(chunks):
        parts = [sums[(3 * c + i) * heads : (3 * c + i + 1) * heads] for i in range(3)]
        cumul = parts[0] + parts[1] + parts[2]
        end = cumul[:, CHUNK - 1 :]
        lb, lk, lq = log_beta[:, here], log_k[:, here], log_q[:, here]
        col_log = cumul - lk
        row_lower = cumul + lb + lk
        row_mix = cumul + lq
        key_end = jnp.exp(end - cumul + lk)
        ends = jnp.exp(end)
        columns = jnp.concatenate(
            [row_lower, row_mix, jnp.exp(lb), jnp.exp(row_lower), jnp.exp(row_mix)], axis=0
        ).T
        for g in range(groups):
            q, k = q_ref[here, g * DK : (g + 1) * DK], k_ref[here, g * DK : (g + 1) * DK]
            q32, k32 = q.astype(F32), k.astype(F32)
            turned = k32.T
            turned_b = turned.astype(BF16)
            key_key = mm(k, turned_b)
            query_key = mm(q, turned_b)
            for r in range(2):
                at = 2 * g + r
                c_lower, c_mix, c_beta, c_weight, c_query = (
                    columns[:, heads * i + at : heads * i + at + 1] for i in range(5)
                )
                b_row = col_log[at : at + 1]
                m = (c, at)
                lowers[m] = decayed(c_lower, b_row, key_key, strict)
                mixings[m] = decayed(c_mix, b_row, query_key, inclusive)
                v32 = v_ref[here, at * DV : (at + 1) * DV].astype(F32)
                rights[m] = jnp.concatenate([c_beta * v32, c_weight * k32], axis=1).astype(BF16)
                queries[m] = c_query * q32
                ended[m] = (turned * key_end[at : at + 1]).astype(BF16)
                decays[m] = ends[at : at + 1]
    names = list(lowers)
    inverses = dict(zip(names, unit_lower_inverses([lowers[m] for m in names])))
    solved = {m: mm(inverses[m], rights[m]) for m in names}
    state = {}
    for c, here in enumerate(chunks):
        all_heads = range(2 * groups)
        if c == 0:
            resid = {a: jnp.concatenate([solved[c, a][:, :DV], -solved[c, a][:, DV:]], axis=1) for a in all_heads}
            resid = {a: resid[a].astype(BF16) for a in all_heads}
            eye = iota((DK, DV + DK), 1) == iota((DK, DV + DK), 0) + DV
            state = {a: jnp.where(eye, decays[c, a], 0.0) + mm(ended[c, a], resid[a]) for a in all_heads}
            result = {a: mm(mixings[c, a], resid[a]) for a in all_heads}
            for a in all_heads:
                out_ref[here, a * DV : (a + 1) * DV] = result[a][:, :DV]
                gain_ref[here, a * DK : (a + 1) * DK] = (result[a][:, DV:] + queries[c, a]).astype(BF16)
        else:
            held = {a: state[a].astype(BF16) for a in all_heads}
            moved = {a: mm(solved[c, a][:, DV:].astype(BF16), held[a]) for a in all_heads}
            resid = {
                a: jnp.concatenate([solved[c, a][:, :DV] - moved[a][:, :DV], -moved[a][:, DV:]], axis=1)
                for a in all_heads
            }
            resid = {a: resid[a].astype(BF16) for a in all_heads}
            state = {a: decays[c, a] * state[a] + mm(ended[c, a], resid[a]) for a in all_heads}
            result = {
                a: mm(queries[c, a].astype(BF16), held[a]) + mm(mixings[c, a], resid[a]) for a in all_heads
            }
            for a in all_heads:
                out_ref[here, a * DV : (a + 1) * DV] = result[a][:, :DV]
                gain_ref[here, a * DK : (a + 1) * DK] = result[a][:, DV:].astype(BF16)
    for a in range(2 * groups):
        ends_ref[a] = state[a].astype(BF16)


def local_part(place, groups, query, keys, values, gate_logit, beta_logit, rate, earlier):
    heads, tokens = gate_logit.shape
    whole = lambda i, place: (0, 0)
    mine = lambda i, place: (0, place[0])
    in_specs = [
        pl.BlockSpec((tokens, groups * DK), mine),
        pl.BlockSpec((tokens, groups * DK), mine),
        pl.BlockSpec((tokens, 2 * groups * DV), mine),
        pl.BlockSpec((heads, tokens), whole),
        pl.BlockSpec((heads, tokens), whole),
        pl.BlockSpec((heads, 1), whole),
    ]
    args = [place, query, keys, values, gate_logit, beta_logit, rate]
    aliases = {}
    if earlier is not None:
        in_specs += [pl.BlockSpec(memory_space=pl.ANY)] * 2
        aliases = {len(args): 1, len(args) + 1: 2}
        args += list(earlier)
    return pl.pallas_call(
        local_kernel,
        grid_spec=pltpu.PrefetchScalarGridSpec(
            num_scalar_prefetch=1,
            grid=(1,),
            in_specs=in_specs,
            out_specs=[
                pl.BlockSpec((2 * groups, DK, DV + DK), lambda i, place: (0, 0, 0)),
                pl.BlockSpec((tokens, 2 * groups * DV), mine),
                pl.BlockSpec((tokens, 2 * groups * DK), mine),
            ],
        ),
        out_shape=[
            jax.ShapeDtypeStruct((2 * groups, DK, DV + DK), BF16),
            jax.ShapeDtypeStruct((tokens, heads * DV), F32),
            jax.ShapeDtypeStruct((tokens, heads * DK), BF16),
        ],
        input_output_aliases=aliases,
        compiler_params=pltpu.CompilerParams(vmem_limit_bytes=LOCAL_VMEM),
        cost_estimate=pl.CostEstimate(
            flops=groups * 4 * 14 * 2 * CHUNK**3, bytes_accessed=groups * 2**20, transcendentals=0
        ),
        name="local_part",
    )(*args)


def small_call(kernel, flag, arrays, out_shapes, flops):
    return pl.pallas_call(
        kernel,
        in_specs=[pl.BlockSpec(memory_space=pltpu.SMEM)]
        + [pl.BlockSpec(memory_space=pltpu.VMEM)] * len(arrays),
        out_specs=[pl.BlockSpec(memory_space=pltpu.VMEM)] * len(out_shapes),
        out_shape=[pltpu.MemorySpace.VMEM(s, BF16) for s in out_shapes],
        cost_estimate=pl.CostEstimate(flops=flops, bytes_accessed=2**18, transcendentals=0),
        name=kernel.__name__.strip("_"),
    )(flag, *[pltpu.with_memory_space_constraint(a, pltpu.VMEM) for a in arrays])


def pair_kernel(upper_ref, own_ref, other_ref, pair_ref):
    upper = upper_ref[0] == 1
    for h in range(own_ref.shape[0]):
        own, other = own_ref[h].astype(F32), other_ref[h].astype(F32)
        one = jnp.where(upper, other, own)
        two = jnp.where(upper, own, other)
        both = mm(two[:, DV:].astype(BF16), one.astype(BF16))
        pair_ref[h] = jnp.concatenate([both[:, :DV] + two[:, :DV], both[:, DV:]], axis=1).astype(BF16)


def hop_kernel(upper_ref, pair_ref, held_ref, came_ref, sum_ref, out_ref):
    for h in range(pair_ref.shape[0]):
        start = held_ref[h] + came_ref[h]
        sum_ref[h] = start
        pair = pair_ref[h]
        out_ref[h] = (mm(pair[:, DV:], start) + pair[:, :DV].astype(F32)).astype(BF16)


def middle_kernel(upper_ref, own_ref, other_ref, held_ref, came_ref, keep_ref, send_ref):
    upper = upper_ref[0] == 1
    for h in range(own_ref.shape[0]):
        start = held_ref[h] + came_ref[h]
        one = jnp.where(upper, other_ref[h].astype(F32), own_ref[h].astype(F32))
        middle = mm(one[:, DV:].astype(BF16), start) + one[:, :DV]
        start = start.astype(F32)
        keep_ref[h] = jnp.where(upper, middle, start).astype(BF16)
        send_ref[h] = jnp.where(upper, start, middle).astype(BF16)


def project_kernel(
    place_ref, out_ref, gain_ref, z_ref, keep_ref, came_ref, norm_ref, w_ref, send_ref, stay_ref
):
    rows = z_ref.shape[0] // 2
    heads = z_ref.shape[1] // DV
    half = heads // 2
    core, upper = place_ref[1], place_ref[2]
    gated = []
    for h in range(heads):
        at = slice(h * DV, (h + 1) * DV)
        kept = keep_ref[h % half].astype(F32)
        came = came_ref[h % half].astype(F32)
        start = jnp.where(upper == h // half, kept, came).astype(BF16)
        core_out = out_ref[:, at] + mm(gain_ref[:, at], start)
        mean = jnp.mean(core_out * core_out, axis=1, keepdims=True)
        z = z_ref[:, at].astype(F32)
        gate = z / (1.0 + jnp.exp(-z))
        gated.append((core_out * lax.rsqrt(mean + 1e-6) * norm_ref[...] * gate).astype(BF16))
    gated = jnp.concatenate(gated, axis=1)
    wide = w_ref.shape[1]
    step = min(wide, 512)
    for at in range(0, wide, step):
        partial = mm(gated, w_ref[:, at : at + step])
        one, two = partial[:rows], partial[rows:]
        send_ref[:, at : at + step] = jnp.where(core == 0, two, one).astype(BF16)
        stay_ref[:, at : at + step] = jnp.where(core == 0, one, two)


def project_part(place, rows, out, gain, z, keep, came, norm_gain, weight):
    width = z.shape[1]
    wide = weight.shape[1]
    half = keep.shape[0]
    block = lambda i, place: (place[0], 0)
    fixed = lambda i, place: (0, 0)
    return pl.pallas_call(
        project_kernel,
        grid_spec=pltpu.PrefetchScalarGridSpec(
            num_scalar_prefetch=1,
            grid=(1,),
            in_specs=[
                pl.BlockSpec((2 * rows, width), block),
                pl.BlockSpec((2 * rows, width), block),
                pl.BlockSpec((2 * rows, width), block),
                pl.BlockSpec((half, DK, DV), lambda i, place: (0, 0, 0)),
                pl.BlockSpec((half, DK, DV), lambda i, place: (0, 0, 0)),
                pl.BlockSpec((1, DV), fixed),
                pl.BlockSpec(weight.shape, fixed),
            ],
            out_specs=[pl.BlockSpec((rows, wide), fixed)] * 2,
        ),
        out_shape=[
            jax.ShapeDtypeStruct((rows, wide), BF16),
            jax.ShapeDtypeStruct((rows, wide), F32),
        ],
        compiler_params=pltpu.CompilerParams(vmem_limit_bytes=PROJECT_VMEM),
        cost_estimate=pl.CostEstimate(
            flops=2 * rows * 2 * width * wide, bytes_accessed=2 * weight.size, transcendentals=0
        ),
        name="project_part",
    )(place, out, gain, z, keep, came, norm_gain, weight)


def on_device(
    query, keys, values, gate_logit, beta_logit, decay_rate, norm_gain, gate_z, out_weight
):
    shards, cores = lax.axis_size("seq"), lax.axis_size("head")
    seq, head = lax.axis_index("seq"), lax.axis_index("head")
    key_heads = query.shape[1] // DK
    groups = key_heads // 2
    half = 2 * groups
    upper = lax.rem(seq, 2)
    flag = upper.reshape(1)
    rate = decay_rate.reshape(-1, 1)
    arrays = (query, keys, values, gate_logit.T, beta_logit.T, rate)

    away, out, gain = local_part((1 - upper).reshape(1), groups, *arrays, None)
    other = lax.ppermute(away, "seq", [(s, s ^ 1) for s in range(shards)])
    own, out, gain = local_part(flag, groups, *arrays, (out, gain))

    state = (half, DK, DV)
    pair = small_call(pair_kernel, flag, (own, other), [own.shape], half * 2**23)[0]
    held = jnp.zeros(state, BF16)
    ending = pair[:, :, :DV]
    came = None
    for step in range(shards // 2 - 1):
        if step:
            held, ending = small_call(hop_kernel, flag, (pair, held, came), [state] * 2, half * 2**22)
        came = lax.ppermute(
            ending, "seq", [(2 * step + i, 2 * step + 2 + i) for i in range(2)]
        )
    keep, send = small_call(middle_kernel, flag, (own, other, held, came), [state] * 2, half * 2**22)
    back = lax.ppermute(send, "seq", [(s, s ^ 1) for s in range(shards)])

    chips = cores // 2
    chip, core = head // 2, lax.rem(head, 2)
    rows = query.shape[0] // cores
    norm_gain = norm_gain.reshape(1, -1)
    swap = [(i, i ^ 1) for i in range(cores)]
    arrived = []
    for by in list(range(1, chips)) + [0]:
        target = lax.rem(chip + by, chips)
        place = jnp.stack([target, core, upper])
        give, stay = project_part(
            place, rows, out, gain, gate_z, keep, back, norm_gain, out_weight
        )
        both = stay + lax.ppermute(give, "head", swap).astype(F32)
        if by:
            moves = [(i, (i + 2 * by) % cores) for i in range(cores)]
            arrived.append(lax.ppermute(both.astype(BF16), "head", moves))
    for part in arrived:
        both = both + part.astype(F32)
    return both.astype(BF16)


def solution(mesh):
    return jax.shard_map(
        on_device,
        mesh=mesh,
        in_specs=(
            P("seq", "head"),
            P("seq", "head"),
            P("seq", "head"),
            P("seq", "head"),
            P("seq", "head"),
            P("head"),
            P(),
            P("seq", "head"),
            P("head", None),
        ),
        out_specs=P(("seq", "head"), None),
        check_vma=False,
    )
```

time: 120 us -> 67.2 us (0.56)
  the two profiles are of different devices: /device:TPU:26 before, /device:TPU:24 now
where the time goes in v2:
time: 67.2 us; the launch traced here: 66.8 us
  waiting for transfers between devices  30.2 us (45%)
  Pallas kernels  21.2 us (32%)
  local copies, waits for them, and re-layouts  7.17 us (11%)
  starting transfers between devices  7.03 us (10%)
  other arithmetic  1.19 us (2%)
    pallas_call x2, Pallas kernels, local_part(): pl.pallas_call(local_kernel, grid_spec=pltpu.PrefetchScalarGridSpec(num_s...  15.7 us
    ppermute x3, waiting for transfers between devices, on_device(): lax.ppermute(ending, 'seq', [(2 * step + i, 2 * step + 2 + i) for i in ra...  13.4 us
    ppermute x1, waiting for transfers between devices, on_device(): arrived.append(lax.ppermute(both.astype(BF16), 'head', moves))  12.4 us
    unnamed x16, local copies, waits for them, and re-layouts  5.81 us
    pallas_call x2, Pallas kernels, project_part(): pl.pallas_call(project_kernel, grid_spec=pltpu.PrefetchScalarGridSpec(num...  4.64 us
    ppermute x1, waiting for transfers between devices, on_device(): back = lax.ppermute(send, 'seq', [(s, s ^ 1) for s in range(shards)])  4.38 us
    ppermute x3, starting transfers between devices, on_device(): lax.ppermute(ending, 'seq', [(2 * step + i, 2 * step + 2 + i) for i in ra...  2.81 us
    ppermute x1, starting transfers between devices, on_device(): arrived.append(lax.ppermute(both.astype(BF16), 'head', moves))  1.56 us
  transfers between devices with their start and end apart: 8, of which 3 were waited for; matrix products, arithmetic and copies ran while one was open for 0% of the time, Pallas kernels for 15%

profile of v2, /device:TPU:24, one launch (start us, length us, event | category | flops | bytes accessed | tf_op | source)
XLA Modules:
  0.0 66.8 jit_solution(12214188861361499608)
XLA Ops:
  0.0 1.3 %copy.13.rate_ref = f32[8,1]{1,0:T(8,128)} copy(f32[8,1]{0,1:T(1,128)} %bitcast.11) | data formatting | bytes 64 | tf_op jit(solution)/shard_map/reshape | solution.py:375
  1.3 7.8 %local_part.2 = (bf16[4,128,256]{2,1,0:T(8,128)(2,1)}, f32[512,1024]{1,0:T(8,128)}, bf16[512,1024]{1,0:T(8,128)(2,1)}) custom-call(s32[1]{0:T(128)} %bitcast.6.place_ref, bf16[512,512]{1,0:T(8,128)(2,1)} %q_ref.3, bf16[512,512]{1,0:T(8,128)(2,1)} %k_ref.3, bf16[512,1024]{1,0:T(8,128)(2,1)} %v_ref.3, f32[8,512]{1,0:T(8,128)} %bitcast.12, f32[8,512]{1,0:T(8,128)} %bitcast.14, ...), custom_call_target="tpu_custom_call" | custom-call | flops 3758096384 | bytes 2097152 | tf_op jit(solution)/shard_map/local_part/pallas_call | solution.py:236
  9.2 1.5 %collective-permute-start = (bf16[4,128,256]{2,1,0:T(8,128)(2,1)}, bf16[4,128,256]{2,1,0:T(8,128)(2,1)S(1)}, u32[]{:S(2)}, u32[]{:S(2)}) collective-permute-start(bf16[4,128,256]{2,1,0:T(8,128)(2,1)} %get-tuple-element.26), channel_id=1, source_target_pairs={{0,4},{4,0},{8,12},{12,8},{16,20},{20,16},{24,28},{28,24},{1,5},{5... | collective-permute-start | bytes 786440 | tf_op jit(solution)/shard_map/ppermute | solution.py:379
  10.7 0.0 copy-start.7
  10.7 7.9 %local_part.3 = (bf16[4,128,256]{2,1,0:T(8,128)(2,1)}, f32[512,1024]{1,0:T(8,128)}, bf16[512,1024]{1,0:T(8,128)(2,1)}) custom-call(s32[1]{0:T(128)} %bitcast.2.place_ref.upper_ref, bf16[512,512]{1,0:T(8,128)(2,1)} %q_ref.3, bf16[512,512]{1,0:T(8,128)(2,1)} %k_ref.3, bf16[512,1024]{1,0:T(8,128)(2,1)} %v_ref.3, ...), custom_call_target="tpu_custom_call", output_to_operand_aliasing={{1}: (7, {}), {2}: (8, {})} | custom-call | flops 3758096384 | bytes 2097152 | tf_op jit(solution)/shard_map/local_part/pallas_call | solution.py:236
  18.6 0.0 copy-start.2
  18.6 0.0 collective-permute-done.other_ref
  18.6 0.0 copy-start.6
  18.6 1.1 %copy-done.6 = bf16[4,128,256]{2,1,0:T(8,128)(2,1)S(1)} copy-done((bf16[4,128,256]{2,1,0:T(8,128)(2,1)S(1)}, bf16[4,128,256]{2,1,0:T(8,128)(2,1)}, u32[]{:S(2)}) %copy-start.6) | copy-done | bytes 262168
  19.7 0.2 pair_kernel.1.pair_ref
  19.9 0.7 %collective-permute-start.1 = (bf16[4,128,128]{2,1,0:T(8,128)(2,1)S(1)}, bf16[4,128,128]{2,1,0:T(8,128)(2,1)S(1)}, u32[]{:S(2)}, u32[]{:S(2)}) collective-permute-start(bf16[4,128,128]{2,1,0:T(8,128)(2,1)S(1)} %slice.4), channel_id=1, source_target_pairs={{0,8},{4,12},{1,9},{5,13},{2,10},{6,14},{3,11},{7,15}} | collective-permute-start | bytes 393224 | tf_op jit(solution)/shard_map/ppermute | solution.py:390
  20.6 0.0 collective-permute-done.1.came_ref
  20.7 0.2 hop_kernel.2
  20.8 0.7 %collective-permute-start.2 = (bf16[4,128,128]{2,1,0:T(8,128)(2,1)S(1)}, bf16[4,128,128]{2,1,0:T(8,128)(2,1)S(1)}, u32[]{:S(2)}, u32[]{:S(2)}) collective-permute-start(bf16[4,128,128]{2,1,0:T(8,128)(2,1)S(1)} %get-tuple-element.28), channel_id=1, source_target_pairs={{8,16},{12,20},{9,17},{13,21},{10,18},{14,22},{11,19},{15,23}} | collective-permute-start | bytes 393224 | tf_op jit(solution)/shard_map/ppermute | solution.py:390
  21.5 0.0 collective-permute-done.2.came_ref
  21.5 0.2 hop_kernel.3
  21.7 1.5 %collective-permute-start.3 = (bf16[4,128,128]{2,1,0:T(8,128)(2,1)S(1)}, bf16[4,128,128]{2,1,0:T(8,128)(2,1)S(1)}, u32[]{:S(2)}, u32[]{:S(2)}) collective-permute-start(bf16[4,128,128]{2,1,0:T(8,128)(2,1)S(1)} %get-tuple-element.30), channel_id=1, source_target_pairs={{16,24},{20,28},{17,25},{21,29},{18,26},{22,30},{19,27},{23,31}} | collective-permute-start | bytes 393224 | tf_op jit(solution)/shard_map/ppermute | solution.py:390
  23.2 13.4 %collective-permute-done.3.came_ref = bf16[4,128,128]{2,1,0:T(8,128)(2,1)S(1)} collective-permute-done((bf16[4,128,128]{2,1,0:T(8,128)(2,1)S(1)}, bf16[4,128,128]{2,1,0:T(8,128)(2,1)S(1)}, u32[]{:S(2)}, u32[]{:S(2)}) %collective-permute-start.3) | collective-permute-done | bytes 131104 | tf_op jit(solution)/shard_map/ppermute | solution.py:390
  36.6 0.2 middle_kernel.1
  36.8 0.6 collective-permute-start.4
  37.3 0.1 add_add_fusion
  37.4 4.4 %collective-permute-done.4.came_ref = bf16[4,128,128]{2,1,0:T(8,128)(2,1)S(1)} collective-permute-done((bf16[4,128,128]{2,1,0:T(8,128)(2,1)S(1)}, bf16[4,128,128]{2,1,0:T(8,128)(2,1)S(1)}, u32[]{:S(2)}, u32[]{:S(2)}) %collective-permute-start.4) | collective-permute-done | bytes 131104 | tf_op jit(solution)/shard_map/ppermute | solution.py:394
  41.8 0.0 copy-done.7
  41.8 0.0 copy-done.2
  41.8 0.0 copy-start
  41.8 2.2 %copy-done = bf16[1024,2048]{1,0:T(8,128)(2,1)S(1)} copy-done((bf16[1024,2048]{1,0:T(8,128)(2,1)S(1)}, bf16[1024,2048]{1,0:T(8,128)(2,1)}, u32[]{:S(2)}) %copy-start) | copy-done | bytes 4194328
  44.0 0.0 copy-start.3
  44.0 1.2 %copy-done.3 = bf16[512,1024]{1,0:T(8,128)(2,1)S(1)} copy-done((bf16[512,1024]{1,0:T(8,128)(2,1)S(1)}, bf16[512,1024]{1,0:T(8,128)(2,1)}, u32[]{:S(2)}) %copy-start.3) | copy-done | bytes 1048600
  45.2 0.0 copy-start.5
  45.2 1.2 %copy-done.5 = bf16[512,1024]{1,0:T(8,128)(2,1)S(1)} copy-done((bf16[512,1024]{1,0:T(8,128)(2,1)S(1)}, bf16[512,1024]{1,0:T(8,128)(2,1)}, u32[]{:S(2)}) %copy-start.5) | copy-done | bytes 1048600
  46.4 0.0 copy-start.1
  46.4 0.0 copy-start.4
  46.4 2.3 %project_part.3 = (bf16[128,2048]{1,0:T(8,128)(2,1)S(1)}, f32[128,2048]{1,0:T(8,128)S(1)}) custom-call(s32[3]{0:T(128)S(1)} %get-tuple-element.38.place_ref, f32[512,1024]{1,0:T(8,128)S(1)} %copy-done.2, bf16[512,1024]{1,0:T(8,128)(2,1)S(1)} %copy-done.5, bf16[512,1024]{1,0:T(8,128)(2,1)S(1)} %copy-done.3, ...), custom_call_target="tpu_custom_call" | custom-call | flops 1073741824 | bytes 4194304 | tf_op jit(solution)/shard_map/project_part/pallas_call | solution.py:337
  48.8 0.1 collective-permute-start.6
  48.9 0.0 copy-done.1
  48.9 0.1 copy-done.4
  48.9 2.3 %project_part.2 = (bf16[128,2048]{1,0:T(8,128)(2,1)S(1)}, f32[128,2048]{1,0:T(8,128)S(1)}) custom-call(s32[3]{0:T(128)S(1)} %get-tuple-element.37.place_ref, f32[512,1024]{1,0:T(8,128)S(1)} %copy-done.2, bf16[512,1024]{1,0:T(8,128)(2,1)S(1)} %copy-done.5, bf16[512,1024]{1,0:T(8,128)(2,1)S(1)} %copy-done.4, ...), custom_call_target="tpu_custom_call" | custom-call | flops 1073741824 | bytes 4194304 | tf_op jit(solution)/shard_map/project_part/pallas_call | solution.py:337
  51.2 0.5 collective-permute-start.5
  51.8 0.0 collective-permute-done.6
  51.8 0.1 add_convert_fusion.1
  51.9 1.6 %collective-permute-start.7 = (bf16[128,2048]{1,0:T(8,128)(2,1)S(1)}, bf16[128,2048]{1,0:T(8,128)(2,1)S(1)}, u32[]{:S(2)}, u32[]{:S(2)}) collective-permute-start(bf16[128,2048]{1,0:T(8,128)(2,1)S(1)} %add_convert_fusion.1), channel_id=1, source_target_pairs={{0,2},{1,3},{2,0},{3,1},{4,6},{5,7},{6,4},{7,5},{8,10},{9,11},{10,... | collective-permute-start | bytes 1572872 | tf_op jit(solution)/shard_map/ppermute | solution.py:411
  53.4 0.0 collective-permute-done.5
  53.4 12.4 %collective-permute-done.7 = bf16[128,2048]{1,0:T(8,128)(2,1)S(1)} collective-permute-done((bf16[128,2048]{1,0:T(8,128)(2,1)S(1)}, bf16[128,2048]{1,0:T(8,128)(2,1)S(1)}, u32[]{:S(2)}, u32[]{:S(2)}) %collective-permute-start.7) | collective-permute-done | bytes 524320 | tf_op jit(solution)/shard_map/ppermute | solution.py:411
  65.8 1.0 %add_convert_fusion = bf16[128,2048]{1,0:T(8,128)(2,1)} fusion(bf16[128,2048]{1,0:T(8,128)(2,1)S(1)} %collective-permute-done.7, f32[128,2048]{1,0:T(8,128)S(1)} %get-tuple-element.33, bf16[128,2048]{1,0:T(8,128)(2,1)S(1)} %collective-permute-done.5), kind=kLoop, calls=%fused_computation | loop fusion | flops 1310720 | bytes 2621440 | tf_op jit(solution)/shard_map/convert_element_type | solution.py:414
  (2 shorter events, 0.0 us)
Async XLA Ops:
  9.2 9.4 %collective-permute-start = (bf16[4,128,256]{2,1,0:T(8,128)(2,1)}, bf16[4,128,256]{2,1,0:T(8,128)(2,1)S(1)}, u32[]{:S(2)}, u32[]{:S(2)}) collective-permute-start(bf16[4,128,256]{2,1,0:T(8,128)(2,1)} %get-tuple-element.26), channel_id=1, source_target_pairs={{0,4},{4,0},{8,12},{12,8},{16,20},{20,16},{24,28},{28,24},{1,5},{5... | collective-permute-start | bytes 786440 | tf_op jit(solution)/shard_map/ppermute | solution.py:379
  10.7 31.1 %copy-start.7 = (f32[128]{0:T(128)S(1)}, f32[128]{0:T(128)}, u32[]{:S(2)}) copy-start(f32[128]{0:T(128)} %param.15) | copy-start | bytes 1540
  18.6 23.2 %copy-start.2 = (f32[512,1024]{1,0:T(8,128)S(1)}, f32[512,1024]{1,0:T(8,128)}, u32[]{:S(2)}) copy-start(f32[512,1024]{1,0:T(8,128)} %get-tuple-element.23.out_ref) | copy-start | bytes 6291460
  18.6 1.1 %copy-start.6 = (bf16[4,128,256]{2,1,0:T(8,128)(2,1)S(1)}, bf16[4,128,256]{2,1,0:T(8,128)(2,1)}, u32[]{:S(2)}) copy-start(bf16[4,128,256]{2,1,0:T(8,128)(2,1)} %get-tuple-element.25.own_ref) | copy-start | bytes 786436
  19.9 0.7 %collective-permute-start.1 = (bf16[4,128,128]{2,1,0:T(8,128)(2,1)S(1)}, bf16[4,128,128]{2,1,0:T(8,128)(2,1)S(1)}, u32[]{:S(2)}, u32[]{:S(2)}) collective-permute-start(bf16[4,128,128]{2,1,0:T(8,128)(2,1)S(1)} %slice.4), channel_id=1, source_target_pairs={{0,8},{4,12},{1,9},{5,13},{2,10},{6,14},{3,11},{7,15}} | collective-permute-start | bytes 393224 | tf_op jit(solution)/shard_map/ppermute | solution.py:390
  20.8 0.7 %collective-permute-start.2 = (bf16[4,128,128]{2,1,0:T(8,128)(2,1)S(1)}, bf16[4,128,128]{2,1,0:T(8,128)(2,1)S(1)}, u32[]{:S(2)}, u32[]{:S(2)}) collective-permute-start(bf16[4,128,128]{2,1,0:T(8,128)(2,1)S(1)} %get-tuple-element.28), channel_id=1, source_target_pairs={{8,16},{12,20},{9,17},{13,21},{10,18},{14,22},{11,19},{15,23}} | collective-permute-start | bytes 393224 | tf_op jit(solution)/shard_map/ppermute | solution.py:390
  21.7 14.8 %collective-permute-start.3 = (bf16[4,128,128]{2,1,0:T(8,128)(2,1)S(1)}, bf16[4,128,128]{2,1,0:T(8,128)(2,1)S(1)}, u32[]{:S(2)}, u32[]{:S(2)}) collective-permute-start(bf16[4,128,128]{2,1,0:T(8,128)(2,1)S(1)} %get-tuple-element.30), channel_id=1, source_target_pairs={{16,24},{20,28},{17,25},{21,29},{18,26},{22,30},{19,27},{23,31}} | collective-permute-start | bytes 393224 | tf_op jit(solution)/shard_map/ppermute | solution.py:390
  36.8 5.0 %collective-permute-start.4 = (bf16[4,128,128]{2,1,0:T(8,128)(2,1)S(1)}, bf16[4,128,128]{2,1,0:T(8,128)(2,1)S(1)}, u32[]{:S(2)}, u32[]{:S(2)}) collective-permute-start(bf16[4,128,128]{2,1,0:T(8,128)(2,1)S(1)} %get-tuple-element.32), channel_id=1, source_target_pairs={{0,4},{4,0},{8,12},{12,8},{16,20},{20,16},{24,28},{28,24},{1,5},{5... | collective-permute-start | bytes 393224 | tf_op jit(solution)/shard_map/ppermute | solution.py:394
  41.8 2.2 %copy-start = (bf16[1024,2048]{1,0:T(8,128)(2,1)S(1)}, bf16[1024,2048]{1,0:T(8,128)(2,1)}, u32[]{:S(2)}) copy-start(bf16[1024,2048]{1,0:T(8,128)(2,1)} %w_ref.3) | copy-start | bytes 12582916
  44.0 1.2 %copy-start.3 = (bf16[512,1024]{1,0:T(8,128)(2,1)S(1)}, bf16[512,1024]{1,0:T(8,128)(2,1)}, u32[]{:S(2)}) copy-start(bf16[512,1024]{1,0:T(8,128)(2,1)} %z_ref.3) | copy-start | bytes 3145732
  45.2 1.2 %copy-start.5 = (bf16[512,1024]{1,0:T(8,128)(2,1)S(1)}, bf16[512,1024]{1,0:T(8,128)(2,1)}, u32[]{:S(2)}) copy-start(bf16[512,1024]{1,0:T(8,128)(2,1)} %get-tuple-element.24.gain_ref) | copy-start | bytes 3145732
  46.4 2.4 %copy-start.1 = (bf16[1024,2048]{1,0:T(8,128)(2,1)S(1)}, bf16[1024,2048]{1,0:T(8,128)(2,1)}, u32[]{:S(2)}) copy-start(bf16[1024,2048]{1,0:T(8,128)(2,1)} %w_ref.3) | copy-start | bytes 12582916
  46.4 2.5 %copy-start.4 = (bf16[512,1024]{1,0:T(8,128)(2,1)S(1)}, bf16[512,1024]{1,0:T(8,128)(2,1)}, u32[]{:S(2)}) copy-start(bf16[512,1024]{1,0:T(8,128)(2,1)} %z_ref.3) | copy-start | bytes 3145732
  48.8 3.0 %collective-permute-start.6 = (bf16[128,2048]{1,0:T(8,128)(2,1)S(1)}, bf16[128,2048]{1,0:T(8,128)(2,1)S(1)}, u32[]{:S(2)}, u32[]{:S(2)}) collective-permute-start(bf16[128,2048]{1,0:T(8,128)(2,1)S(1)} %get-tuple-element.36), channel_id=1, source_target_pairs={{0,1},{1,0},{2,3},{3,2},{4,5},{5,4},{6,7},{7,6},{8,9},{9,8},{10,11... | collective-permute-start | bytes 1572872 | tf_op jit(solution)/shard_map/ppermute | solution.py:408
  51.2 2.2 %collective-permute-start.5 = (bf16[128,2048]{1,0:T(8,128)(2,1)S(1)}, bf16[128,2048]{1,0:T(8,128)(2,1)S(1)}, u32[]{:S(2)}, u32[]{:S(2)}) collective-permute-start(bf16[128,2048]{1,0:T(8,128)(2,1)S(1)} %get-tuple-element.34), channel_id=1, source_target_pairs={{0,1},{1,0},{2,3},{3,2},{4,5},{5,4},{6,7},{7,6},{8,9},{9,8},{10,11... | collective-permute-start | bytes 1572872 | tf_op jit(solution)/shard_map/ppermute | solution.py:408
  51.9 14.0 %collective-permute-start.7 = (bf16[128,2048]{1,0:T(8,128)(2,1)S(1)}, bf16[128,2048]{1,0:T(8,128)(2,1)S(1)}, u32[]{:S(2)}, u32[]{:S(2)}) collective-permute-start(bf16[128,2048]{1,0:T(8,128)(2,1)S(1)} %add_convert_fusion.1), channel_id=1, source_target_pairs={{0,2},{1,3},{2,0},{3,1},{4,6},{5,7},{6,4},{7,5},{8,10},{9,11},{10,... | collective-permute-start | bytes 1572872 | tf_op jit(solution)/shard_map/ppermute | solution.py:411

commit v3 on v2

v3 whole, which is shorter than its diff:
```python
import functools

import jax
import jax.numpy as jnp
from jax import lax
from jax.experimental import pallas as pl
from jax.experimental.pallas import tpu as pltpu
from jax.sharding import PartitionSpec as P

DK = 128
DV = 128
CHUNK = 256
F32 = jnp.float32
BF16 = jnp.bfloat16
NEG = -1e30
DELTA_VMEM = 20 * 1024 * 1024
OUTPUT_VMEM = 12 * 1024 * 1024
PROJECT_VMEM = 24 * 1024 * 1024


def mm(left, right):
    return lax.dot_general(left, right, (((1,), (0,)), ((), ())), preferred_element_type=F32)


def mm_nt(left, right):
    return lax.dot_general(left, right, (((1,), (1,)), ((), ())), preferred_element_type=F32)


def iota(shape, dim):
    return lax.broadcasted_iota(jnp.int32, shape, dim)


def split3(x):
    hi = x.astype(BF16).astype(F32)
    mid = (x - hi).astype(BF16).astype(F32)
    return hi, mid, x - hi - mid


def softplus(x):
    small = jnp.exp(-jnp.abs(x))
    one = 1.0 + small
    log1p = jnp.where(one == 1.0, small, jnp.log(one) * (small / jnp.where(one == 1.0, 1.0, one - 1.0)))
    return jnp.maximum(x, 0.0) + log1p


def log_inverse_norm(x, rows):
    square = x.astype(F32) * x.astype(F32)
    high = square.astype(BF16)
    low = (square - high.astype(F32)).astype(BF16)
    ones = jnp.ones((rows, x.shape[1]), BF16)
    return -0.5 * jnp.log(mm_nt(ones, high) + mm_nt(ones, low) + 1e-6)


def odd_rows(x, n):
    return jnp.concatenate([x[i + n : i + 2 * n] for i in range(0, x.shape[0], 2 * n)], axis=0)


def weave(even, odd, n):
    parts = []
    for at in range(0, odd.shape[0], n):
        parts.append(even[2 * at : 2 * at + n])
        parts.append(odd[at : at + n])
    return jnp.concatenate(parts, axis=0)


def as_mask(where):
    return jnp.where(where, 1.0, 0.0).astype(BF16)


def unit_lower_inverses(lowers):
    size = lowers[0].shape[0]
    half = size // 2
    row, col = iota((size, size), 0), iota((size, size), 1)
    crow, ccol = iota((half, size), 0), iota((half, size), 1)
    zeros = jnp.zeros((size, size), BF16)
    eye, pair = as_mask(row == col), as_mask(row // 2 == col // 2)
    xs = [eye - lower * pair for lower in lowers]
    n = 2
    while n < size:
        if n < 16:
            mask = as_mask((row // n == col // n + 1) & (row // (2 * n) == col // (2 * n)))
            ys = [mm(lower * mask, x).astype(BF16) for lower, x in zip(lowers, xs)]
            zs = [mm(x, y).astype(BF16) for x, y in zip(xs, ys)]
            xs = [x - z for x, z in zip(xs, zs)]
        elif n < half:
            mask = as_mask(ccol // n == 2 * (crow // n))
            ys = [mm(odd_rows(lower, n) * mask, x).astype(BF16) for lower, x in zip(lowers, xs)]
            odds = [odd_rows(x, n) for x in xs]
            zs = [mm(odd, weave(zeros, y, n)).astype(BF16) for odd, y in zip(odds, ys)]
            xs = [weave(x, odd - z, n) for x, odd, z in zip(xs, odds, zs)]
        else:
            ys = [mm(lower[half:, :half], x[:half, :half]).astype(BF16) for lower, x in zip(lowers, xs)]
            zs = [mm(x[half:, half:], y).astype(BF16) for x, y in zip(xs, ys)]
            xs = [
                jnp.concatenate([x[:half], jnp.concatenate([-z, x[half:, half:]], axis=1)], axis=0)
                for x, z in zip(xs, zs)
            ]
        n *= 2
    return xs


def decayed(c, b, product, mask):
    h = CHUNK // 2

    def quarter(i, j):
        arg = c[i * h : (i + 1) * h] - b[:, j * h : (j + 1) * h]
        if i == j:
            arg = jnp.where(mask, arg, NEG)
        return (jnp.exp(arg) * product[i * h : (i + 1) * h, j * h : (j + 1) * h]).astype(BF16)

    top = jnp.concatenate([quarter(0, 0), jnp.zeros((h, h), BF16)], axis=1)
    return jnp.concatenate([top, jnp.concatenate([quarter(1, 0), quarter(1, 1)], axis=1)], axis=0)


def chosen(x, second):
    half = x.shape[0] // 2
    return jnp.where(second, jnp.concatenate([x[half:], x[:half]], axis=0), x)


def delta_kernel(rate, gate, beta, k_ref, v_ref, second, ends_ref, resid_ref, held_ref, cumul_ref, log_ref):
    tokens = k_ref.shape[0]
    heads = gate.shape[0]
    groups = k_ref.shape[1] // DK
    chunks = [slice(at, at + CHUNK) for at in range(0, tokens, CHUNK)]

    diagonal = iota((heads, heads), 0) == iota((heads, heads), 1)
    rate = jnp.sum(jnp.where(diagonal, rate, 0.0), axis=1, keepdims=True)
    decay = -chosen(rate, second) * softplus(chosen(gate, second))
    log_beta = -softplus(-chosen(beta, second))
    log_k = log_norms(k_ref, heads)

    row, col = iota((CHUNK, CHUNK), 0), iota((CHUNK, CHUNK), 1)
    upto = jnp.where(row <= col, 1.0, 0.0).astype(BF16)
    sums = mm(
        jnp.concatenate([p for here in chunks for p in split3(decay[:, here])], axis=0).astype(BF16), upto
    )
    square = CHUNK // 2
    strict = iota((square, square), 1) < iota((square, square), 0)

    lowers, rights, ended, decays = {}, {}, {}, {}
    for c, here in enumerate(chunks):
        parts = [sums[(3 * c + i) * heads : (3 * c + i + 1) * heads] for i in range(3)]
        cumul = parts[0] + parts[1] + parts[2]
        end = cumul[:, CHUNK - 1 :]
        lb, lk = log_beta[:, here], log_k[:, here]
        col_log = cumul - lk
        row_lower = cumul + lb + lk
        cumul_ref[:, here] = cumul
        log_ref[:, here] = col_log
        key_end = jnp.exp(end - cumul + lk)
        ends = jnp.exp(end)
        columns = jnp.concatenate([row_lower, jnp.exp(lb), jnp.exp(row_lower)], axis=0).T
        for g in range(groups):
            k = k_ref[here, g * DK : (g + 1) * DK]
            k32 = k.astype(F32)
            turned = k32.T
            key_key = mm(k, turned.astype(BF16))
            for r in range(2):
                at = 2 * g + r
                c_lower, c_beta, c_weight = (
                    columns[:, heads * i + at : heads * i + at + 1] for i in range(3)
                )
                m = (c, at)
                lowers[m] = decayed(c_lower, col_log[at : at + 1], key_key, strict)
                v32 = v_ref[here, at * DV : (at + 1) * DV].astype(F32)
                rights[m] = jnp.concatenate([c_beta * v32, c_weight * k32], axis=1).astype(BF16)
                ended[m] = (turned * key_end[at : at + 1]).astype(BF16)
                decays[m] = ends[at : at + 1]
    names = list(lowers)
    inverses = dict(zip(names, unit_lower_inverses([lowers[m] for m in names])))
    solved = {m: mm(inverses[m], rights[m]) for m in names}
    state = {}
    all_heads = range(2 * groups)
    for c, here in enumerate(chunks):
        if c == 0:
            resid = {a: jnp.concatenate([solved[c, a][:, :DV], -solved[c, a][:, DV:]], axis=1) for a in all_heads}
            before = iota((DK, DV + DK), 1) == iota((DK, DV + DK), 0) + DV
            before = {a: jnp.where(before, 1.0, 0.0) for a in all_heads}
        else:
            held = {a: state[a].astype(BF16) for a in all_heads}
            for a in all_heads:
                held_ref[c - 1, a] = held[a]
            moved = {a: mm(solved[c, a][:, DV:].astype(BF16), held[a]) for a in all_heads}
            resid = {
                a: jnp.concatenate([solved[c, a][:, :DV] - moved[a][:, :DV], -moved[a][:, DV:]], axis=1)
                for a in all_heads
            }
            before = state
        resid = {a: resid[a].astype(BF16) for a in all_heads}
        for a in all_heads:
            resid_ref[c, a] = resid[a]
        state = {a: decays[c, a] * before[a] + mm(ended[c, a], resid[a]) for a in all_heads}
    for a in all_heads:
        ends_ref[a] = state[a].astype(BF16)


def log_norms(ref, heads):
    tokens = ref.shape[0]
    head_row = iota((heads, tokens), 0)
    total = log_inverse_norm(ref[:, :DK], heads)
    for g in range(1, ref.shape[1] // DK):
        more = log_inverse_norm(ref[:, g * DK : (g + 1) * DK], heads)
        total = jnp.where(head_row < 2 * g, total, more)
    return total


def lanes(source, which, target):
    width = target.shape[1]
    return source.at[:, pl.ds(pl.multiple_of(which * width, 128), width)], target


def started(moves, sems):
    copies = [pltpu.make_async_copy(a, b, sems.at[i]) for i, (a, b) in enumerate(moves)]
    for copy in copies:
        copy.start()
    return copies


def waited(copies):
    for copy in copies:
        copy.wait()


def first_kernel(
    place_ref, rate_hbm, q_hbm, k_hbm, v_hbm, gate_hbm, beta_hbm, ends, resid, held, cumul, logs,
    rate, gate, beta, k_own, v_own, q_away, k_away, v_away, sems
):
    away = place_ref[0]
    moves = [(rate_hbm, rate), (gate_hbm, gate), (beta_hbm, beta)]
    moves += [lanes(k_hbm, away, k_away), lanes(v_hbm, away, v_away)]
    moves += [lanes(k_hbm, 1 - away, k_own), lanes(v_hbm, 1 - away, v_own), lanes(q_hbm, away, q_away)]
    copies = started(moves, sems)
    waited(copies[:5])
    delta_kernel(rate[...], gate[...], beta[...], k_away, v_away, away == 1, ends, resid, held, cumul, logs)
    waited(copies[5:])


def second_kernel(
    place_ref, q_hbm, rate, gate, beta, k_own, v_own, q_away, k_away, cumul_away, logs_away, resid_away, held_away,
    ends, resid, held, cumul, logs, out, gain, q_own, sems
):
    copies = started([lanes(q_hbm, 1 - place_ref[0], q_own)], sems)
    delta_kernel(rate[...], gate[...], beta[...], k_own, v_own, place_ref[0] == 0, ends, resid, held, cumul, logs)
    local_outputs(q_away, k_away, cumul_away, logs_away, resid_away, held_away, out, gain)
    waited(copies)


def in_vmem(array):
    return pltpu.with_memory_space_constraint(array, pltpu.VMEM)


def delta_shapes(tokens, heads):
    half, chunks = heads // 2, tokens // CHUNK
    return [
        pltpu.MemorySpace.VMEM((half, DK, DV + DK), BF16),
        pltpu.MemorySpace.VMEM((chunks, half, CHUNK, DV + DK), BF16),
        pltpu.MemorySpace.VMEM((chunks - 1, half, DK, DV + DK), BF16),
        pltpu.MemorySpace.VMEM((heads, tokens), F32),
        pltpu.MemorySpace.VMEM((heads, tokens), F32),
    ]


def in_hbm(array):
    return pltpu.with_memory_space_constraint(array, pltpu.HBM)


def output_shapes(tokens, heads):
    return [pltpu.MemorySpace.VMEM((tokens, heads // 2 * DV), BF16)] * 2


def first_part(place, rate, query, keys, values, gate_logit, beta_logit):
    heads, tokens = gate_logit.shape
    half = heads // 2
    vmem = pltpu.MemorySpace.VMEM
    key_part, value_part = (tokens, half // 2 * DK), (tokens, half * DV)
    shapes = delta_shapes(tokens, heads) + [
        vmem((1, heads), F32),
        vmem((heads, tokens), F32),
        vmem((heads, tokens), F32),
        vmem(key_part, BF16),
        vmem(value_part, BF16),
        vmem(key_part, BF16),
        vmem(key_part, BF16),
    ]
    return pl.pallas_call(
        first_kernel,
        in_specs=[pl.BlockSpec(memory_space=pltpu.SMEM)] + [pl.BlockSpec(memory_space=pltpu.HBM)] * 6,
        out_specs=[pl.BlockSpec(memory_space=pltpu.VMEM)] * len(shapes),
        out_shape=shapes,
        scratch_shapes=[pltpu.VMEM(value_part, BF16), pltpu.SemaphoreType.DMA((8,))],
        compiler_params=pltpu.CompilerParams(vmem_limit_bytes=DELTA_VMEM),
        cost_estimate=pl.CostEstimate(flops=4 * 10**9, bytes_accessed=2**20, transcendentals=0),
        name="first_part",
    )(place, *map(in_hbm, (rate, query, keys, values, gate_logit, beta_logit)))


def second_part(place, query, *arrays):
    heads, tokens = arrays[1].shape
    key_part = arrays[3].shape
    shapes = delta_shapes(tokens, heads) + output_shapes(tokens, heads)
    shapes += [pltpu.MemorySpace.VMEM(key_part, BF16)]
    return pl.pallas_call(
        second_kernel,
        in_specs=[pl.BlockSpec(memory_space=pltpu.SMEM), pl.BlockSpec(memory_space=pltpu.HBM)]
        + [pl.BlockSpec(memory_space=pltpu.VMEM)] * len(arrays),
        out_specs=[pl.BlockSpec(memory_space=pltpu.VMEM)] * len(shapes),
        out_shape=shapes,
        scratch_shapes=[pltpu.SemaphoreType.DMA((1,))],
        compiler_params=pltpu.CompilerParams(vmem_limit_bytes=DELTA_VMEM),
        cost_estimate=pl.CostEstimate(flops=5 * 10**9, bytes_accessed=2**20, transcendentals=0),
        name="second_part",
    )(place, in_hbm(query), *map(in_vmem, arrays))


def local_outputs(q_ref, k_ref, cumul_ref, log_ref, resid_ref, held_ref, out_ref, gain_ref):
    tokens = q_ref.shape[0]
    heads = cumul_ref.shape[0]
    groups = q_ref.shape[1] // DK
    square = CHUNK // 2
    inclusive = iota((square, square), 1) <= iota((square, square), 0)
    row_mix = cumul_ref[...] + log_norms(q_ref, heads)
    for c in range(tokens // CHUNK):
        here = slice(c * CHUNK, (c + 1) * CHUNK)
        mix = row_mix[:, here]
        columns = jnp.concatenate([mix, jnp.exp(mix)], axis=0).T
        mixings, queries = {}, {}
        for g in range(groups):
            q, k = q_ref[here, g * DK : (g + 1) * DK], k_ref[here, g * DK : (g + 1) * DK]
            query_key = mm_nt(q, k)
            q32 = q.astype(F32)
            for a in (2 * g, 2 * g + 1):
                b_row = log_ref[a : a + 1, here]
                mixings[a] = decayed(columns[:, a : a + 1], b_row, query_key, inclusive)
                queries[a] = columns[:, heads + a : heads + a + 1] * q32
        for a in range(2 * groups):
            result = mm(mixings[a], resid_ref[c, a])
            if c:
                result = result + mm(queries[a].astype(BF16), held_ref[c - 1, a])
                gain = result[:, DV:]
            else:
                gain = result[:, DV:] + queries[a]
            out_ref[here, a * DV : (a + 1) * DV] = result[:, :DV].astype(BF16)
            gain_ref[here, a * DK : (a + 1) * DK] = gain.astype(BF16)


def third_kernel(*refs):
    local_outputs(*refs[:6], *refs[-2:])


def third_part(q, k, cumul, logs, resid, held, after):
    heads, tokens = cumul.shape
    return pl.pallas_call(
        third_kernel,
        in_specs=[pl.BlockSpec(memory_space=pltpu.VMEM)] * 6 + [pl.BlockSpec(memory_space=pl.ANY)],
        out_specs=[pl.BlockSpec(memory_space=pltpu.VMEM)] * 2,
        out_shape=output_shapes(tokens, heads),
        compiler_params=pltpu.CompilerParams(vmem_limit_bytes=OUTPUT_VMEM),
        cost_estimate=pl.CostEstimate(flops=2 * 10**9, bytes_accessed=2**20, transcendentals=0),
        name="third_part",
    )(*map(in_vmem, (q, k, cumul, logs, resid, held)), after)


def small_call(kernel, flag, arrays, out_shapes, flops, after=()):
    return pl.pallas_call(
        kernel,
        in_specs=[pl.BlockSpec(memory_space=pltpu.SMEM)]
        + [pl.BlockSpec(memory_space=pltpu.VMEM)] * len(arrays)
        + [pl.BlockSpec(memory_space=pl.ANY)] * len(after),
        out_specs=[pl.BlockSpec(memory_space=pltpu.VMEM)] * len(out_shapes),
        out_shape=[pltpu.MemorySpace.VMEM(s, BF16) for s in out_shapes],
        cost_estimate=pl.CostEstimate(flops=flops, bytes_accessed=2**18, transcendentals=0),
        name="hand_over",
    )(flag, *map(in_vmem, arrays), *after)


def pair_kernel(upper_ref, own_ref, other_ref, pair_ref, *ending_refs):
    upper = upper_ref[0] == 1
    count = ending_refs[0].shape[0]
    for h in range(own_ref.shape[0]):
        own, other = own_ref[h].astype(F32), other_ref[h].astype(F32)
        one = jnp.where(upper, other, own)
        two = jnp.where(upper, own, other)
        both = mm(two[:, DV:].astype(BF16), one.astype(BF16))
        inject = (both[:, :DV] + two[:, :DV]).astype(BF16)
        ending_refs[h // count][h % count] = inject
        pair_ref[h] = jnp.concatenate([inject, both[:, DV:].astype(BF16)], axis=1)


def hop_kernel(part, came, upper_ref, pair_ref, *refs):
    sum_ref, out_ref = refs[-2:]
    count = sum_ref.shape[0]
    for h in range(count):
        start = refs[0][h]
        for came_ref in refs[1:came]:
            start = start + came_ref[h]
        sum_ref[h] = start
        pair = pair_ref[part * count + h]
        out_ref[h] = (mm(pair[:, DV:], start) + pair[:, :DV].astype(F32)).astype(BF16)


def middle_kernel(part, came, upper_ref, own_ref, other_ref, *refs):
    keep_ref, send_ref = refs[-2:]
    upper = upper_ref[0] == 1
    count = keep_ref.shape[0]
    for h in range(count):
        start = refs[0][h]
        for came_ref in refs[1:came]:
            start = start + came_ref[h]
        at = part * count + h
        one = jnp.where(upper, other_ref[at].astype(F32), own_ref[at].astype(F32))
        middle = mm(one[:, DV:].astype(BF16), start) + one[:, :DV]
        start = start.astype(F32)
        keep_ref[h] = jnp.where(upper, middle, start).astype(BF16)
        send_ref[h] = jnp.where(upper, start, middle).astype(BF16)


def gated_rows(out, gain, z, at, start_refs, norm):
    parts = []
    count = start_refs[0].shape[0]
    for h in range(count * len(start_refs)):
        cols = slice(h * DV, (h + 1) * DV)
        core = out[at, cols].astype(F32) + mm(gain[at, cols], start_refs[h // count][h % count])
        mean = jnp.mean(core * core, axis=1, keepdims=True)
        z_here = z[:, cols].astype(F32)
        gate = z_here / (1.0 + jnp.exp(-z_here))
        parts.append((core * lax.rsqrt(mean + 1e-6) * norm * gate).astype(BF16))
    return jnp.concatenate(parts, axis=1)


def chip_rows(place_ref, rows):
    return pl.ds(pl.multiple_of(place_ref[0] * rows, rows), rows)


def patch(source, row, group, target):
    height, width = target.shape
    at = (
        pl.ds(pl.multiple_of(row * height, height), height),
        pl.ds(pl.multiple_of(group * width, 128), width),
    )
    return source.at[at], target


def bands(source, group, target):
    height = target.shape[0]
    return source.at[pl.ds(pl.multiple_of(group * height, 128), height), :], target


def group_moves(place_ref, group, z_hbm, w_hbm, z, w):
    return [patch(z_hbm, place_ref[0], group, z), bands(w_hbm, group, w)]


def group_buffers(rows, width, wide, make):
    return [make((rows, width), BF16), make((width, wide), BF16)]


def keep_kernel(place_ref, z_hbm, w_hbm, norm_hbm, out, gain, *refs):
    start_refs, (sum_ref, norm, z_away, w_away, z_own, w_own, sems) = refs[:-7], refs[-7:]
    group = place_ref[2]
    moves = [(norm_hbm, norm)] + group_moves(place_ref, group, z_hbm, w_hbm, z_own, w_own)
    moves += group_moves(place_ref, 1 - group, z_hbm, w_hbm, z_away, w_away)
    copies = started(moves, sems)
    waited(copies[:2])
    gated = gated_rows(out, gain, z_own, chip_rows(place_ref, z_own.shape[0]), start_refs, norm[...])
    waited(copies[2:3])
    sum_ref[...] = mm(gated, w_own[...])
    waited(copies[3:])


def keep_part(place, rows, gate_z, weight, norm_gain, out, gain, start):
    wide = weight.shape[1]
    width = weight.shape[0] // 2
    vmem = pltpu.MemorySpace.VMEM
    shapes = [vmem((2 * rows, wide), F32), vmem((1, DV), F32)] + group_buffers(2 * rows, width, wide, vmem)
    return pl.pallas_call(
        keep_kernel,
        in_specs=[pl.BlockSpec(memory_space=pltpu.SMEM)]
        + [pl.BlockSpec(memory_space=pltpu.HBM)] * 3
        + [pl.BlockSpec(memory_space=pltpu.VMEM)] * (2 + len(start)),
        out_specs=[pl.BlockSpec(memory_space=pltpu.VMEM)] * len(shapes),
        out_shape=shapes,
        scratch_shapes=group_buffers(2 * rows, width, wide, pltpu.VMEM) + [pltpu.SemaphoreType.DMA((5,))],
        compiler_params=pltpu.CompilerParams(vmem_limit_bytes=PROJECT_VMEM),
        cost_estimate=pl.CostEstimate(
            flops=4 * rows * width * wide, bytes_accessed=2**20, transcendentals=0
        ),
        name="keep_part",
    )(place, *map(in_hbm, (gate_z, weight, norm_gain)), *map(in_vmem, (out, gain, *start)))


def send_rows(partial, core, send_refs, stay_ref):
    rows, width = send_refs[0].shape
    one, two = partial[:rows], partial[rows:]
    send = jnp.where(core == 0, two, one).astype(BF16)
    for i, ref in enumerate(send_refs):
        ref[...] = send[:, i * width : (i + 1) * width]
    stay_ref[...] = jnp.where(core == 0, one, two)


def away_kernel(place_ref, sum_ref, norm, z, w, out, gain, *refs):
    start_refs, (send_ref, stay_ref) = refs[:-2], refs[-2:]
    gated = gated_rows(out, gain, z, chip_rows(place_ref, z.shape[0]), start_refs, norm[...])
    send_rows(mm(gated, w[...]) + sum_ref[...], place_ref[1], [send_ref], stay_ref)


def away_part(place, kept, out, gain, start):
    rows, wide = kept[0].shape[0] // 2, kept[0].shape[1]
    vmem = pltpu.MemorySpace.VMEM
    arrays = (*kept, out, gain, *start)
    return pl.pallas_call(
        away_kernel,
        in_specs=[pl.BlockSpec(memory_space=pltpu.SMEM)] + [pl.BlockSpec(memory_space=pltpu.VMEM)] * len(arrays),
        out_specs=[pl.BlockSpec(memory_space=pltpu.VMEM)] * 2,
        out_shape=[vmem((rows, wide), BF16), vmem((rows, wide), F32)],
        compiler_params=pltpu.CompilerParams(vmem_limit_bytes=PROJECT_VMEM),
        cost_estimate=pl.CostEstimate(
            flops=4 * rows * kept[-1].size, bytes_accessed=2**20, transcendentals=0
        ),
        name="away_part",
    )(place, *map(in_vmem, arrays))


def whole_kernel(place_ref, z_hbm, w_hbm, norm_hbm, own_out, own_gain, away_out, away_gain, *refs):
    starts, (send_one, send_two, stay_ref, norm, z_own, w_own, z_away, w_away, sems) = refs[:-9], refs[-9:]
    group = place_ref[2]
    moves = [(norm_hbm, norm)] + group_moves(place_ref, group, z_hbm, w_hbm, z_own, w_own)
    moves += group_moves(place_ref, 1 - group, z_hbm, w_hbm, z_away, w_away)
    copies = started(moves, sems)
    waited(copies[:2])
    at = chip_rows(place_ref, z_own.shape[0])
    first = gated_rows(own_out, own_gain, z_own, at, starts[: len(starts) // 2], norm[...])
    waited(copies[2:4])
    second = gated_rows(away_out, away_gain, z_away, at, starts[len(starts) // 2 :], norm[...])
    waited(copies[4:])
    partial = mm(first, w_own[...]) + mm(second, w_away[...])
    send_rows(partial, place_ref[1], [send_one, send_two], stay_ref)


def whole_part(place, rows, gate_z, weight, norm_gain, *arrays):
    wide = weight.shape[1]
    width = weight.shape[0] // 2
    vmem = pltpu.MemorySpace.VMEM
    return pl.pallas_call(
        whole_kernel,
        in_specs=[pl.BlockSpec(memory_space=pltpu.SMEM)]
        + [pl.BlockSpec(memory_space=pltpu.HBM)] * 3
        + [pl.BlockSpec(memory_space=pltpu.VMEM)] * len(arrays),
        out_specs=[pl.BlockSpec(memory_space=pltpu.VMEM)] * 3,
        out_shape=[vmem((rows, wide // 2), BF16)] * 2 + [vmem((rows, wide), F32)],
        scratch_shapes=[pltpu.VMEM((1, DV), F32)]
        + group_buffers(2 * rows, width, wide, pltpu.VMEM) * 2
        + [pltpu.SemaphoreType.DMA((5,))],
        compiler_params=pltpu.CompilerParams(vmem_limit_bytes=PROJECT_VMEM),
        cost_estimate=pl.CostEstimate(
            flops=8 * rows * width * wide, bytes_accessed=2**22, transcendentals=0
        ),
        name="whole_part",
    )(place, *map(in_hbm, (gate_z, weight, norm_gain)), *map(in_vmem, arrays))


def on_device(
    query, keys, values, gate_logit, beta_logit, decay_rate, norm_gain, gate_z, out_weight
):
    shards, cores = lax.axis_size("seq"), lax.axis_size("head")
    seq, head = lax.axis_index("seq"), lax.axis_index("head")
    half = values.shape[1] // DV // 2
    upper = lax.rem(seq, 2)
    flag = upper.reshape(1)
    place = (1 - upper).reshape(1)

    rate, norm_gain = decay_rate.reshape(1, -1), norm_gain.reshape(1, -1)

    away, resid, held, cumul, logs, rate, gate, beta, k_own, v_own, q_away, k_away = first_part(
        place, rate, query, keys, values, gate_logit.T, beta_logit.T
    )
    other = lax.ppermute(away, "seq", [(s, s ^ 1) for s in range(shards)])
    own, resid, held, cumul, logs, out_away, gain_away, q_own = second_part(
        place, query, rate, gate, beta, k_own, v_own, q_away, k_away, cumul, logs, resid, held
    )
    parts = 2 if half % 2 == 0 else 1
    state = (half // parts, DK, DV)
    pair, *endings = small_call(
        pair_kernel, flag, (own, other), [own.shape] + [state] * parts, half * 2**23
    )
    out_own, gain_own = third_part(q_own, k_own, cumul, logs, resid, held, pair)
    came = [[] for _ in range(parts)]
    for step in range(shards // 2 - 1):
        along = [(2 * step + i, 2 * step + 2 + i) for i in range(2)]
        for p in range(parts):
            if step:
                start, endings[p] = small_call(
                    functools.partial(hop_kernel, p, len(came[p])), flag, (pair, *came[p]), [state] * 2, half * 2**22,
                    (out_own,) if step == 1 and p == parts - 1 else (),
                )
                came[p] = [start]
            came[p].append(lax.ppermute(endings[p], "seq", along))
    keep, back = [], []
    for p in range(parts):
        kept, send = small_call(
            functools.partial(middle_kernel, p, len(came[p])), flag, (own, other, *came[p]), [state] * 2, half * 2**22
        )
        keep.append(kept)
        back.append(lax.ppermute(send, "seq", [(s, s ^ 1) for s in range(shards)]))

    chips = cores // 2
    chip, core = head // 2, lax.rem(head, 2)
    rows = query.shape[0] // cores
    swap = [(i, i ^ 1) for i in range(cores)]
    arrived = []
    for by in range(1, chips):
        spot = jnp.stack([lax.rem(chip + by, chips), core, upper])
        kept = keep_part(spot, rows, gate_z, out_weight, norm_gain, out_own, gain_own, keep)
        give, stay = away_part(spot, kept, out_away, gain_away, back)
        both = (stay + lax.ppermute(give, "head", swap).astype(F32)).astype(BF16)
        moves = [(i, (i + 2 * by) % cores) for i in range(cores)]
        arrived.append(lax.ppermute(both, "head", moves))
    spot = jnp.stack([chip, core, upper])
    if arrived:
        spot, both = lax.optimization_barrier((spot, both))
    *gives, stay = whole_part(
        spot, rows, gate_z, out_weight, norm_gain, out_own, gain_own, out_away, gain_away, *keep, *back
    )
    total = stay + jnp.concatenate([lax.ppermute(g, "head", swap) for g in gives], axis=1).astype(F32)
    for part in arrived:
        total = total + part.astype(F32)
    return total.astype(BF16)


def solution(mesh):
    return jax.shard_map(
        on_device,
        mesh=mesh,
        in_specs=(
            P("seq", "head"),
            P("seq", "head"),
            P("seq", "head"),
            P("seq", "head"),
            P("seq", "head"),
            P("head"),
            P(),
            P("seq", "head"),
            P("head", None),
        ),
        out_specs=P(("seq", "head"), None),
        check_vma=False,
    )
```

time: 67.2 us -> 56.3 us (0.84)
  the two profiles are of different devices: /device:TPU:24 before, /device:TPU:26 now
where the time goes in v3:
time: 56.3 us; the launch traced here: 56 us
  Pallas kernels  23.8 us (42%)
  waiting for transfers between devices  18 us (32%)
  starting transfers between devices  9.72 us (17%)
  local copies, waits for them, and re-layouts  2.99 us (5%)
  other arithmetic  1.25 us (2%)
    ppermute x6, waiting for transfers between devices, on_device(): came[p].append(lax.ppermute(endings[p], 'seq', along))  7.26 us
    ppermute x1, waiting for transfers between devices, on_device(): arrived.append(lax.ppermute(both, 'head', moves))  7.18 us
    pallas_call x1, Pallas kernels, second_part(): pl.pallas_call(second_kernel, in_specs=[pl.BlockSpec(memory_space=pltpu.S...  6.36 us
    pallas_call x1, Pallas kernels, first_part(): pl.pallas_call(first_kernel, in_specs=[pl.BlockSpec(memory_space=pltpu.SM...  6.08 us
    ppermute x6, starting transfers between devices, on_device(): came[p].append(lax.ppermute(endings[p], 'seq', along))  5.41 us
    pallas_call x1, Pallas kernels, whole_part(): pl.pallas_call(whole_kernel, in_specs=[pl.BlockSpec(memory_space=pltpu.SM...  4.26 us
    pallas_call x1, Pallas kernels, keep_part(): pl.pallas_call(keep_kernel, in_specs=[pl.BlockSpec(memory_space=pltpu.SME...  3.01 us
    unnamed x8, local copies, waits for them, and re-layouts  2.99 us
  transfers between devices with their start and end apart: 13, of which 7 were waited for; matrix products, arithmetic and copies ran while one was open for 0% of the time, Pallas kernels for 28%

profile of v3, /device:TPU:26, one launch (start us, length us, event | category | flops | bytes accessed | tf_op | source)
XLA Modules:
  0.0 56.0 jit_solution(8580631177534927861)
XLA Ops:
  0.0 6.1 %first_part.1 = (bf16[4,128,256]{2,1,0:T(8,128)(2,1)S(1)}, bf16[2,4,256,256]{3,2,1,0:T(8,128)(2,1)S(1)}, bf16[1,4,128,256]{3,2,1,0:T(8,128)(2,1)S(1)}, f32[8,512...) custom-call(s32[1]{0:T(128)} %bitcast.5.place_ref, ...), custom_call_target="tpu_custom_call" | custom-call | flops 4000000000 | bytes 1048576 | tf_op jit(solution)/shard_map/first_part/pallas_call | solution.py:285
  6.1 1.6 %collective-permute-start = (bf16[4,128,256]{2,1,0:T(8,128)(2,1)S(1)}, bf16[4,128,256]{2,1,0:T(8,128)(2,1)S(1)}, u32[]{:S(2)}, u32[]{:S(2)}) collective-permute-start(bf16[4,128,256]{2,1,0:T(8,128)(2,1)S(1)} %get-tuple-element.69), channel_id=1, source_target_pairs={{0,4},{4,0},{8,12},{12,8},{16,20},{20,16},{24,28},{28,24},{1,5},{5... | collective-permute-start | bytes 786440 | tf_op jit(solution)/shard_map/ppermute | solution.py:575
  7.7 6.4 %second_part.1 = (bf16[4,128,256]{2,1,0:T(8,128)(2,1)S(1)}, bf16[2,4,256,256]{3,2,1,0:T(8,128)(2,1)S(1)}, bf16[1,4,128,256]{3,2,1,0:T(8,128)(2,1)S(1)}, f32[8,51...) custom-call(s32[1]{0:T(128)} %bitcast.5.place_ref, ...), custom_call_target="tpu_custom_call" | custom-call | flops 5000000000 | bytes 1048576 | tf_op jit(solution)/shard_map/second_part/pallas_call | solution.py:302
  14.1 0.0 copy-start.2
  14.1 1.0 %copy-done.2 = bf16[2,4,256,256]{3,2,1,0:T(8,128)(2,1)} copy-done((bf16[2,4,256,256]{3,2,1,0:T(8,128)(2,1)}, bf16[2,4,256,256]{3,2,1,0:T(8,128)(2,1)S(1)}, u32[]{:S(2)}) %copy-start.2) | copy-done | bytes 1048600
  15.0 0.0 collective-permute-done.other_ref
  15.1 0.2 hand_over.7
  15.3 0.7 %collective-permute-start.1 = (bf16[2,128,128]{2,1,0:T(8,128)(2,1)S(1)}, bf16[2,128,128]{2,1,0:T(8,128)(2,1)S(1)}, u32[]{:S(2)}, u32[]{:S(2)}) collective-permute-start(bf16[2,128,128]{2,1,0:T(8,128)(2,1)S(1)} %get-tuple-element.73), channel_id=1, source_target_pairs={{0,8},{4,12},{1,9},{5,13},{2,10},{6,14},{3,11},{7,15}} | collective-permute-start | bytes 196616 | tf_op jit(solution)/shard_map/ppermute | solution.py:595
  16.0 0.7 %collective-permute-start.4 = (bf16[2,128,128]{2,1,0:T(8,128)(2,1)S(1)}, bf16[2,128,128]{2,1,0:T(8,128)(2,1)S(1)}, u32[]{:S(2)}, u32[]{:S(2)}) collective-permute-start(bf16[2,128,128]{2,1,0:T(8,128)(2,1)S(1)} %get-tuple-element.79), channel_id=1, source_target_pairs={{0,8},{4,12},{1,9},{5,13},{2,10},{6,14},{3,11},{7,15}} | collective-permute-start | bytes 196616 | tf_op jit(solution)/shard_map/ppermute | solution.py:595
  16.6 0.0 copy-start.3
  16.7 1.2 %copy-done.3 = bf16[2,4,256,256]{3,2,1,0:T(8,128)(2,1)S(1)} copy-done((bf16[2,4,256,256]{3,2,1,0:T(8,128)(2,1)S(1)}, bf16[2,4,256,256]{3,2,1,0:T(8,128)(2,1)}, u32[]{:S(2)}) %copy-start.3) | copy-done | bytes 1048600
  17.9 1.3 %third_part.1 = (bf16[512,512]{1,0:T(8,128)(2,1)S(1)}, bf16[512,512]{1,0:T(8,128)(2,1)S(1)}) custom-call(bf16[512,256]{1,0:T(8,128)(2,1)S(1)} %get-tuple-element.63.refs_0_, bf16[512,256]{1,0:T(8,128)(2,1)S(1)} %get-tuple-element.55.k_own.refs_1_, f32[8,512]{1,0:T(8,128)S(1)} %get-tuple-element.64.refs_2_, f32[8,512]{1,0:T(8,128)S(1)} %get-tuple-element.65.refs_3_, ...), custom_call_target="tpu_custom_call" | custom-call | flops 2000000000 | bytes 1048576 | tf_op jit(solution)/shard_map/third_part/pallas_call | solution.py:352
  19.2 0.0 copy-start
  19.2 0.8 %copy-done = bf16[512,512]{1,0:T(8,128)(2,1)} copy-done((bf16[512,512]{1,0:T(8,128)(2,1)}, bf16[512,512]{1,0:T(8,128)(2,1)S(1)}, u32[]{:S(2)}) %copy-start) | copy-done | bytes 524312
  20.0 0.0 collective-permute-done.1.refs_0_
  20.0 0.0 copy-start.1
  20.0 0.2 hand_over.8
  20.1 0.8 %collective-permute-start.2 = (bf16[2,128,128]{2,1,0:T(8,128)(2,1)S(1)}, bf16[2,128,128]{2,1,0:T(8,128)(2,1)S(1)}, u32[]{:S(2)}, u32[]{:S(2)}) collective-permute-start(bf16[2,128,128]{2,1,0:T(8,128)(2,1)S(1)} %get-tuple-element.75), channel_id=1, source_target_pairs={{8,16},{12,20},{9,17},{13,21},{10,18},{14,22},{11,19},{15,23}} | collective-permute-start | bytes 196616 | tf_op jit(solution)/shard_map/ppermute | solution.py:595
  21.0 0.0 collective-permute-done.4.refs_0_
  21.0 0.2 hand_over.11
  21.1 0.7 %collective-permute-start.5 = (bf16[2,128,128]{2,1,0:T(8,128)(2,1)S(1)}, bf16[2,128,128]{2,1,0:T(8,128)(2,1)S(1)}, u32[]{:S(2)}, u32[]{:S(2)}) collective-permute-start(bf16[2,128,128]{2,1,0:T(8,128)(2,1)S(1)} %get-tuple-element.81), channel_id=1, source_target_pairs={{8,16},{12,20},{9,17},{13,21},{10,18},{14,22},{11,19},{15,23}} | collective-permute-start | bytes 196616 | tf_op jit(solution)/shard_map/ppermute | solution.py:595
  21.8 0.0 collective-permute-done.2.refs_1_
  21.8 0.2 hand_over.9
  22.0 1.3 %collective-permute-start.3 = (bf16[2,128,128]{2,1,0:T(8,128)(2,1)S(1)}, bf16[2,128,128]{2,1,0:T(8,128)(2,1)S(1)}, u32[]{:S(2)}, u32[]{:S(2)}) collective-permute-start(bf16[2,128,128]{2,1,0:T(8,128)(2,1)S(1)} %get-tuple-element.77), channel_id=1, source_target_pairs={{16,24},{20,28},{17,25},{21,29},{18,26},{22,30},{19,27},{23,31}} | collective-permute-start | bytes 196616 | tf_op jit(solution)/shard_map/ppermute | solution.py:595
  23.3 0.0 collective-permute-done.5.refs_1_
  23.3 0.2 hand_over.12
  23.4 1.3 %collective-permute-start.6 = (bf16[2,128,128]{2,1,0:T(8,128)(2,1)S(1)}, bf16[2,128,128]{2,1,0:T(8,128)(2,1)S(1)}, u32[]{:S(2)}, u32[]{:S(2)}) collective-permute-start(bf16[2,128,128]{2,1,0:T(8,128)(2,1)S(1)} %get-tuple-element.83), channel_id=1, source_target_pairs={{16,24},{20,28},{17,25},{21,29},{18,26},{22,30},{19,27},{23,31}} | collective-permute-start | bytes 196616 | tf_op jit(solution)/shard_map/ppermute | solution.py:595
  24.8 6.6 %collective-permute-done.3.refs_1_ = bf16[2,128,128]{2,1,0:T(8,128)(2,1)S(1)} collective-permute-done((bf16[2,128,128]{2,1,0:T(8,128)(2,1)S(1)}, bf16[2,128,128]{2,1,0:T(8,128)(2,1)S(1)}, u32[]{:S(2)}, u32[]{:S(2)}) %collective-permute-start.3) | collective-permute-done | bytes 65568 | tf_op jit(solution)/shard_map/ppermute | solution.py:595
  31.4 0.2 hand_over.10
  31.6 0.5 collective-permute-start.7
  32.1 0.6 %collective-permute-done.6.refs_1_ = bf16[2,128,128]{2,1,0:T(8,128)(2,1)S(1)} collective-permute-done((bf16[2,128,128]{2,1,0:T(8,128)(2,1)S(1)}, bf16[2,128,128]{2,1,0:T(8,128)(2,1)S(1)}, u32[]{:S(2)}, u32[]{:S(2)}) %collective-permute-start.6) | collective-permute-done | bytes 65568 | tf_op jit(solution)/shard_map/ppermute | solution.py:595
  32.7 0.2 hand_over.13
  32.9 1.0 %collective-permute-start.8 = (bf16[2,128,128]{2,1,0:T(8,128)(2,1)S(1)}, bf16[2,128,128]{2,1,0:T(8,128)(2,1)S(1)}, u32[]{:S(2)}, u32[]{:S(2)}) collective-permute-start(bf16[2,128,128]{2,1,0:T(8,128)(2,1)S(1)} %get-tuple-element.92), channel_id=1, source_target_pairs={{0,4},{4,0},{8,12},{12,8},{16,20},{20,16},{24,28},{28,24},{1,5},{5... | collective-permute-start | bytes 196616 | tf_op jit(solution)/shard_map/ppermute | solution.py:602
  33.9 0.1 add_add_fusion.1.place_ref
  34.0 0.0 copy-done.1
  34.0 3.0 %keep_part.1 = (f32[256,2048]{1,0:T(8,128)S(1)}, f32[1,128]{1,0:T(1,128)S(1)}, bf16[256,512]{1,0:T(8,128)(2,1)S(1)}, bf16[512,2048]{1,0:T(8,128)(2,1)S(1)}) custom-call(s32[3]{0:T(128)S(1)} %add_add_fusion.1.place_ref, bf16[512,1024]{1,0:T(8,128)(2,1)} %z_hbm.3, bf16[1024,2048]{1,0:T(8,128)(2,1)} %w_hbm.3, f32[1,128]{1,0:T(1,128)} %bitcast.9, ...), custom_call_target="tpu_custom_call" | custom-call | flops 536870912 | bytes 1048576 | tf_op jit(solution)/shard_map/keep_part/pallas_call | solution.py:474
  37.0 0.0 collective-permute-done.7.refs_0_.refs_2_
  37.0 0.2 collective-permute-done.8.refs_1_.refs_3_
  37.2 1.6 %away_part.1 = (bf16[128,2048]{1,0:T(8,128)(2,1)S(1)}, f32[128,2048]{1,0:T(8,128)S(1)}) custom-call(s32[3]{0:T(128)S(1)} %add_add_fusion.1.place_ref, f32[256,2048]{1,0:T(8,128)S(1)} %get-tuple-element.85.sum_ref, f32[1,128]{1,0:T(1,128)S(1)} %get-tuple-element.86.norm, bf16[256,512]{1,0:T(8,128)(2,1)S(1)} %get-tuple-element.87.z, ...), custom_call_target="tpu_custom_call" | custom-call | flops 536870912 | bytes 1048576 | tf_op jit(solution)/shard_map/away_part/pallas_call | solution.py:509
  38.9 0.1 collective-permute-start.9
  39.0 1.9 %collective-permute-done.9 = bf16[128,2048]{1,0:T(8,128)(2,1)S(1)} collective-permute-done((bf16[128,2048]{1,0:T(8,128)(2,1)S(1)}, bf16[128,2048]{1,0:T(8,128)(2,1)S(1)}, u32[]{:S(2)}, u32[]{:S(2)}) %collective-permute-start.9) | collective-permute-done | bytes 524320 | tf_op jit(solution)/shard_map/ppermute | solution.py:613
  40.9 0.1 add_convert_fusion.1
  41.0 0.5 collective-permute-start.12
  41.5 0.1 add_add_fusion.place_ref
  41.6 4.3 %whole_part.1 = (bf16[128,1024]{1,0:T(8,128)(2,1)S(1)}, bf16[128,1024]{1,0:T(8,128)(2,1)S(1)}, f32[128,2048]{1,0:T(8,128)S(1)}) custom-call(s32[3]{0:T(128)S(1)} %add_add_fusion.place_ref, bf16[512,1024]{1,0:T(8,128)(2,1)} %z_hbm.3, bf16[1024,2048]{1,0:T(8,128)(2,1)} %w_hbm.3, f32[1,128]{1,0:T(1,128)} %bitcast.10, bf16[512,512]{1,0:T(8,128)(2,1)S(1)} %copy-done.1, ...), custom_call_target="tpu_custom_call" | custom-call | flops 1073741824 | bytes 4194304 | tf_op jit(solution)/shard_map/whole_part/pallas_call | solution.py:542
  45.9 0.1 collective-permute-start.10
  45.9 0.5 collective-permute-start.11
  46.4 1.0 %collective-permute-done.10 = bf16[128,1024]{1,0:T(8,128)(2,1)S(1)} collective-permute-done((bf16[128,1024]{1,0:T(8,128)(2,1)S(1)}, bf16[128,1024]{1,0:T(8,128)(2,1)S(1)}, u32[]{:S(2)}, u32[]{:S(2)}) %collective-permute-start.10) | collective-permute-done | bytes 262176 | tf_op jit(solution)/shard_map/ppermute | solution.py:622
  47.5 0.4 collective-permute-done.11
  47.8 7.2 %collective-permute-done.12 = bf16[128,2048]{1,0:T(8,128)(2,1)S(1)} collective-permute-done((bf16[128,2048]{1,0:T(8,128)(2,1)S(1)}, bf16[128,2048]{1,0:T(8,128)(2,1)S(1)}, u32[]{:S(2)}, u32[]{:S(2)}) %collective-permute-start.12) | collective-permute-done | bytes 524320 | tf_op jit(solution)/shard_map/ppermute | solution.py:615
  55.0 1.0 %add_convert_fusion = bf16[128,2048]{1,0:T(8,128)(2,1)} fusion(bf16[128,2048]{1,0:T(8,128)(2,1)S(1)} %collective-permute-done.12, f32[128,2048]{1,0:T(8,128)S(1)} %get-tuple-element.96, bf16[128,1024]{1,0:T(8,128)(2,1)S(1)} %collective-permute-done.11, bf16[128,1024]{1,0:T(8,128)(2,1)S(1)} %collective-permute-done.10), kind=kLoop, calls=%fused_computation | loop fusion | flops 2097152 | bytes 2621440 | tf_op jit(solution)/shard_map/convert_element_type | solution.py:625
Async XLA Ops:
  6.1 9.0 %collective-permute-start = (bf16[4,128,256]{2,1,0:T(8,128)(2,1)S(1)}, bf16[4,128,256]{2,1,0:T(8,128)(2,1)S(1)}, u32[]{:S(2)}, u32[]{:S(2)}) collective-permute-start(bf16[4,128,256]{2,1,0:T(8,128)(2,1)S(1)} %get-tuple-element.69), channel_id=1, source_target_pairs={{0,4},{4,0},{8,12},{12,8},{16,20},{20,16},{24,28},{28,24},{1,5},{5... | collective-permute-start | bytes 786440 | tf_op jit(solution)/shard_map/ppermute | solution.py:575
  14.1 1.0 %copy-start.2 = (bf16[2,4,256,256]{3,2,1,0:T(8,128)(2,1)}, bf16[2,4,256,256]{3,2,1,0:T(8,128)(2,1)S(1)}, u32[]{:S(2)}) copy-start(bf16[2,4,256,256]{3,2,1,0:T(8,128)(2,1)S(1)} %get-tuple-element.66.refs_4_) | copy-start | bytes 3145732
  15.3 4.7 %collective-permute-start.1 = (bf16[2,128,128]{2,1,0:T(8,128)(2,1)S(1)}, bf16[2,128,128]{2,1,0:T(8,128)(2,1)S(1)}, u32[]{:S(2)}, u32[]{:S(2)}) collective-permute-start(bf16[2,128,128]{2,1,0:T(8,128)(2,1)S(1)} %get-tuple-element.73), channel_id=1, source_target_pairs={{0,8},{4,12},{1,9},{5,13},{2,10},{6,14},{3,11},{7,15}} | collective-permute-start | bytes 196616 | tf_op jit(solution)/shard_map/ppermute | solution.py:595
  16.0 5.0 %collective-permute-start.4 = (bf16[2,128,128]{2,1,0:T(8,128)(2,1)S(1)}, bf16[2,128,128]{2,1,0:T(8,128)(2,1)S(1)}, u32[]{:S(2)}, u32[]{:S(2)}) collective-permute-start(bf16[2,128,128]{2,1,0:T(8,128)(2,1)S(1)} %get-tuple-element.79), channel_id=1, source_target_pairs={{0,8},{4,12},{1,9},{5,13},{2,10},{6,14},{3,11},{7,15}} | collective-permute-start | bytes 196616 | tf_op jit(solution)/shard_map/ppermute | solution.py:595
  16.6 1.2 %copy-start.3 = (bf16[2,4,256,256]{3,2,1,0:T(8,128)(2,1)S(1)}, bf16[2,4,256,256]{3,2,1,0:T(8,128)(2,1)}, u32[]{:S(2)}) copy-start(bf16[2,4,256,256]{3,2,1,0:T(8,128)(2,1)} %copy-done.2) | copy-start | bytes 3145732
  19.2 0.8 %copy-start = (bf16[512,512]{1,0:T(8,128)(2,1)}, bf16[512,512]{1,0:T(8,128)(2,1)S(1)}, u32[]{:S(2)}) copy-start(bf16[512,512]{1,0:T(8,128)(2,1)S(1)} %get-tuple-element.71.refs_1_.out.own_out) | copy-start | bytes 1572868
  20.0 14.0 %copy-start.1 = (bf16[512,512]{1,0:T(8,128)(2,1)S(1)}, bf16[512,512]{1,0:T(8,128)(2,1)}, u32[]{:S(2)}) copy-start(bf16[512,512]{1,0:T(8,128)(2,1)} %copy-done) | copy-start | bytes 1572868
  20.1 1.7 %collective-permute-start.2 = (bf16[2,128,128]{2,1,0:T(8,128)(2,1)S(1)}, bf16[2,128,128]{2,1,0:T(8,128)(2,1)S(1)}, u32[]{:S(2)}, u32[]{:S(2)}) collective-permute-start(bf16[2,128,128]{2,1,0:T(8,128)(2,1)S(1)} %get-tuple-element.75), channel_id=1, source_target_pairs={{8,16},{12,20},{9,17},{13,21},{10,18},{14,22},{11,19},{15,23}} | collective-permute-start | bytes 196616 | tf_op jit(solution)/shard_map/ppermute | solution.py:595
  21.1 2.1 %collective-permute-start.5 = (bf16[2,128,128]{2,1,0:T(8,128)(2,1)S(1)}, bf16[2,128,128]{2,1,0:T(8,128)(2,1)S(1)}, u32[]{:S(2)}, u32[]{:S(2)}) collective-permute-start(bf16[2,128,128]{2,1,0:T(8,128)(2,1)S(1)} %get-tuple-element.81), channel_id=1, source_target_pairs={{8,16},{12,20},{9,17},{13,21},{10,18},{14,22},{11,19},{15,23}} | collective-permute-start | bytes 196616 | tf_op jit(solution)/shard_map/ppermute | solution.py:595
  22.0 9.4 %collective-permute-start.3 = (bf16[2,128,128]{2,1,0:T(8,128)(2,1)S(1)}, bf16[2,128,128]{2,1,0:T(8,128)(2,1)S(1)}, u32[]{:S(2)}, u32[]{:S(2)}) collective-permute-start(bf16[2,128,128]{2,1,0:T(8,128)(2,1)S(1)} %get-tuple-element.77), channel_id=1, source_target_pairs={{16,24},{20,28},{17,25},{21,29},{18,26},{22,30},{19,27},{23,31}} | collective-permute-start | bytes 196616 | tf_op jit(solution)/shard_map/ppermute | solution.py:595
  23.4 9.3 %collective-permute-start.6 = (bf16[2,128,128]{2,1,0:T(8,128)(2,1)S(1)}, bf16[2,128,128]{2,1,0:T(8,128)(2,1)S(1)}, u32[]{:S(2)}, u32[]{:S(2)}) collective-permute-start(bf16[2,128,128]{2,1,0:T(8,128)(2,1)S(1)} %get-tuple-element.83), channel_id=1, source_target_pairs={{16,24},{20,28},{17,25},{21,29},{18,26},{22,30},{19,27},{23,31}} | collective-permute-start | bytes 196616 | tf_op jit(solution)/shard_map/ppermute | solution.py:595
  31.6 5.4 %collective-permute-start.7 = (bf16[2,128,128]{2,1,0:T(8,128)(2,1)S(1)}, bf16[2,128,128]{2,1,0:T(8,128)(2,1)S(1)}, u32[]{:S(2)}, u32[]{:S(2)}) collective-permute-start(bf16[2,128,128]{2,1,0:T(8,128)(2,1)S(1)} %get-tuple-element.91), channel_id=1, source_target_pairs={{0,4},{4,0},{8,12},{12,8},{16,20},{20,16},{24,28},{28,24},{1,5},{5... | collective-permute-start | bytes 196616 | tf_op jit(solution)/shard_map/ppermute | solution.py:602
  32.9 4.3 %collective-permute-start.8 = (bf16[2,128,128]{2,1,0:T(8,128)(2,1)S(1)}, bf16[2,128,128]{2,1,0:T(8,128)(2,1)S(1)}, u32[]{:S(2)}, u32[]{:S(2)}) collective-permute-start(bf16[2,128,128]{2,1,0:T(8,128)(2,1)S(1)} %get-tuple-element.92), channel_id=1, source_target_pairs={{0,4},{4,0},{8,12},{12,8},{16,20},{20,16},{24,28},{28,24},{1,5},{5... | collective-permute-start | bytes 196616 | tf_op jit(solution)/shard_map/ppermute | solution.py:602
  38.9 2.0 %collective-permute-start.9 = (bf16[128,2048]{1,0:T(8,128)(2,1)S(1)}, bf16[128,2048]{1,0:T(8,128)(2,1)S(1)}, u32[]{:S(2)}, u32[]{:S(2)}) collective-permute-start(bf16[128,2048]{1,0:T(8,128)(2,1)S(1)} %get-tuple-element.94), channel_id=1, source_target_pairs={{0,1},{1,0},{2,3},{3,2},{4,5},{5,4},{6,7},{7,6},{8,9},{9,8},{10,11... | collective-permute-start | bytes 1572872 | tf_op jit(solution)/shard_map/ppermute | solution.py:613
  41.0 14.0 %collective-permute-start.12 = (bf16[128,2048]{1,0:T(8,128)(2,1)S(1)}, bf16[128,2048]{1,0:T(8,128)(2,1)S(1)}, u32[]{:S(2)}, u32[]{:S(2)}) collective-permute-start(bf16[128,2048]{1,0:T(8,128)(2,1)S(1)} %add_convert_fusion.1), channel_id=1, source_target_pairs={{0,2},{1,3},{2,0},{3,1},{4,6},{5,7},{6,4},{7,5},{8,10},{9,11},{10,... | collective-permute-start | bytes 1572872 | tf_op jit(solution)/shard_map/ppermute | solution.py:615
  45.9 1.6 %collective-permute-start.10 = (bf16[128,1024]{1,0:T(8,128)(2,1)S(1)}, bf16[128,1024]{1,0:T(8,128)(2,1)S(1)}, u32[]{:S(2)}, u32[]{:S(2)}) collective-permute-start(bf16[128,1024]{1,0:T(8,128)(2,1)S(1)} %get-tuple-element.97), channel_id=1, source_target_pairs={{0,1},{1,0},{2,3},{3,2},{4,5},{5,4},{6,7},{7,6},{8,9},{9,8},{10,11... | collective-permute-start | bytes 786440 | tf_op jit(solution)/shard_map/ppermute | solution.py:622
  45.9 1.9 %collective-permute-start.11 = (bf16[128,1024]{1,0:T(8,128)(2,1)S(1)}, bf16[128,1024]{1,0:T(8,128)(2,1)S(1)}, u32[]{:S(2)}, u32[]{:S(2)}) collective-permute-start(bf16[128,1024]{1,0:T(8,128)(2,1)S(1)} %get-tuple-element.98), channel_id=1, source_target_pairs={{0,1},{1,0},{2,3},{3,2},{4,5},{5,4},{6,7},{7,6},{8,9},{9,8},{10,11... | collective-permute-start | bytes 786440 | tf_op jit(solution)/shard_map/ppermute | solution.py:622

commit v4 on v0

v4 whole, which is shorter than its diff:
```python
import jax
import jax.numpy as jnp
from jax import lax
from jax.experimental import pallas as pl
from jax.experimental.pallas import tpu as pltpu
from jax.sharding import PartitionSpec as P

DK = 128
DV = 128
CHUNK = 256
F32 = jnp.float32
BF16 = jnp.bfloat16
NEG = -1e30
SMALL_VMEM = 8 * 1024 * 1024
DELTA_VMEM = 28 * 1024 * 1024
OUTPUT_VMEM = 20 * 1024 * 1024
PROJECT_VMEM = 24 * 1024 * 1024


def mm(left, right):
    return lax.dot_general(left, right, (((1,), (0,)), ((), ())), preferred_element_type=F32)


def mm_nt(left, right):
    return lax.dot_general(left, right, (((1,), (1,)), ((), ())), preferred_element_type=F32)


def iota(shape, dim):
    return lax.broadcasted_iota(jnp.int32, shape, dim)


def split3(x):
    hi = x.astype(BF16).astype(F32)
    mid = (x - hi).astype(BF16).astype(F32)
    return hi, mid, x - hi - mid


def softplus(x):
    small = jnp.exp(-jnp.abs(x))
    one = 1.0 + small
    log1p = jnp.where(one == 1.0, small, jnp.log(one) * (small / jnp.where(one == 1.0, 1.0, one - 1.0)))
    return jnp.maximum(x, 0.0) + log1p


def log_inverse_norm(x, rows):
    square = x.astype(F32) * x.astype(F32)
    high = square.astype(BF16)
    low = (square - high.astype(F32)).astype(BF16)
    ones = jnp.ones((rows, x.shape[1]), BF16)
    return -0.5 * jnp.log(mm_nt(ones, high) + mm_nt(ones, low) + 1e-6)


def odd_rows(x, n):
    return jnp.concatenate([x[i + n : i + 2 * n] for i in range(0, x.shape[0], 2 * n)], axis=0)


def weave(even, odd, n):
    parts = []
    for at in range(0, odd.shape[0], n):
        parts.append(even[2 * at : 2 * at + n])
        parts.append(odd[at : at + n])
    return jnp.concatenate(parts, axis=0)


def as_mask(where):
    return jnp.where(where, 1.0, 0.0).astype(BF16)


def unit_lower_inverses(lowers):
    size = lowers[0].shape[0]
    half = size // 2
    row, col = iota((size, size), 0), iota((size, size), 1)
    crow, ccol = iota((half, size), 0), iota((half, size), 1)
    zeros = jnp.zeros((size, size), BF16)
    eye, pair = as_mask(row == col), as_mask(row // 2 == col // 2)
    xs = [eye - lower * pair for lower in lowers]
    n = 2
    while n < size:
        if n < 16:
            mask = as_mask((row // n == col // n + 1) & (row // (2 * n) == col // (2 * n)))
            ys = [mm(lower * mask, x).astype(BF16) for lower, x in zip(lowers, xs)]
            zs = [mm(x, y).astype(BF16) for x, y in zip(xs, ys)]
            xs = [x - z for x, z in zip(xs, zs)]
        elif n < half:
            mask = as_mask(ccol // n == 2 * (crow // n))
            ys = [mm(odd_rows(lower, n) * mask, x).astype(BF16) for lower, x in zip(lowers, xs)]
            odds = [odd_rows(x, n) for x in xs]
            zs = [mm(odd, weave(zeros, y, n)).astype(BF16) for odd, y in zip(odds, ys)]
            xs = [weave(x, odd - z, n) for x, odd, z in zip(xs, odds, zs)]
        else:
            ys = [mm(lower[half:, :half], x[:half, :half]).astype(BF16) for lower, x in zip(lowers, xs)]
            zs = [mm(x[half:, half:], y).astype(BF16) for x, y in zip(xs, ys)]
            xs = [
                jnp.concatenate([x[:half], jnp.concatenate([-z, x[half:, half:]], axis=1)], axis=0)
                for x, z in zip(xs, zs)
            ]
        n *= 2
    return xs


def decayed(c, b, product, mask):
    h = CHUNK // 2

    def quarter(i, j):
        arg = c[i * h : (i + 1) * h] - b[:, j * h : (j + 1) * h]
        if i == j:
            arg = jnp.where(mask, arg, NEG)
        return (jnp.exp(arg) * product[i * h : (i + 1) * h, j * h : (j + 1) * h]).astype(BF16)

    top = jnp.concatenate([quarter(0, 0), jnp.zeros((h, h), BF16)], axis=1)
    return jnp.concatenate([top, jnp.concatenate([quarter(1, 0), quarter(1, 1)], axis=1)], axis=0)


def reordered(x, quarters, first):
    row = iota(x.shape, 0)
    total = jnp.zeros_like(x)
    for j, quarter in enumerate(quarters, first):
        for r in range(2):
            picked = jnp.sum(jnp.where(row == 2 * quarter + r, x, 0.0), axis=0, keepdims=True)
            total = jnp.where(row == 2 * j + r, picked, total)
    return total


def log_norms(refs, heads, first=0):
    tokens = refs[0].shape[0]
    head_row = iota((heads, tokens), 0)
    total = log_inverse_norm(refs[0][...], heads)
    for j, ref in enumerate(refs[1:], first + 1):
        total = jnp.where(head_row < 2 * j, total, log_inverse_norm(ref[...], heads))
    return total


def delta_kernel(rate, gate, beta, quarters, first, k_refs, v_refs, ends_refs, resid_ref, held_ref, cumul_ref, log_ref):
    tokens = k_refs[0].shape[0]
    heads = gate.shape[0]
    chunks = [slice(at, at + CHUNK) for at in range(0, tokens, CHUNK)]

    diagonal = iota((heads, heads), 0) == iota((heads, heads), 1)
    rate = jnp.sum(jnp.where(diagonal, rate, 0.0), axis=1, keepdims=True)
    decay = reordered(-rate * softplus(gate), quarters, first)
    log_beta = reordered(-softplus(-beta), quarters, first)
    log_k = log_norms(k_refs, heads, first)

    row, col = iota((CHUNK, CHUNK), 0), iota((CHUNK, CHUNK), 1)
    upto = jnp.where(row <= col, 1.0, 0.0).astype(BF16)
    sums = mm(
        jnp.concatenate([p for here in chunks for p in split3(decay[:, here])], axis=0).astype(BF16), upto
    )
    square = CHUNK // 2
    strict = iota((square, square), 1) < iota((square, square), 0)

    lowers, rights, ended, decays = {}, {}, {}, {}
    for c, here in enumerate(chunks):
        parts = [sums[(3 * c + i) * heads : (3 * c + i + 1) * heads] for i in range(3)]
        cumul = parts[0] + parts[1] + parts[2]
        end = cumul[:, CHUNK - 1 :]
        lb, lk = log_beta[:, here], log_k[:, here]
        col_log = cumul - lk
        row_lower = cumul + lb + lk
        cumul_ref[:, here] = cumul
        log_ref[:, here] = col_log
        key_end = jnp.exp(end - cumul + lk)
        ends = jnp.exp(end)
        columns = jnp.concatenate([row_lower, jnp.exp(lb), jnp.exp(row_lower)], axis=0).T
        for j, (k_ref, v_ref) in enumerate(zip(k_refs, v_refs)):
            k = k_ref[here, :]
            k32 = k.astype(F32)
            turned = k32.T
            key_key = mm(k, turned.astype(BF16))
            for r in range(2):
                at = 2 * (first + j) + r
                c_lower, c_beta, c_weight = (
                    columns[:, heads * i + at : heads * i + at + 1] for i in range(3)
                )
                m = (c, 2 * j + r)
                lowers[m] = decayed(c_lower, col_log[at : at + 1], key_key, strict)
                v32 = v_ref[here, r * DV : (r + 1) * DV].astype(F32)
                rights[m] = jnp.concatenate([c_beta * v32, c_weight * k32], axis=1).astype(BF16)
                ended[m] = (turned * key_end[at : at + 1]).astype(BF16)
                decays[m] = ends[at : at + 1]
    names = list(lowers)
    inverses = dict(zip(names, unit_lower_inverses([lowers[m] for m in names])))
    solved = {m: mm(inverses[m], rights[m]) for m in names}
    all_heads = range(2 * len(k_refs))
    state = {}
    for c, here in enumerate(chunks):
        if c == 0:
            resid = {a: jnp.concatenate([solved[c, a][:, :DV], -solved[c, a][:, DV:]], axis=1) for a in all_heads}
            before = iota((DK, DV + DK), 1) == iota((DK, DV + DK), 0) + DV
            before = {a: jnp.where(before, 1.0, 0.0) for a in all_heads}
            for a in all_heads:
                held_ref[a // 2, c, a % 2] = before[a].astype(BF16)
        else:
            held = {a: state[a].astype(BF16) for a in all_heads}
            for a in all_heads:
                held_ref[a // 2, c, a % 2] = held[a]
            moved = {a: mm(solved[c, a][:, DV:].astype(BF16), held[a]) for a in all_heads}
            resid = {
                a: jnp.concatenate([solved[c, a][:, :DV] - moved[a][:, :DV], -moved[a][:, DV:]], axis=1)
                for a in all_heads
            }
            before = state
        resid = {a: resid[a].astype(BF16) for a in all_heads}
        for a in all_heads:
            resid_ref[a // 2, c, a % 2] = resid[a]
        state = {a: decays[c, a] * before[a] + mm(ended[c, a], resid[a]) for a in all_heads}
    for a in all_heads:
        ends_refs[a // 2][a % 2] = state[a].astype(BF16)


def local_outputs(q_refs, k_refs, cumul, logs, waits, resid, held, out_ref, gain_ref):
    tokens = q_refs[0].shape[0]
    heads = cumul.shape[0]
    square = CHUNK // 2
    inclusive = iota((square, square), 1) <= iota((square, square), 0)
    row_mix = cumul + log_norms(q_refs, heads)
    mixings, queries = {}, {}
    for c in range(tokens // CHUNK):
        here = slice(c * CHUNK, (c + 1) * CHUNK)
        mix = row_mix[:, here]
        columns = jnp.concatenate([mix, jnp.exp(mix)], axis=0).T
        for j, (q_ref, k_ref) in enumerate(zip(q_refs, k_refs)):
            q, k = q_ref[here, :], k_ref[here, :]
            query_key = mm_nt(q, k)
            q32 = q.astype(F32)
            for a in (2 * j, 2 * j + 1):
                b_row = logs[a : a + 1, here]
                mixings[c, a] = decayed(columns[:, a : a + 1], b_row, query_key, inclusive)
                queries[c, a] = (columns[:, heads + a : heads + a + 1] * q32).astype(BF16)
    waited(waits)
    for c, a in mixings:
        here = slice(c * CHUNK, (c + 1) * CHUNK)
        result = mm(queries[c, a], held(c, a)) + mm(mixings[c, a], resid(c, a))
        out_ref[here, a * DV : (a + 1) * DV] = result[:, :DV].astype(BF16)
        gain_ref[here, a * DK : (a + 1) * DK] = result[:, DV:].astype(BF16)


def lanes(source, which, target):
    width = target.shape[1]
    return source.at[:, pl.ds(pl.multiple_of(which * width, 128), width)], target


def started(moves, sems, first=0):
    copies = [pltpu.make_async_copy(a, b, sems.at[first + i]) for i, (a, b) in enumerate(moves)]
    for copy in copies:
        copy.start()
    return copies


def waited(copies):
    for copy in copies:
        copy.wait()


def in_vmem(array):
    return pltpu.with_memory_space_constraint(array, pltpu.VMEM)


def in_hbm(array):
    return pltpu.with_memory_space_constraint(array, pltpu.HBM)


def call(kernel, name, groups, outs, scratch, vmem_bytes, flops):
    specs, args = [], []
    for space, arrays in groups:
        specs += [pl.BlockSpec(memory_space=space)] * len(arrays)
        if space is pltpu.VMEM or space is pltpu.HBM:
            arrays = [pltpu.with_memory_space_constraint(a, space) for a in arrays]
        args += arrays
    return pl.pallas_call(
        kernel,
        in_specs=specs,
        out_specs=[pl.BlockSpec(memory_space=space) for space, _, _ in outs],
        out_shape=[space(shape, kind) for space, shape, kind in outs],
        scratch_shapes=scratch,
        compiler_params=pltpu.CompilerParams(vmem_limit_bytes=vmem_bytes),
        cost_estimate=pl.CostEstimate(flops=flops, bytes_accessed=2**20, transcendentals=0),
        name=name,
    )(*args)


def local_shapes(count, tokens, heads):
    chunks = tokens // CHUNK
    return [
        ((count, chunks, 2, CHUNK, DV + DK), BF16),
        ((count, chunks, 2, DK, DV + DK), BF16),
        ((heads, tokens), F32),
        ((heads, tokens), F32),
    ]


def first_part(member, turns, rate, keys, values, gate_logit, beta_logit):
    heads, tokens = gate_logit.shape
    count = len(turns)
    key_part, value_part = (tokens, DK), (tokens, 2 * DV)

    def kernel(member_ref, rate_hbm, k_hbm, v_hbm, gate_hbm, beta_hbm, *refs):
        ends, (resid, held, cumul, logs, rate, gate, beta, k_own, v_own), refs = (
            refs[:count], refs[count : count + 9], refs[count + 9 :]
        )
        k_refs, v_refs, sems = refs[:count], refs[count : 2 * count], refs[-1]
        quarters = [jnp.bitwise_xor(member_ref[0], turn) for turn in turns]
        moves = [(rate_hbm, rate), (gate_hbm, gate), (beta_hbm, beta)]
        moves += [lanes(k_hbm, q, ref) for q, ref in zip(quarters, k_refs)]
        moves += [lanes(v_hbm, q, ref) for q, ref in zip(quarters, v_refs)]
        moves += [lanes(k_hbm, member_ref[0], k_own), lanes(v_hbm, member_ref[0], v_own)]
        copies = started(moves, sems)
        waited(copies[:-2])
        delta_kernel(
            rate[...], gate[...], beta[...], quarters, 0, k_refs, v_refs, ends, resid, held, cumul, logs
        )
        waited(copies[-2:])

    vmem = pltpu.VMEM
    outs = [(vmem, (2, DK, DV + DK), BF16)] * count
    outs += [(vmem, *shape) for shape in local_shapes(count, tokens, heads)]
    outs += [(vmem, (1, heads), F32), (vmem, (heads, tokens), F32), (vmem, (heads, tokens), F32)]
    outs += [(vmem, key_part, BF16), (vmem, value_part, BF16)]
    outs = [(pltpu.MemorySpace.VMEM, *rest) for _, *rest in outs]
    scratch = [vmem(key_part, BF16)] * count + [vmem(value_part, BF16)] * count
    scratch += [pltpu.SemaphoreType.DMA((5 + 2 * count,))]
    groups = [(pltpu.SMEM, [member]), (pltpu.HBM, [rate, keys, values, gate_logit, beta_logit])]
    result = call(kernel, "first_part", groups, outs, scratch, DELTA_VMEM, 6 * 10**9)
    return result[:count], result[count : count + 4], result[count + 4 :]


def second_part(member, operands, earlier):
    heads, tokens = operands[1].shape

    def kernel(member_ref, rate, gate, beta, k_own, v_own, *refs):
        earlier_refs, (ends,), out_hbm, local, sems = refs[:4], refs[4:5], refs[5:13], refs[13:17], refs[17]
        copies = started(zip(earlier_refs, out_hbm[:4]), sems)
        delta_kernel(
            rate[...], gate[...], beta[...], [member_ref[0]], heads // 2 - 1, [k_own], [v_own], [ends], *local
        )
        copies += started(zip(local, out_hbm[4:]), sems, 4)
        waited(copies)

    shapes = local_shapes(1, tokens, heads)
    outs = [(pltpu.MemorySpace.VMEM, (2, DK, DV + DK), BF16)]
    outs += [(pltpu.MemorySpace.HBM, a.shape, a.dtype) for a in earlier]
    outs += [(pltpu.MemorySpace.HBM, *shape) for shape in shapes]
    scratch = [pltpu.VMEM(*shape) for shape in shapes] + [pltpu.SemaphoreType.DMA((8,))]
    groups = [(pltpu.SMEM, [member]), (pltpu.VMEM, [*operands, *earlier])]
    ends, *rest = call(kernel, "second_part", groups, outs, scratch, DELTA_VMEM, 2 * 10**9)
    return ends, rest[:4], rest[4:]


def third_part(place, turns, chunks, query, keys, earlier, own, after):
    count = len(turns) + 1
    tokens = chunks * CHUNK
    heads = 2 * count

    def kernel(place_ref, q_hbm, k_hbm, *refs):
        sources, (_, out, gain), refs = refs[:8], refs[8:11], refs[11:]
        q_refs, k_refs, local, sems = refs[:count], refs[count : 2 * count], refs[2 * count : -1], refs[-1]
        first = place_ref[0] * chunks
        rows = pl.ds(pl.multiple_of(first * CHUNK, CHUNK), tokens)
        quarters = [jnp.bitwise_xor(place_ref[2], turn) for turn in (*turns, 0)]
        moves = []
        for hbm, targets in ((q_hbm, q_refs), (k_hbm, k_refs)):
            for quarter, ref in zip(quarters, targets):
                moves.append((hbm.at[rows, pl.ds(pl.multiple_of(quarter * DK, DK), DK)], ref))
        for i in (2, 3, 6, 7):
            moves.append((sources[i].at[:, rows], local[i]))
        for i in (0, 1, 4, 5):
            moves.append((sources[i].at[:, pl.ds(first, chunks)], local[i]))
        copies = started(moves, sems)
        waited(copies[:-4])
        theirs = iota((heads, tokens), 0) < heads - 2
        cumul = jnp.where(theirs, local[2][...], local[6][...])
        logs = jnp.where(theirs, local[3][...], local[7][...])

        def read(which):
            return lambda c, a: local[which][a // 2, c, a % 2] if a < heads - 2 else local[which + 4][0, c, a % 2]

        local_outputs(q_refs, k_refs, cumul, logs, copies[-4:], read(0), read(1), out, gain)

    outs = [(pltpu.MemorySpace.VMEM, (tokens, heads * DV), BF16)] * 2
    scratch = [pltpu.VMEM((tokens, DK), BF16)] * (2 * count)
    for pairs in (count - 1, 1):
        scratch += [pltpu.VMEM(*shape) for shape in local_shapes(pairs, tokens, heads)]
    scratch += [pltpu.SemaphoreType.DMA((2 * count + 8,))]
    groups = [(pltpu.SMEM, [place]), (pltpu.HBM, [query, keys, *earlier, *own, after])]
    return call(kernel, "third_part", groups, outs, scratch, OUTPUT_VMEM, 3 * 10**9)


def in_order(member_ref, turns, own_ref, other_refs, order_ref):
    order_ref[member_ref[0]] = own_ref[...]
    for turn, ref in zip(turns, other_refs):
        order_ref[jnp.bitwise_xor(member_ref[0], turn)] = ref[...]


def after_shard(ends, state):
    return mm(ends[:, DV:], state.astype(BF16)) + ends[:, :DV].astype(F32)


def group_part(member, turns, own, others, chained):
    count = len(turns) + 1

    def kernel(member_ref, own_ref, *refs):
        other_refs, (order, ending_ref, *total_refs) = refs[: count - 1], refs[count - 1 :]
        in_order(member_ref, turns, own_ref, other_refs, order)
        states = [order[0, h][:, :DV].astype(F32) for h in range(2)]
        for i in range(1, count):
            states = [after_shard(order[i, h], states[h]) for h in range(2)]
        for h in range(2):
            ending_ref[h] = states[h].astype(BF16)
        for total_ref in total_refs:
            for h in range(2):
                transit = order[0, h][:, DV:]
                for i in range(1, count):
                    transit = mm(order[i, h][:, DV:], transit).astype(BF16)
                total_ref[h] = jnp.concatenate([states[h].astype(BF16), transit], axis=1)

    vmem = pltpu.MemorySpace.VMEM
    outs = [(vmem, (count, *own.shape), BF16), (vmem, (2, DK, DV), BF16)]
    if chained:
        outs.append((vmem, own.shape, BF16))
    groups = [(pltpu.SMEM, [member]), (pltpu.VMEM, [own, *others])]
    return call(kernel, "group_part", groups, outs, [], SMALL_VMEM, 10**8)


def hop_part(total, came):
    def kernel(total_ref, *refs):
        sum_ref, out_ref = refs[-2:]
        for h in range(2):
            start = refs[0][h]
            for ref in refs[1:-2]:
                start = start + ref[h]
            sum_ref[h] = start
            out_ref[h] = after_shard(total_ref[h], start).astype(BF16)

    outs = [(pltpu.MemorySpace.VMEM, (2, DK, DV), BF16)] * 2
    return call(kernel, "hop_part", [(pltpu.VMEM, [total, *came])], outs, [], SMALL_VMEM, 10**7)


def starts_part(member, turns, order, came, after):
    count = len(turns) + 1

    def kernel(member_ref, order_ref, *refs):
        came_refs, outs, states_ref = refs[: len(came)], refs[len(came) + 1 : -1], refs[-1]
        states = [came_refs[0][h] for h in range(2)]
        for ref in came_refs[1:]:
            states = [states[h] + ref[h] for h in range(2)]
        for i in range(count):
            for h in range(2):
                states_ref[i, h] = states[h].astype(BF16)
            if i < count - 1:
                states = [after_shard(order_ref[i, h], states[h]) for h in range(2)]
        for turn, ref in zip((0, *turns), outs):
            ref[...] = states_ref[jnp.bitwise_xor(member_ref[0], turn)]

    state = (2, DK, DV)
    outs = [(pltpu.MemorySpace.VMEM, state, BF16)] * count
    groups = [(pltpu.SMEM, [member]), (pltpu.VMEM, [order, *came]), (pltpu.VMEM, [after])]
    return call(kernel, "starts_part", groups, outs, [pltpu.VMEM((count, *state), BF16)], SMALL_VMEM, 10**8)


def gated_rows(out, gain, z, at, first, start_refs, norm):
    parts = []
    for h in range(2 * len(start_refs)):
        cols = slice(h * DV, (h + 1) * DV)
        local = slice((2 * first + h) * DV, (2 * first + h + 1) * DV)
        core = out[at, local].astype(F32) + mm(gain[at, local], start_refs[h // 2][h % 2])
        mean = jnp.mean(core * core, axis=1, keepdims=True)
        z_here = z[:, cols].astype(F32)
        gate = z_here / (1.0 + jnp.exp(-z_here))
        parts.append((core * lax.rsqrt(mean + 1e-6) * norm * gate).astype(BF16))
    return jnp.concatenate(parts, axis=1)


def pair_moves(place_ref, turns, z_hbm, w_hbm, z, w):
    rows, width = z.shape[0], 2 * DV
    here = pl.ds(pl.multiple_of(place_ref[0] * rows, rows), rows)
    gates, bands = [], []
    for j, turn in enumerate(turns):
        at = pl.ds(pl.multiple_of(jnp.bitwise_xor(place_ref[2], turn) * width, width), width)
        part = slice(j * width, (j + 1) * width)
        gates.append((z_hbm.at[here, at], z.at[:, part]))
        bands.append((w_hbm.at[at, :], w.at[part, :]))
    return gates + bands


def pair_buffers(count, rows, wide):
    width = 2 * count * DV
    return [((rows, width), BF16), ((width, wide), BF16)]


def local_rows(place_ref, rows, out):
    return slice(None) if out.shape[0] == rows else pl.ds(pl.multiple_of(place_ref[0] * rows, rows), rows)


def keep_part(place, turns, rows, gate_z, weight, norm_gain, out, gain, start):
    wide = weight.shape[1]
    count = len(turns)

    def kernel(place_ref, z_hbm, w_hbm, norm_hbm, out, gain, start_ref, sum_ref, norm, *refs):
        away, own, sems = refs[:2], refs[2:4], refs[4]
        moves = [(norm_hbm, norm)] + pair_moves(place_ref, [0], z_hbm, w_hbm, *own)
        copies = started(moves + pair_moves(place_ref, turns, z_hbm, w_hbm, *away), sems)
        waited(copies[:2])
        gated = gated_rows(out, gain, own[0], local_rows(place_ref, rows, out), count, [start_ref], norm[...])
        waited(copies[2:3])
        sum_ref[...] = mm(gated, own[1][...])
        waited(copies[3:])

    vmem = pltpu.MemorySpace.VMEM
    outs = [(vmem, (rows, wide), F32), (vmem, (1, DV), F32)]
    outs += [(vmem, *shape) for shape in pair_buffers(count, rows, wide)]
    scratch = [pltpu.VMEM(*shape) for shape in pair_buffers(1, rows, wide)]
    scratch += [pltpu.SemaphoreType.DMA((3 + 2 * count,))]
    groups = [(pltpu.SMEM, [place]), (pltpu.HBM, [gate_z, weight, norm_gain]), (pltpu.VMEM, [out, gain, start])]
    return call(kernel, "keep_part", groups, outs, scratch, PROJECT_VMEM, 4 * rows * DV * wide)


def send_rows(partial, core, send_refs, stay_ref):
    rows, width = send_refs[0].shape
    one, two = partial[:rows], partial[rows:]
    send = jnp.where(core == 0, two, one).astype(BF16)
    for i, ref in enumerate(send_refs):
        ref[...] = send[:, i * width : (i + 1) * width]
    stay_ref[...] = jnp.where(core == 0, one, two)


def away_part(place, kept, out, gain, starts):
    rows, wide = kept[0].shape

    def kernel(place_ref, sum_ref, norm, z, w, out, gain, *refs):
        start_refs, (send_ref, stay_ref) = refs[:-2], refs[-2:]
        gated = gated_rows(out, gain, z, local_rows(place_ref, rows, out), 0, start_refs, norm[...])
        send_rows(mm(gated, w[...]) + sum_ref[...], place_ref[1], [send_ref], stay_ref)

    vmem = pltpu.MemorySpace.VMEM
    outs = [(vmem, (rows // 2, wide), BF16), (vmem, (rows // 2, wide), F32)]
    groups = [(pltpu.SMEM, [place]), (pltpu.VMEM, [*kept, out, gain, *starts])]
    return call(kernel, "away_part", groups, outs, [], PROJECT_VMEM, 2 * rows * kept[-1].size)


def whole_part(place, turns, rows, gate_z, weight, norm_gain, out, gain, starts):
    wide = weight.shape[1]
    count = len(turns) + 1

    def kernel(place_ref, z_hbm, w_hbm, norm_hbm, out, gain, *refs):
        start_refs, sends, (stay_ref, norm, z, w, sems) = refs[:count], refs[count : count + 2], refs[count + 2 :]
        moves = [(norm_hbm, norm)] + pair_moves(place_ref, (*turns, 0), z_hbm, w_hbm, z, w)
        copies = started(moves, sems)
        waited(copies[: 1 + count])
        gated = gated_rows(out, gain, z, local_rows(place_ref, rows, out), 0, start_refs, norm[...])
        waited(copies[1 + count :])
        send_rows(mm(gated, w[...]), place_ref[1], sends, stay_ref)

    vmem = pltpu.MemorySpace.VMEM
    outs = [(vmem, (rows // 2, wide // 2), BF16)] * 2 + [(vmem, (rows // 2, wide), F32)]
    scratch = [pltpu.VMEM((1, DV), F32)] + [pltpu.VMEM(*shape) for shape in pair_buffers(count, rows, wide)]
    scratch += [pltpu.SemaphoreType.DMA((1 + 2 * count,))]
    groups = [(pltpu.SMEM, [place]), (pltpu.HBM, [gate_z, weight, norm_gain]), (pltpu.VMEM, [out, gain, *starts])]
    return call(kernel, "whole_part", groups, outs, scratch, PROJECT_VMEM, 2 * rows * weight.size)


def on_device(
    query, keys, values, gate_logit, beta_logit, decay_rate, norm_gain, gate_z, out_weight
):
    shards, cores = lax.axis_size("seq"), lax.axis_size("head")
    seq, head = lax.axis_index("seq"), lax.axis_index("head")
    members = query.shape[1] // DK
    turns = sorted(range(1, members), key=lambda turn: (-bin(turn).count("1"), turn))
    pairs = {turn: [(s, s ^ turn) for s in range(shards)] for turn in turns}
    member_at = lax.rem(seq, members)
    member = member_at.reshape(1)
    rate, norm_gain = decay_rate.reshape(1, -1), norm_gain.reshape(1, -1)

    away, earlier, operands = first_part(member, turns, rate, keys, values, gate_logit.T, beta_logit.T)
    others = [lax.ppermute(a, "seq", pairs[turn]) for a, turn in zip(away, turns)]
    own, earlier, mine = second_part(member, operands, earlier)
    groups = shards // members
    order, ending, *total = group_part(member, turns, own, others, groups > 2)

    chips = cores // 2
    chip, core = head // 2, lax.rem(head, 2)
    rows = query.shape[0] // chips
    spots = [jnp.stack([lax.rem(chip + by, chips), core, member_at]) for by in range(chips)]
    apart = rows == CHUNK and chips == 2
    chunks = 1 if apart else query.shape[0] // CHUNK
    spot = spots[1] if apart else jnp.zeros_like(spots[0]).at[2].set(member_at)
    out, gain = third_part(spot, turns, chunks, query, keys, earlier, mine, ending)

    came = []
    for step in range(groups - 1):
        if step:
            start, ending = hop_part(*total, came)
            came = [start]
        along = [(step * members + i, (step + 1) * members + i) for i in range(members)]
        came.append(lax.ppermute(ending, "seq", along))
    if not came:
        came = [jnp.zeros_like(ending)]
    keep, *gives = starts_part(member, turns, order, came, out)
    back = [lax.ppermute(g, "seq", pairs[turn]) for g, turn in zip(gives, turns)]

    swap = [(i, i ^ 1) for i in range(cores)]
    arrived = []
    for by in range(1, chips):
        kept = keep_part(spots[by], turns, rows, gate_z, out_weight, norm_gain, out, gain, keep)
        give, stay = away_part(spots[by], kept, out, gain, back)
        both = (stay + lax.ppermute(give, "head", swap).astype(F32)).astype(BF16)
        arrived.append(lax.ppermute(both, "head", [(i, (i + 2 * by) % cores) for i in range(cores)]))
    spot = spots[0]
    if arrived:
        spot, both = lax.optimization_barrier((spot, both))
    if apart:
        out, gain = third_part(spot, turns, chunks, query, keys, earlier, mine, ending)
    *gives, stay = whole_part(spot, turns, rows, gate_z, out_weight, norm_gain, out, gain, [*back, keep])
    total = stay + jnp.concatenate([lax.ppermute(g, "head", swap) for g in gives], axis=1).astype(F32)
    for part in arrived:
        total = total + part.astype(F32)
    return total.astype(BF16)


def solution(mesh):
    return jax.shard_map(
        on_device,
        mesh=mesh,
        in_specs=(
            P("seq", "head"),
            P("seq", "head"),
            P("seq", "head"),
            P("seq", "head"),
            P("seq", "head"),
            P("head"),
            P(),
            P("seq", "head"),
            P("head", None),
        ),
        out_specs=P(("seq", "head"), None),
        check_vma=False,
    )
```

time: 611 us -> 54.6 us (0.09); the launches traced: 601 us -> 54.4 us
  other arithmetic: 330 us -> 1.24 us
  matrix products: 134 us -> 0 us
  waiting for transfers between devices: 60.6 us -> 7.68 us
  Pallas kernels: 0 us -> 30.2 us
  starting transfers between devices: 35 us -> 15.1 us
  blocking collectives: 17 us -> 0 us
  between operations: 14.2 us -> 0.18 us
  local copies, waits for them, and re-layouts: 8.51 us -> 0.01 us
    another operation x5 -> x2, other arithmetic: 318 us -> 0.15 us  [on_device(): jnp.stack([lax.rem(chip + by, chips), core, member_at])]
    dot_general x60 -> x0, matrix products: 126 us -> none  [the longest x23 33.3 us: matmul_heads(): jnp.einsum('hef,hfg->heg', left, right, precision=lax.Precision.HIGHEST)]
    ppermute x7 -> x11, waiting for transfers between devices: 59.9 us -> 7.68 us  [the longest x1 2.58 us: on_device(): lax.ppermute(both, 'head', [(i, (i + 2 * by) % cores) for i in range(core...]
    pallas_call x0 -> x9, Pallas kernels: none -> 30.2 us  [call(): pl.pallas_call(kernel, in_specs=specs, out_specs=[pl.BlockSpec(memory_spa...]
    ppermute x7 -> x11, starting transfers between devices: 34.9 us -> 15.1 us  [the longest x3 4.69 us: on_device(): lax.ppermute(a, 'seq', pairs[turn])]
    all_to_all x1 -> x0, blocking collectives: 17 us -> none  [on_device(): lax.all_to_all(gated, 'head', split_axis=0, concat_axis=1, tiled=True)]
    another operation x2 -> x0, matrix products: 7.69 us -> none  [the longest x1 4.06 us: block_terms(): lax.linalg.triangular_solve(lower, rhs_values, left_side=True, lower=True...]
  transfers between devices with their start and end apart: 8 -> 11, of which waited for: 7 -> 7; matrix products, arithmetic and copies ran while one was open for 77% -> 0% of each run, Pallas kernels for 0% -> 35%
where the time goes in v4:
time: 54.6 us; the launch traced here: 54.4 us
  Pallas kernels  30.2 us (55%)
  starting transfers between devices  15.1 us (28%)
  waiting for transfers between devices  7.68 us (14%)
  other arithmetic  1.24 us (2%)
    pallas_call x9, Pallas kernels, call(): pl.pallas_call(kernel, in_specs=specs, out_specs=[pl.BlockSpec(memory_spa...  30.2 us
    ppermute x3, starting transfers between devices, on_device(): lax.ppermute(a, 'seq', pairs[turn])  4.69 us
    ppermute x1, starting transfers between devices, on_device(): came.append(lax.ppermute(ending, 'seq', along))  4.69 us
    ppermute x3, starting transfers between devices, on_device(): lax.ppermute(g, 'seq', pairs[turn])  3.55 us
    ppermute x1, waiting for transfers between devices, on_device(): lax.ppermute(both, 'head', [(i, (i + 2 * by) % cores) for i in range(core...  2.58 us
    ppermute x1, waiting for transfers between devices, on_device(): both = (stay + lax.ppermute(give, 'head', swap).astype(F32)).astype(BF16)  1.81 us
    ppermute x1, starting transfers between devices, on_device(): lax.ppermute(both, 'head', [(i, (i + 2 * by) % cores) for i in range(core...  1.55 us
    ppermute x2, waiting for transfers between devices, on_device(): lax.ppermute(g, 'head', swap)  1.4 us
  transfers between devices with their start and end apart: 11, of which 7 were waited for; matrix products, arithmetic and copies ran while one was open for 0% of the time, Pallas kernels for 35%

profile of v4, /device:TPU:0, one launch (start us, length us, event | category | flops | bytes accessed | tf_op | source)
XLA Modules:
  0.0 54.4 jit_solution(3648910532637473016)
XLA Ops:
  0.0 8.1 %first_part.1 = (bf16[2,128,256]{2,1,0:T(8,128)(2,1)S(1)}, bf16[2,128,256]{2,1,0:T(8,128)(2,1)S(1)}, bf16[2,128,256]{2,1,0:T(8,128)(2,1)S(1)}, bf16[3,2,2,256,25...) custom-call(s32[1]{0:T(128)} %bitcast.2.member_ref, ...), custom_call_target="tpu_custom_call" | custom-call | flops 6000000000 | bytes 1048576 | tf_op jit(solution)/shard_map/first_part/pallas_call | solution.py:270
  8.1 4.0 %collective-permute-start = (bf16[2,128,256]{2,1,0:T(8,128)(2,1)S(1)}, bf16[2,128,256]{2,1,0:T(8,128)(2,1)S(1)}, u32[]{:S(2)}, u32[]{:S(2)}) collective-permute-start(bf16[2,128,256]{2,1,0:T(8,128)(2,1)S(1)} %get-tuple-element.64), channel_id=1, source_target_pairs={{0,12},{4,8},{8,4},{12,0},{16,28},{20,24},{24,20},{28,16},{1,13},{... | collective-permute-start | bytes 393224 | tf_op jit(solution)/shard_map/ppermute | solution.py:574
  12.1 0.5 collective-permute-start.1
  12.6 0.1 collective-permute-start.2
  12.8 4.6 %second_part.1 = (bf16[2,128,256]{2,1,0:T(8,128)(2,1)S(1)}, bf16[3,2,2,256,256]{4,3,2,1,0:T(8,128)(2,1)}, bf16[3,2,2,128,256]{4,3,2,1,0:T(8,128)(2,1)}, f32[8,51...) custom-call(s32[1]{0:T(128)} %bitcast.2.member_ref, ...), custom_call_target="tpu_custom_call" | custom-call | flops 2000000000 | bytes 1048576 | tf_op jit(solution)/shard_map/second_part/pallas_call | solution.py:270
  17.4 0.1 add_add_fusion.1.place_ref
  17.5 0.0 collective-permute-done.refs_0_
  17.5 0.9 %collective-permute-done.1.refs_1_ = bf16[2,128,256]{2,1,0:T(8,128)(2,1)S(1)} collective-permute-done((bf16[2,128,256]{2,1,0:T(8,128)(2,1)S(1)}, bf16[2,128,256]{2,1,0:T(8,128)(2,1)S(1)}, u32[]{:S(2)}, u32[]{:S(2)}) %collective-permute-start.1) | collective-permute-done | bytes 131104 | tf_op jit(solution)/shard_map/ppermute | solution.py:574
  18.4 0.2 collective-permute-done.2.refs_2_
  18.6 0.5 group_part.1
  19.1 0.0 copy-start
  19.1 4.7 %collective-permute-start.3 = (bf16[2,128,128]{2,1,0:T(8,128)(2,1)S(1)}, bf16[2,128,128]{2,1,0:T(8,128)(2,1)S(1)}, u32[]{:S(2)}, u32[]{:S(2)}) collective-permute-start(bf16[2,128,128]{2,1,0:T(8,128)(2,1)S(1)} %get-tuple-element.67.refs_8_), channel_id=1, source_target_pairs={{0,16},{4,20},{8,24},{12,28},{1,17},{5,21},{9,25},{13,29},{2,18},{... | collective-permute-start | bytes 196616 | tf_op jit(solution)/shard_map/ppermute | solution.py:594
  23.8 0.0 copy-done
  23.8 3.6 %third_part.2 = (bf16[256,1024]{1,0:T(8,128)(2,1)S(1)}, bf16[256,1024]{1,0:T(8,128)(2,1)S(1)}) custom-call(s32[3]{0:T(128)S(1)} %add_add_fusion.1.place_ref, bf16[512,512]{1,0:T(8,128)(2,1)} %q_hbm.3, bf16[512,512]{1,0:T(8,128)(2,1)} %k_hbm.5, bf16[3,2,2,256,256]{4,3,2,1,0:T(8,128)(2,1)} %get-tuple-element.55.refs_0_, ...), custom_call_target="tpu_custom_call" | custom-call | flops 3000000000 | bytes 1048576 | tf_op jit(solution)/shard_map/third_part/pallas_call | solution.py:270
  27.3 0.0 collective-permute-done.3.refs_0_
  27.3 0.5 starts_part.1
  27.8 1.9 %collective-permute-start.4 = (bf16[2,128,128]{2,1,0:T(8,128)(2,1)S(1)}, bf16[2,128,128]{2,1,0:T(8,128)(2,1)S(1)}, u32[]{:S(2)}, u32[]{:S(2)}) collective-permute-start(bf16[2,128,128]{2,1,0:T(8,128)(2,1)S(1)} %get-tuple-element.76), channel_id=1, source_target_pairs={{0,12},{4,8},{8,4},{12,0},{16,28},{20,24},{24,20},{28,16},{1,13},{... | collective-permute-start | bytes 196616 | tf_op jit(solution)/shard_map/ppermute | solution.py:598
  29.7 1.3 %collective-permute-start.5 = (bf16[2,128,128]{2,1,0:T(8,128)(2,1)S(1)}, bf16[2,128,128]{2,1,0:T(8,128)(2,1)S(1)}, u32[]{:S(2)}, u32[]{:S(2)}) collective-permute-start(bf16[2,128,128]{2,1,0:T(8,128)(2,1)S(1)} %get-tuple-element.77), channel_id=1, source_target_pairs={{0,4},{4,0},{8,12},{12,8},{16,20},{20,16},{24,28},{28,24},{1,5},{5... | collective-permute-start | bytes 196616 | tf_op jit(solution)/shard_map/ppermute | solution.py:598
  31.0 0.4 collective-permute-start.6
  31.4 3.0 %keep_part.1 = (f32[256,2048]{1,0:T(8,128)S(1)}, f32[1,128]{1,0:T(1,128)S(1)}, bf16[256,768]{1,0:T(8,128)(2,1)S(1)}, bf16[768,2048]{1,0:T(8,128)(2,1)S(1)}) custom-call(s32[3]{0:T(128)S(1)} %add_add_fusion.1.place_ref, bf16[512,1024]{1,0:T(8,128)(2,1)} %z_hbm.3, bf16[1024,2048]{1,0:T(8,128)(2,1)} %w_hbm.3, f32[1,128]{1,0:T(1,128)} %bitcast.8, ...), custom_call_target="tpu_custom_call" | custom-call | flops 268435456 | bytes 1048576 | tf_op jit(solution)/shard_map/keep_part/pallas_call | solution.py:270
  34.4 0.0 collective-permute-done.4.refs_0_
  34.4 0.0 collective-permute-done.5.refs_1_
  34.4 0.8 %collective-permute-done.6.refs_2_ = bf16[2,128,128]{2,1,0:T(8,128)(2,1)S(1)} collective-permute-done((bf16[2,128,128]{2,1,0:T(8,128)(2,1)S(1)}, bf16[2,128,128]{2,1,0:T(8,128)(2,1)S(1)}, u32[]{:S(2)}, u32[]{:S(2)}) %collective-permute-start.6) | collective-permute-done | bytes 65568 | tf_op jit(solution)/shard_map/ppermute | solution.py:598
  35.2 2.0 %away_part.1 = (bf16[128,2048]{1,0:T(8,128)(2,1)S(1)}, f32[128,2048]{1,0:T(8,128)S(1)}) custom-call(s32[3]{0:T(128)S(1)} %add_add_fusion.1.place_ref, f32[256,2048]{1,0:T(8,128)S(1)} %get-tuple-element.72.sum_ref, f32[1,128]{1,0:T(1,128)S(1)} %get-tuple-element.73.norm, bf16[256,768]{1,0:T(8,128)(2,1)S(1)} %get-tuple-element.74.z, ...), custom_call_target="tpu_custom_call" | custom-call | flops 805306368 | bytes 1048576 | tf_op jit(solution)/shard_map/away_part/pallas_call | solution.py:270
  37.3 0.1 collective-permute-start.7
  37.4 0.1 add_add_fusion.place_ref
  37.4 1.8 %collective-permute-done.7 = bf16[128,2048]{1,0:T(8,128)(2,1)S(1)} collective-permute-done((bf16[128,2048]{1,0:T(8,128)(2,1)S(1)}, bf16[128,2048]{1,0:T(8,128)(2,1)S(1)}, u32[]{:S(2)}, u32[]{:S(2)}) %collective-permute-start.7) | collective-permute-done | bytes 524320 | tf_op jit(solution)/shard_map/ppermute | solution.py:605
  39.3 0.1 add_convert_fusion.1
  39.4 1.6 %collective-permute-start.10 = (bf16[128,2048]{1,0:T(8,128)(2,1)S(1)}, bf16[128,2048]{1,0:T(8,128)(2,1)S(1)}, u32[]{:S(2)}, u32[]{:S(2)}) collective-permute-start(bf16[128,2048]{1,0:T(8,128)(2,1)S(1)} %add_convert_fusion.1), channel_id=1, source_target_pairs={{0,2},{1,3},{2,0},{3,1},{4,6},{5,7},{6,4},{7,5},{8,10},{9,11},{10,... | collective-permute-start | bytes 1572872 | tf_op jit(solution)/shard_map/ppermute | solution.py:606
  40.9 3.6 %third_part.3 = (bf16[256,1024]{1,0:T(8,128)(2,1)S(1)}, bf16[256,1024]{1,0:T(8,128)(2,1)S(1)}) custom-call(s32[3]{0:T(128)S(1)} %add_add_fusion.place_ref, bf16[512,512]{1,0:T(8,128)(2,1)} %q_hbm.3, bf16[512,512]{1,0:T(8,128)(2,1)} %k_hbm.5, bf16[3,2,2,256,256]{4,3,2,1,0:T(8,128)(2,1)} %get-tuple-element.55.refs_0_, ...), custom_call_target="tpu_custom_call" | custom-call | flops 3000000000 | bytes 1048576 | tf_op jit(solution)/shard_map/third_part/pallas_call | solution.py:270
  44.5 4.4 %whole_part.1 = (bf16[128,1024]{1,0:T(8,128)(2,1)S(1)}, bf16[128,1024]{1,0:T(8,128)(2,1)S(1)}, f32[128,2048]{1,0:T(8,128)S(1)}) custom-call(s32[3]{0:T(128)S(1)} %add_add_fusion.place_ref, bf16[512,1024]{1,0:T(8,128)(2,1)} %z_hbm.3, bf16[1024,2048]{1,0:T(8,128)(2,1)} %w_hbm.3, f32[1,128]{1,0:T(1,128)} %bitcast.9, ...), custom_call_target="tpu_custom_call" | custom-call | flops 1073741824 | bytes 1048576 | tf_op jit(solution)/shard_map/whole_part/pallas_call | solution.py:270
  48.8 0.1 collective-permute-start.8
  48.9 0.5 collective-permute-start.9
  49.4 1.0 %collective-permute-done.8 = bf16[128,1024]{1,0:T(8,128)(2,1)S(1)} collective-permute-done((bf16[128,1024]{1,0:T(8,128)(2,1)S(1)}, bf16[128,1024]{1,0:T(8,128)(2,1)S(1)}, u32[]{:S(2)}, u32[]{:S(2)}) %collective-permute-start.8) | collective-permute-done | bytes 262176 | tf_op jit(solution)/shard_map/ppermute | solution.py:613
  50.4 0.4 collective-permute-done.9
  50.8 2.6 %collective-permute-done.10 = bf16[128,2048]{1,0:T(8,128)(2,1)S(1)} collective-permute-done((bf16[128,2048]{1,0:T(8,128)(2,1)S(1)}, bf16[128,2048]{1,0:T(8,128)(2,1)S(1)}, u32[]{:S(2)}, u32[]{:S(2)}) %collective-permute-start.10) | collective-permute-done | bytes 524320 | tf_op jit(solution)/shard_map/ppermute | solution.py:606
  53.4 1.0 %add_convert_fusion = bf16[128,2048]{1,0:T(8,128)(2,1)} fusion(bf16[128,2048]{1,0:T(8,128)(2,1)S(1)} %collective-permute-done.10, f32[128,2048]{1,0:T(8,128)S(1)} %get-tuple-element.84, bf16[128,1024]{1,0:T(8,128)(2,1)S(1)} %collective-permute-done.9, bf16[128,1024]{1,0:T(8,128)(2,1)S(1)} %collective-permute-done.8), kind=kLoop, calls=%fused_computation | loop fusion | flops 2097152 | bytes 2621440 | tf_op jit(solution)/shard_map/convert_element_type | solution.py:616
Async XLA Ops:
  8.1 9.5 %collective-permute-start = (bf16[2,128,256]{2,1,0:T(8,128)(2,1)S(1)}, bf16[2,128,256]{2,1,0:T(8,128)(2,1)S(1)}, u32[]{:S(2)}, u32[]{:S(2)}) collective-permute-start(bf16[2,128,256]{2,1,0:T(8,128)(2,1)S(1)} %get-tuple-element.64), channel_id=1, source_target_pairs={{0,12},{4,8},{8,4},{12,0},{16,28},{20,24},{24,20},{28,16},{1,13},{... | collective-permute-start | bytes 393224 | tf_op jit(solution)/shard_map/ppermute | solution.py:574
  12.1 6.3 %collective-permute-start.1 = (bf16[2,128,256]{2,1,0:T(8,128)(2,1)S(1)}, bf16[2,128,256]{2,1,0:T(8,128)(2,1)S(1)}, u32[]{:S(2)}, u32[]{:S(2)}) collective-permute-start(bf16[2,128,256]{2,1,0:T(8,128)(2,1)S(1)} %get-tuple-element.65), channel_id=1, source_target_pairs={{0,4},{4,0},{8,12},{12,8},{16,20},{20,16},{24,28},{28,24},{1,5},{5... | collective-permute-start | bytes 393224 | tf_op jit(solution)/shard_map/ppermute | solution.py:574
  12.6 6.0 %collective-permute-start.2 = (bf16[2,128,256]{2,1,0:T(8,128)(2,1)S(1)}, bf16[2,128,256]{2,1,0:T(8,128)(2,1)S(1)}, u32[]{:S(2)}, u32[]{:S(2)}) collective-permute-start(bf16[2,128,256]{2,1,0:T(8,128)(2,1)S(1)} %get-tuple-element.66), channel_id=1, source_target_pairs={{0,8},{4,12},{8,0},{12,4},{16,24},{20,28},{24,16},{28,20},{1,9},{5... | collective-permute-start | bytes 393224 | tf_op jit(solution)/shard_map/ppermute | solution.py:574
  19.1 4.7 %copy-start = (bf16[2,128,128]{2,1,0:T(8,128)(2,1)}, bf16[2,128,128]{2,1,0:T(8,128)(2,1)S(1)}, u32[]{:S(2)}) copy-start(bf16[2,128,128]{2,1,0:T(8,128)(2,1)S(1)} %get-tuple-element.67.refs_8_) | copy-start | bytes 196612
  19.1 8.3 %collective-permute-start.3 = (bf16[2,128,128]{2,1,0:T(8,128)(2,1)S(1)}, bf16[2,128,128]{2,1,0:T(8,128)(2,1)S(1)}, u32[]{:S(2)}, u32[]{:S(2)}) collective-permute-start(bf16[2,128,128]{2,1,0:T(8,128)(2,1)S(1)} %get-tuple-element.67.refs_8_), channel_id=1, source_target_pairs={{0,16},{4,20},{8,24},{12,28},{1,17},{5,21},{9,25},{13,29},{2,18},{... | collective-permute-start | bytes 196616 | tf_op jit(solution)/shard_map/ppermute | solution.py:594
  27.8 6.6 %collective-permute-start.4 = (bf16[2,128,128]{2,1,0:T(8,128)(2,1)S(1)}, bf16[2,128,128]{2,1,0:T(8,128)(2,1)S(1)}, u32[]{:S(2)}, u32[]{:S(2)}) collective-permute-start(bf16[2,128,128]{2,1,0:T(8,128)(2,1)S(1)} %get-tuple-element.76), channel_id=1, source_target_pairs={{0,12},{4,8},{8,4},{12,0},{16,28},{20,24},{24,20},{28,16},{1,13},{... | collective-permute-start | bytes 196616 | tf_op jit(solution)/shard_map/ppermute | solution.py:598
  29.7 4.7 %collective-permute-start.5 = (bf16[2,128,128]{2,1,0:T(8,128)(2,1)S(1)}, bf16[2,128,128]{2,1,0:T(8,128)(2,1)S(1)}, u32[]{:S(2)}, u32[]{:S(2)}) collective-permute-start(bf16[2,128,128]{2,1,0:T(8,128)(2,1)S(1)} %get-tuple-element.77), channel_id=1, source_target_pairs={{0,4},{4,0},{8,12},{12,8},{16,20},{20,16},{24,28},{28,24},{1,5},{5... | collective-permute-start | bytes 196616 | tf_op jit(solution)/shard_map/ppermute | solution.py:598
  31.0 4.3 %collective-permute-start.6 = (bf16[2,128,128]{2,1,0:T(8,128)(2,1)S(1)}, bf16[2,128,128]{2,1,0:T(8,128)(2,1)S(1)}, u32[]{:S(2)}, u32[]{:S(2)}) collective-permute-start(bf16[2,128,128]{2,1,0:T(8,128)(2,1)S(1)} %get-tuple-element.78), channel_id=1, source_target_pairs={{0,8},{4,12},{8,0},{12,4},{16,24},{20,28},{24,16},{28,20},{1,9},{5... | collective-permute-start | bytes 196616 | tf_op jit(solution)/shard_map/ppermute | solution.py:598
  37.3 2.0 %collective-permute-start.7 = (bf16[128,2048]{1,0:T(8,128)(2,1)S(1)}, bf16[128,2048]{1,0:T(8,128)(2,1)S(1)}, u32[]{:S(2)}, u32[]{:S(2)}) collective-permute-start(bf16[128,2048]{1,0:T(8,128)(2,1)S(1)} %get-tuple-element.80), channel_id=1, source_target_pairs={{0,1},{1,0},{2,3},{3,2},{4,5},{5,4},{6,7},{7,6},{8,9},{9,8},{10,11... | collective-permute-start | bytes 1572872 | tf_op jit(solution)/shard_map/ppermute | solution.py:605
  39.4 14.0 %collective-permute-start.10 = (bf16[128,2048]{1,0:T(8,128)(2,1)S(1)}, bf16[128,2048]{1,0:T(8,128)(2,1)S(1)}, u32[]{:S(2)}, u32[]{:S(2)}) collective-permute-start(bf16[128,2048]{1,0:T(8,128)(2,1)S(1)} %add_convert_fusion.1), channel_id=1, source_target_pairs={{0,2},{1,3},{2,0},{3,1},{4,6},{5,7},{6,4},{7,5},{8,10},{9,11},{10,... | collective-permute-start | bytes 1572872 | tf_op jit(solution)/shard_map/ppermute | solution.py:606
  48.8 1.6 %collective-permute-start.8 = (bf16[128,1024]{1,0:T(8,128)(2,1)S(1)}, bf16[128,1024]{1,0:T(8,128)(2,1)S(1)}, u32[]{:S(2)}, u32[]{:S(2)}) collective-permute-start(bf16[128,1024]{1,0:T(8,128)(2,1)S(1)} %get-tuple-element.85), channel_id=1, source_target_pairs={{0,1},{1,0},{2,3},{3,2},{4,5},{5,4},{6,7},{7,6},{8,9},{9,8},{10,11... | collective-permute-start | bytes 786440 | tf_op jit(solution)/shard_map/ppermute | solution.py:613
  48.9 1.9 %collective-permute-start.9 = (bf16[128,1024]{1,0:T(8,128)(2,1)S(1)}, bf16[128,1024]{1,0:T(8,128)(2,1)S(1)}, u32[]{:S(2)}, u32[]{:S(2)}) collective-permute-start(bf16[128,1024]{1,0:T(8,128)(2,1)S(1)} %get-tuple-element.86), channel_id=1, source_target_pairs={{0,1},{1,0},{2,3},{3,2},{4,5},{5,4},{6,7},{7,6},{8,9},{9,8},{10,11... | collective-permute-start | bytes 786440 | tf_op jit(solution)/shard_map/ppermute | solution.py:613

commit v5 on v4

--- a/solution.py
+++ b/solution.py
@@ -66,36 +66,45 @@
     return jnp.where(where, 1.0, 0.0).astype(BF16)
 
 
+def spread(beside):
+    half = beside.shape[1] // 2
+    zeros = jnp.zeros((half, half), BF16)
+    top = jnp.concatenate([beside[:, :half], zeros], axis=1)
+    return jnp.concatenate([top, jnp.concatenate([zeros, beside[:, half:]], axis=1)], axis=0)
+
+
 def unit_lower_inverses(lowers):
     size = lowers[0].shape[0]
     half = size // 2
-    row, col = iota((size, size), 0), iota((size, size), 1)
-    crow, ccol = iota((half, size), 0), iota((half, size), 1)
-    zeros = jnp.zeros((size, size), BF16)
+    row, col = iota((half, size), 0), iota((half, size), 1)
+    col = jnp.bitwise_and(col, half - 1)
+    crow, ccol = iota((half // 2, size), 0), iota((half // 2, size), 1)
+    ccol = jnp.bitwise_and(ccol, half - 1)
+    zeros = jnp.zeros((half, size), BF16)
     eye, pair = as_mask(row == col), as_mask(row // 2 == col // 2)
-    xs = [eye - lower * pair for lower in lowers]
+    sides = [jnp.concatenate([lower[:half, :half], lower[half:, half:]], axis=1) for lower in lowers]
+    xs = [eye - side * pair for side in sides]
     n = 2
-    while n < size:
+    while n < half:
         if n < 16:
             mask = as_mask((row // n == col // n + 1) & (row // (2 * n) == col // (2 * n)))
-            ys = [mm(lower * mask, x).astype(BF16) for lower, x in zip(lowers, xs)]
-            zs = [mm(x, y).astype(BF16) for x, y in zip(xs, ys)]
+            ys = [mm(side * mask, spread(x)).astype(BF16) for side, x in zip(sides, xs)]
+            zs = [mm(x, spread(y)).astype(BF16) for x, y in zip(xs, ys)]
             xs = [x - z for x, z in zip(xs, zs)]
-        elif n < half:
+        else:
             mask = as_mask(ccol // n == 2 * (crow // n))
-            ys = [mm(odd_rows(lower, n) * mask, x).astype(BF16) for lower, x in zip(lowers, xs)]
+            ys = [mm(odd_rows(side, n) * mask, spread(x)).astype(BF16) for side, x in zip(sides, xs)]
             odds = [odd_rows(x, n) for x in xs]
-            zs = [mm(odd, weave(zeros, y, n)).astype(BF16) for odd, y in zip(odds, ys)]
+            zs = [mm(odd, spread(weave(zeros, y, n))).astype(BF16) for odd, y in zip(odds, ys)]
             xs = [weave(x, odd - z, n) for x, odd, z in zip(xs, odds, zs)]
-        else:
-            ys = [mm(lower[half:, :half], x[:half, :half]).astype(BF16) for lower, x in zip(lowers, xs)]
-            zs = [mm(x[half:, half:], y).astype(BF16) for x, y in zip(xs, ys)]
-            xs = [
-                jnp.concatenate([x[:half], jnp.concatenate([-z, x[half:, half:]], axis=1)], axis=0)
-                for x, z in zip(xs, zs)
-            ]
         n *= 2
-    return xs
+    ys = [mm(lower[half:, :half], x[:, :half]).astype(BF16) for lower, x in zip(lowers, xs)]
+    zs = [mm(x[:, half:], y).astype(BF16) for x, y in zip(xs, ys)]
+    full = []
+    for x, z in zip(xs, zs):
+        top = jnp.concatenate([x[:, :half], jnp.zeros((half, half), BF16)], axis=1)
+        full.append(jnp.concatenate([top, jnp.concatenate([-z, x[:, half:]], axis=1)], axis=0))
+    return full
 
 
 def decayed(c, b, product, mask):
@@ -105,10 +114,16 @@
         arg = c[i * h : (i + 1) * h] - b[:, j * h : (j + 1) * h]
         if i == j:
             arg = jnp.where(mask, arg, NEG)
-        return (jnp.exp(arg) * product[i * h : (i + 1) * h, j * h : (j + 1) * h]).astype(BF16)
-
-    top = jnp.concatenate([quarter(0, 0), jnp.zeros((h, h), BF16)], axis=1)
-    return jnp.concatenate([top, jnp.concatenate([quarter(1, 0), quarter(1, 1)], axis=1)], axis=0)
+        exact = jnp.exp(arg) * product[i * h : (i + 1) * h, j * h : (j + 1) * h]
+        rounded = exact.astype(BF16)
+        return rounded, (exact - rounded.astype(F32)).astype(BF16)
+
+    quarters = [quarter(0, 0), quarter(1, 0), quarter(1, 1)]
+    results = []
+    for a, b, c in zip(*quarters):
+        top = jnp.concatenate([a, jnp.zeros((h, h), BF16)], axis=1)
+        results.append(jnp.concatenate([top, jnp.concatenate([b, c], axis=1)], axis=0))
+    return results
 
 
 def reordered(x, quarters, first):
@@ -130,16 +145,16 @@
     return total
 
 
-def delta_kernel(rate, gate, beta, quarters, first, k_refs, v_refs, ends_refs, resid_ref, held_ref, cumul_ref, log_ref):
+def delta_kernel(waits, rate, gate, beta, quarters, first, k_refs, v_refs, ends_refs, resid_ref, held_ref, cumul_ref, log_ref):
+    waited(waits[0])
     tokens = k_refs[0].shape[0]
     heads = gate.shape[0]
     chunks = [slice(at, at + CHUNK) for at in range(0, tokens, CHUNK)]
 
     diagonal = iota((heads, heads), 0) == iota((heads, heads), 1)
-    rate = jnp.sum(jnp.where(diagonal, rate, 0.0), axis=1, keepdims=True)
-    decay = reordered(-rate * softplus(gate), quarters, first)
-    log_beta = reordered(-softplus(-beta), quarters, first)
-    log_k = log_norms(k_refs, heads, first)
+    rate = jnp.sum(jnp.where(diagonal, rate[...], 0.0), axis=1, keepdims=True)
+    decay = reordered(-rate * softplus(gate[...]), quarters, first)
+    log_beta = reordered(-softplus(-beta[...]), quarters, first)
 
     row, col = iota((CHUNK, CHUNK), 0), iota((CHUNK, CHUNK), 1)
     upto = jnp.where(row <= col, 1.0, 0.0).astype(BF16)
@@ -149,7 +164,10 @@
     square = CHUNK // 2
     strict = iota((square, square), 1) < iota((square, square), 0)
 
-    lowers, rights, ended, decays = {}, {}, {}, {}
+    waited(waits[1])
+    log_k = log_norms(k_refs, heads, first)
+    waited(waits[2])
+    lowers, rests, rights, ended, decays = {}, {}, {}, {}, {}
     for c, here in enumerate(chunks):
         parts = [sums[(3 * c + i) * heads : (3 * c + i + 1) * heads] for i in range(3)]
         cumul = parts[0] + parts[1] + parts[2]
@@ -161,26 +179,28 @@
         log_ref[:, here] = col_log
         key_end = jnp.exp(end - cumul + lk)
         ends = jnp.exp(end)
-        columns = jnp.concatenate([row_lower, jnp.exp(lb), jnp.exp(row_lower)], axis=0).T
+        columns = jnp.concatenate([row_lower, jnp.exp(lb), jnp.exp(row_lower), key_end], axis=0).T
         for j, (k_ref, v_ref) in enumerate(zip(k_refs, v_refs)):
             k = k_ref[here, :]
             k32 = k.astype(F32)
-            turned = k32.T
-            key_key = mm(k, turned.astype(BF16))
+            turned = k32.T.astype(BF16)
+            key_key = mm(k, turned)
             for r in range(2):
                 at = 2 * (first + j) + r
-                c_lower, c_beta, c_weight = (
-                    columns[:, heads * i + at : heads * i + at + 1] for i in range(3)
+                c_lower, c_beta, c_weight, c_end = (
+                    columns[:, heads * i + at : heads * i + at + 1] for i in range(4)
                 )
                 m = (c, 2 * j + r)
-                lowers[m] = decayed(c_lower, col_log[at : at + 1], key_key, strict)
+                lowers[m], rests[m] = decayed(c_lower, col_log[at : at + 1], key_key, strict)
                 v32 = v_ref[here, r * DV : (r + 1) * DV].astype(F32)
                 rights[m] = jnp.concatenate([c_beta * v32, c_weight * k32], axis=1).astype(BF16)
-                ended[m] = (turned * key_end[at : at + 1]).astype(BF16)
+                ended[m] = turned, c_end
                 decays[m] = ends[at : at + 1]
     names = list(lowers)
     inverses = dict(zip(names, unit_lower_inverses([lowers[m] for m in names])))
     solved = {m: mm(inverses[m], rights[m]) for m in names}
+    missed = {m: mm(rests[m], solved[m].astype(BF16)).astype(BF16) for m in names}
+    solved = {m: solved[m] - mm(inverses[m], missed[m]) for m in names}
     all_heads = range(2 * len(k_refs))
     state = {}
     for c, here in enumerate(chunks):
@@ -200,10 +220,12 @@
                 for a in all_heads
             }
             before = state
-        resid = {a: resid[a].astype(BF16) for a in all_heads}
         for a in all_heads:
-            resid_ref[a // 2, c, a % 2] = resid[a]
-        state = {a: decays[c, a] * before[a] + mm(ended[c, a], resid[a]) for a in all_heads}
+            resid_ref[a // 2, c, a % 2] = resid[a].astype(BF16)
+        state = {
+            a: decays[c, a] * before[a] + mm(ended[c, a][0], (ended[c, a][1] * resid[a]).astype(BF16))
+            for a in all_heads
+        }
     for a in all_heads:
         ends_refs[a // 2][a % 2] = state[a].astype(BF16)
 
@@ -225,7 +247,7 @@
             q32 = q.astype(F32)
             for a in (2 * j, 2 * j + 1):
                 b_row = logs[a : a + 1, here]
-                mixings[c, a] = decayed(columns[:, a : a + 1], b_row, query_key, inclusive)
+                mixings[c, a], _ = decayed(columns[:, a : a + 1], b_row, query_key, inclusive)
                 queries[c, a] = (columns[:, heads + a : heads + a + 1] * q32).astype(BF16)
     waited(waits)
     for c, a in mixings:
@@ -305,10 +327,8 @@
         moves += [lanes(v_hbm, q, ref) for q, ref in zip(quarters, v_refs)]
         moves += [lanes(k_hbm, member_ref[0], k_own), lanes(v_hbm, member_ref[0], v_own)]
         copies = started(moves, sems)
-        waited(copies[:-2])
-        delta_kernel(
-            rate[...], gate[...], beta[...], quarters, 0, k_refs, v_refs, ends, resid, held, cumul, logs
-        )
+        waits = copies[:3], copies[3 : 3 + count], copies[3 + count : -2]
+        delta_kernel(waits, rate, gate, beta, quarters, 0, k_refs, v_refs, ends, resid, held, cumul, logs)
         waited(copies[-2:])
 
     vmem = pltpu.VMEM
@@ -331,7 +351,7 @@
         earlier_refs, (ends,), out_hbm, local, sems = refs[:4], refs[4:5], refs[5:13], refs[13:17], refs[17]
         copies = started(zip(earlier_refs, out_hbm[:4]), sems)
         delta_kernel(
-            rate[...], gate[...], beta[...], [member_ref[0]], heads // 2 - 1, [k_own], [v_own], [ends], *local
+            [[]] * 3, rate, gate, beta, [member_ref[0]], heads // 2 - 1, [k_own], [v_own], [ends], *local
         )
         copies += started(zip(local, out_hbm[4:]), sems, 4)
         waited(copies)
@@ -457,17 +477,26 @@
     return call(kernel, "starts_part", groups, outs, [pltpu.VMEM((count, *state), BF16)], SMALL_VMEM, 10**8)
 
 
-def gated_rows(out, gain, z, at, first, start_refs, norm):
-    parts = []
-    for h in range(2 * len(start_refs)):
-        cols = slice(h * DV, (h + 1) * DV)
-        local = slice((2 * first + h) * DV, (2 * first + h + 1) * DV)
-        core = out[at, local].astype(F32) + mm(gain[at, local], start_refs[h // 2][h % 2])
-        mean = jnp.mean(core * core, axis=1, keepdims=True)
-        z_here = z[:, cols].astype(F32)
-        gate = z_here / (1.0 + jnp.exp(-z_here))
-        parts.append((core * lax.rsqrt(mean + 1e-6) * norm * gate).astype(BF16))
-    return jnp.concatenate(parts, axis=1)
+def gates(z, norm):
+    halved = 0.5 * z.astype(F32)
+    return halved * (1.0 + jnp.tanh(halved)) * norm
+
+
+def gated_pairs(out, gain, gate, at, first, start_refs):
+    pairs = []
+    ones = jnp.full((DV, DV), 1.0 / DV, BF16)
+    for j, start_ref in enumerate(start_refs):
+        parts = []
+        for r in range(2):
+            cols = slice((2 * j + r) * DV, (2 * j + r + 1) * DV)
+            local = slice((2 * (first + j) + r) * DV, (2 * (first + j) + r + 1) * DV)
+            rows = [jnp.concatenate([ref[i, local] for i, _ in at], axis=0) for ref in (out, gain)]
+            core = rows[0].astype(F32) + mm(rows[1], start_ref[r])
+            mean = mm((core * core).astype(BF16), ones)
+            weight = jnp.concatenate([gate[i, cols] for _, i in at], axis=0)
+            parts.append((core * lax.rsqrt(mean + 1e-6) * weight).astype(BF16))
+        pairs.append(jnp.concatenate(parts, axis=1))
+    return pairs
 
 
 def pair_moves(place_ref, turns, z_hbm, w_hbm, z, w):
@@ -487,49 +516,63 @@
     return [((rows, width), BF16), ((width, wide), BF16)]
 
 
-def local_rows(place_ref, rows, out):
-    return slice(None) if out.shape[0] == rows else pl.ds(pl.multiple_of(place_ref[0] * rows, rows), rows)
+def core_rows(place_ref, rows, out):
+    half = rows // 2
+    slices = []
+    for core in (1 - place_ref[1], place_ref[1]):
+        chip = 0 if out.shape[0] == rows else place_ref[0] * rows
+        slices.append([pl.ds(pl.multiple_of(start + core * half, half), half) for start in (chip, 0)])
+    return slices
+
+
+def projected(pairs, w):
+    width = 2 * DV
+    total = None
+    for j, gated in enumerate(pairs):
+        term = mm(gated, w[j * width : (j + 1) * width, :])
+        total = term if total is None else total + term
+    return total
 
 
 def keep_part(place, turns, rows, gate_z, weight, norm_gain, out, gain, start):
     wide = weight.shape[1]
     count = len(turns)
 
-    def kernel(place_ref, z_hbm, w_hbm, norm_hbm, out, gain, start_ref, sum_ref, norm, *refs):
-        away, own, sems = refs[:2], refs[2:4], refs[4]
-        moves = [(norm_hbm, norm)] + pair_moves(place_ref, [0], z_hbm, w_hbm, *own)
-        copies = started(moves + pair_moves(place_ref, turns, z_hbm, w_hbm, *away), sems)
+    def kernel(place_ref, z_hbm, w_hbm, norm_hbm, out, gain, start_ref, sum_ref, gate_ref, w_away, *refs):
+        norm, own_gate, z_away, z_own, w_own, sems = refs
+        moves = [(norm_hbm, norm)] + pair_moves(place_ref, [0], z_hbm, w_hbm, z_own, w_own)
+        copies = started(moves + pair_moves(place_ref, turns, z_hbm, w_hbm, z_away, w_away), sems)
         waited(copies[:2])
-        gated = gated_rows(out, gain, own[0], local_rows(place_ref, rows, out), count, [start_ref], norm[...])
-        waited(copies[2:3])
-        sum_ref[...] = mm(gated, own[1][...])
-        waited(copies[3:])
+        for h in range(2):
+            cols = slice(h * DV, (h + 1) * DV)
+            own_gate[:, cols] = gates(z_own[:, cols], norm[...])
+        pairs = gated_pairs(out, gain, own_gate, core_rows(place_ref, rows, out), count, [start_ref])
+        waited(copies[2 : 3 + count])
+        for h in range(2 * count):
+            cols = slice(h * DV, (h + 1) * DV)
+            gate_ref[:, cols] = gates(z_away[:, cols], norm[...])
+        sum_ref[...] = projected(pairs, w_own)
+        waited(copies[3 + count :])
 
     vmem = pltpu.MemorySpace.VMEM
-    outs = [(vmem, (rows, wide), F32), (vmem, (1, DV), F32)]
-    outs += [(vmem, *shape) for shape in pair_buffers(count, rows, wide)]
-    scratch = [pltpu.VMEM(*shape) for shape in pair_buffers(1, rows, wide)]
+    (z_shape, _), (w_shape, _) = pair_buffers(count, rows, wide)
+    outs = [(vmem, (rows, wide), F32), (vmem, z_shape, F32), (vmem, w_shape, BF16)]
+    scratch = [pltpu.VMEM((1, DV), F32), pltpu.VMEM((rows, 2 * DV), F32), pltpu.VMEM(z_shape, BF16)]
+    scratch += [pltpu.VMEM(*shape) for shape in pair_buffers(1, rows, wide)]
     scratch += [pltpu.SemaphoreType.DMA((3 + 2 * count,))]
     groups = [(pltpu.SMEM, [place]), (pltpu.HBM, [gate_z, weight, norm_gain]), (pltpu.VMEM, [out, gain, start])]
     return call(kernel, "keep_part", groups, outs, scratch, PROJECT_VMEM, 4 * rows * DV * wide)
 
 
-def send_rows(partial, core, send_refs, stay_ref):
-    rows, width = send_refs[0].shape
-    one, two = partial[:rows], partial[rows:]
-    send = jnp.where(core == 0, two, one).astype(BF16)
-    for i, ref in enumerate(send_refs):
-        ref[...] = send[:, i * width : (i + 1) * width]
-    stay_ref[...] = jnp.where(core == 0, one, two)
-
-
 def away_part(place, kept, out, gain, starts):
     rows, wide = kept[0].shape
 
-    def kernel(place_ref, sum_ref, norm, z, w, out, gain, *refs):
+    def kernel(place_ref, sum_ref, gate, w, out, gain, *refs):
         start_refs, (send_ref, stay_ref) = refs[:-2], refs[-2:]
-        gated = gated_rows(out, gain, z, local_rows(place_ref, rows, out), 0, start_refs, norm[...])
-        send_rows(mm(gated, w[...]) + sum_ref[...], place_ref[1], [send_ref], stay_ref)
+        pairs = gated_pairs(out, gain, gate, core_rows(place_ref, rows, out), 0, start_refs)
+        partial = projected(pairs, w) + sum_ref[...]
+        send_ref[...] = partial[: rows // 2].astype(BF16)
+        stay_ref[...] = partial[rows // 2 :]
 
     vmem = pltpu.MemorySpace.VMEM
     outs = [(vmem, (rows // 2, wide), BF16), (vmem, (rows // 2, wide), F32)]
@@ -542,17 +585,25 @@
     count = len(turns) + 1
 
     def kernel(place_ref, z_hbm, w_hbm, norm_hbm, out, gain, *refs):
-        start_refs, sends, (stay_ref, norm, z, w, sems) = refs[:count], refs[count : count + 2], refs[count + 2 :]
+        start_refs, sends, (stay_ref, norm, gate, z, w, sems) = refs[:count], refs[count : count + 2], refs[count + 2 :]
         moves = [(norm_hbm, norm)] + pair_moves(place_ref, (*turns, 0), z_hbm, w_hbm, z, w)
         copies = started(moves, sems)
         waited(copies[: 1 + count])
-        gated = gated_rows(out, gain, z, local_rows(place_ref, rows, out), 0, start_refs, norm[...])
+        for h in range(2 * count):
+            cols = slice(h * DV, (h + 1) * DV)
+            gate[:, cols] = gates(z[:, cols], norm[...])
+        pairs = gated_pairs(out, gain, gate, core_rows(place_ref, rows, out), 0, start_refs)
         waited(copies[1 + count :])
-        send_rows(mm(gated, w[...]), place_ref[1], sends, stay_ref)
+        partial = projected(pairs, w)
+        for i, ref in enumerate(sends):
+            ref[...] = partial[: rows // 2, i * (wide // 2) : (i + 1) * (wide // 2)].astype(BF16)
+        stay_ref[...] = partial[rows // 2 :]
 
     vmem = pltpu.MemorySpace.VMEM
     outs = [(vmem, (rows // 2, wide // 2), BF16)] * 2 + [(vmem, (rows // 2, wide), F32)]
-    scratch = [pltpu.VMEM((1, DV), F32)] + [pltpu.VMEM(*shape) for shape in pair_buffers(count, rows, wide)]
+    (z_shape, _), _ = pair_buffers(count, rows, wide)
+    scratch = [pltpu.VMEM((1, DV), F32), pltpu.VMEM(z_shape, F32)]
+    scratch += [pltpu.VMEM(*shape) for shape in pair_buffers(count, rows, wide)]
     scratch += [pltpu.SemaphoreType.DMA((1 + 2 * count,))]
     groups = [(pltpu.SMEM, [place]), (pltpu.HBM, [gate_z, weight, norm_gain]), (pltpu.VMEM, [out, gain, *starts])]
     return call(kernel, "whole_part", groups, outs, scratch, PROJECT_VMEM, 2 * rows * weight.size)

time: 54.6 us -> 54.4 us (level)
  transfers between devices with their start and end apart: 11 -> 11, of which waited for: 7 -> 7; matrix products, arithmetic and copies ran while one was open for 0% -> 0% of each run, Pallas kernels for 35% -> 36%
where the time goes in v5:
time: 54.4 us; the launch traced here: 54.2 us
  Pallas kernels  30.2 us (56%)
  starting transfers between devices  15.1 us (28%)
  waiting for transfers between devices  7.5 us (14%)
  other arithmetic  1.24 us (2%)
    pallas_call x9, Pallas kernels, call(): pl.pallas_call(kernel, in_specs=specs, out_specs=[pl.BlockSpec(memory_spa...  30.2 us
    ppermute x3, starting transfers between devices, on_device(): lax.ppermute(a, 'seq', pairs[turn])  4.69 us
    ppermute x1, starting transfers between devices, on_device(): came.append(lax.ppermute(ending, 'seq', along))  4.66 us
    ppermute x3, starting transfers between devices, on_device(): lax.ppermute(g, 'seq', pairs[turn])  3.55 us
    ppermute x1, waiting for transfers between devices, on_device(): lax.ppermute(both, 'head', [(i, (i + 2 * by) % cores) for i in range(core...  2.58 us
    ppermute x1, waiting for transfers between devices, on_device(): both = (stay + lax.ppermute(give, 'head', swap).astype(F32)).astype(BF16)  1.81 us
    ppermute x1, starting transfers between devices, on_device(): lax.ppermute(both, 'head', [(i, (i + 2 * by) % cores) for i in range(core...  1.56 us
    ppermute x2, waiting for transfers between devices, on_device(): lax.ppermute(g, 'head', swap)  1.4 us
  transfers between devices with their start and end apart: 11, of which 7 were waited for; matrix products, arithmetic and copies ran while one was open for 0% of the time, Pallas kernels for 36%

profile of v5, /device:TPU:0, one launch (start us, length us, event | category | flops | bytes accessed | tf_op | source)
XLA Modules:
  0.0 54.2 jit_solution(108866538517752893)
XLA Ops:
  0.0 8.0 %first_part.1 = (bf16[2,128,256]{2,1,0:T(8,128)(2,1)S(1)}, bf16[2,128,256]{2,1,0:T(8,128)(2,1)S(1)}, bf16[2,128,256]{2,1,0:T(8,128)(2,1)S(1)}, bf16[3,2,2,256,25...) custom-call(s32[1]{0:T(128)} %bitcast.2.member_ref, ...), custom_call_target="tpu_custom_call" | custom-call | flops 6000000000 | bytes 1048576 | tf_op jit(solution)/shard_map/first_part/pallas_call | solution.py:292
  8.1 4.0 %collective-permute-start = (bf16[2,128,256]{2,1,0:T(8,128)(2,1)S(1)}, bf16[2,128,256]{2,1,0:T(8,128)(2,1)S(1)}, u32[]{:S(2)}, u32[]{:S(2)}) collective-permute-start(bf16[2,128,256]{2,1,0:T(8,128)(2,1)S(1)} %get-tuple-element.63), channel_id=1, source_target_pairs={{0,12},{4,8},{8,4},{12,0},{16,28},{20,24},{24,20},{28,16},{1,13},{... | collective-permute-start | bytes 393224 | tf_op jit(solution)/shard_map/ppermute | solution.py:625
  12.1 0.5 collective-permute-start.1
  12.6 0.1 collective-permute-start.2
  12.7 4.8 %second_part.1 = (bf16[2,128,256]{2,1,0:T(8,128)(2,1)S(1)}, bf16[3,2,2,256,256]{4,3,2,1,0:T(8,128)(2,1)}, bf16[3,2,2,128,256]{4,3,2,1,0:T(8,128)(2,1)}, f32[8,51...) custom-call(s32[1]{0:T(128)} %bitcast.2.member_ref, ...), custom_call_target="tpu_custom_call" | custom-call | flops 2000000000 | bytes 1048576 | tf_op jit(solution)/shard_map/second_part/pallas_call | solution.py:292
  17.6 0.1 add_add_fusion.1.place_ref
  17.7 0.0 collective-permute-done.refs_0_
  17.7 0.7 %collective-permute-done.1.refs_1_ = bf16[2,128,256]{2,1,0:T(8,128)(2,1)S(1)} collective-permute-done((bf16[2,128,256]{2,1,0:T(8,128)(2,1)S(1)}, bf16[2,128,256]{2,1,0:T(8,128)(2,1)S(1)}, u32[]{:S(2)}, u32[]{:S(2)}) %collective-permute-start.1) | collective-permute-done | bytes 131104 | tf_op jit(solution)/shard_map/ppermute | solution.py:625
  18.4 0.2 collective-permute-done.2.refs_2_
  18.6 0.5 group_part.1
  19.1 0.0 copy-start
  19.1 4.7 %collective-permute-start.3 = (bf16[2,128,128]{2,1,0:T(8,128)(2,1)S(1)}, bf16[2,128,128]{2,1,0:T(8,128)(2,1)S(1)}, u32[]{:S(2)}, u32[]{:S(2)}) collective-permute-start(bf16[2,128,128]{2,1,0:T(8,128)(2,1)S(1)} %get-tuple-element.66.refs_8_), channel_id=1, source_target_pairs={{0,16},{4,20},{8,24},{12,28},{1,17},{5,21},{9,25},{13,29},{2,18},{... | collective-permute-start | bytes 196616 | tf_op jit(solution)/shard_map/ppermute | solution.py:645
  23.7 0.0 copy-done
  23.7 3.6 %third_part.2 = (bf16[256,1024]{1,0:T(8,128)(2,1)S(1)}, bf16[256,1024]{1,0:T(8,128)(2,1)S(1)}) custom-call(s32[3]{0:T(128)S(1)} %add_add_fusion.1.place_ref, bf16[512,512]{1,0:T(8,128)(2,1)} %q_hbm.3, bf16[512,512]{1,0:T(8,128)(2,1)} %k_hbm.5, bf16[3,2,2,256,256]{4,3,2,1,0:T(8,128)(2,1)} %get-tuple-element.54.refs_0_, ...), custom_call_target="tpu_custom_call" | custom-call | flops 3000000000 | bytes 1048576 | tf_op jit(solution)/shard_map/third_part/pallas_call | solution.py:292
  27.3 0.0 collective-permute-done.3.refs_0_
  27.3 0.5 starts_part.1
  27.8 2.1 %collective-permute-start.4 = (bf16[2,128,128]{2,1,0:T(8,128)(2,1)S(1)}, bf16[2,128,128]{2,1,0:T(8,128)(2,1)S(1)}, u32[]{:S(2)}, u32[]{:S(2)}) collective-permute-start(bf16[2,128,128]{2,1,0:T(8,128)(2,1)S(1)} %get-tuple-element.74), channel_id=1, source_target_pairs={{0,12},{4,8},{8,4},{12,0},{16,28},{20,24},{24,20},{28,16},{1,13},{... | collective-permute-start | bytes 196616 | tf_op jit(solution)/shard_map/ppermute | solution.py:649
  29.9 1.1 %collective-permute-start.5 = (bf16[2,128,128]{2,1,0:T(8,128)(2,1)S(1)}, bf16[2,128,128]{2,1,0:T(8,128)(2,1)S(1)}, u32[]{:S(2)}, u32[]{:S(2)}) collective-permute-start(bf16[2,128,128]{2,1,0:T(8,128)(2,1)S(1)} %get-tuple-element.75), channel_id=1, source_target_pairs={{0,4},{4,0},{8,12},{12,8},{16,20},{20,16},{24,28},{28,24},{1,5},{5... | collective-permute-start | bytes 196616 | tf_op jit(solution)/shard_map/ppermute | solution.py:649
  31.0 0.4 collective-permute-start.6
  31.4 3.0 %keep_part.1 = (f32[256,2048]{1,0:T(8,128)S(1)}, f32[256,768]{1,0:T(8,128)S(1)}, bf16[768,2048]{1,0:T(8,128)(2,1)S(1)}) custom-call(s32[3]{0:T(128)S(1)} %add_add_fusion.1.place_ref, bf16[512,1024]{1,0:T(8,128)(2,1)} %z_hbm.3, bf16[1024,2048]{1,0:T(8,128)(2,1)} %w_hbm.3, f32[1,128]{1,0:T(1,128)} %bitcast.8, ...), custom_call_target="tpu_custom_call" | custom-call | flops 268435456 | bytes 1048576 | tf_op jit(solution)/shard_map/keep_part/pallas_call | solution.py:292
  34.4 0.0 collective-permute-done.4.refs_0_
  34.4 0.0 collective-permute-done.5.refs_1_
  34.4 0.8 %collective-permute-done.6.refs_2_ = bf16[2,128,128]{2,1,0:T(8,128)(2,1)S(1)} collective-permute-done((bf16[2,128,128]{2,1,0:T(8,128)(2,1)S(1)}, bf16[2,128,128]{2,1,0:T(8,128)(2,1)S(1)}, u32[]{:S(2)}, u32[]{:S(2)}) %collective-permute-start.6) | collective-permute-done | bytes 65568 | tf_op jit(solution)/shard_map/ppermute | solution.py:649
  35.2 1.9 %away_part.1 = (bf16[128,2048]{1,0:T(8,128)(2,1)S(1)}, f32[128,2048]{1,0:T(8,128)S(1)}) custom-call(s32[3]{0:T(128)S(1)} %add_add_fusion.1.place_ref, f32[256,2048]{1,0:T(8,128)S(1)} %get-tuple-element.71.sum_ref, f32[256,768]{1,0:T(8,128)S(1)} %get-tuple-element.72.gate, bf16[768,2048]{1,0:T(8,128)(2,1)S(1)} %get-tuple-element.73.w, ...), custom_call_target="tpu_custom_call" | custom-call | flops 805306368 | bytes 1048576 | tf_op jit(solution)/shard_map/away_part/pallas_call | solution.py:292
  37.1 0.1 collective-permute-start.7
  37.2 0.1 add_add_fusion.place_ref
  37.3 1.8 %collective-permute-done.7 = bf16[128,2048]{1,0:T(8,128)(2,1)S(1)} collective-permute-done((bf16[128,2048]{1,0:T(8,128)(2,1)S(1)}, bf16[128,2048]{1,0:T(8,128)(2,1)S(1)}, u32[]{:S(2)}, u32[]{:S(2)}) %collective-permute-start.7) | collective-permute-done | bytes 524320 | tf_op jit(solution)/shard_map/ppermute | solution.py:656
  39.1 0.1 add_convert_fusion.1
  39.2 1.6 %collective-permute-start.10 = (bf16[128,2048]{1,0:T(8,128)(2,1)S(1)}, bf16[128,2048]{1,0:T(8,128)(2,1)S(1)}, u32[]{:S(2)}, u32[]{:S(2)}) collective-permute-start(bf16[128,2048]{1,0:T(8,128)(2,1)S(1)} %add_convert_fusion.1), channel_id=1, source_target_pairs={{0,2},{1,3},{2,0},{3,1},{4,6},{5,7},{6,4},{7,5},{8,10},{9,11},{10,... | collective-permute-start | bytes 1572872 | tf_op jit(solution)/shard_map/ppermute | solution.py:657
  40.8 3.6 %third_part.3 = (bf16[256,1024]{1,0:T(8,128)(2,1)S(1)}, bf16[256,1024]{1,0:T(8,128)(2,1)S(1)}) custom-call(s32[3]{0:T(128)S(1)} %add_add_fusion.place_ref, bf16[512,512]{1,0:T(8,128)(2,1)} %q_hbm.3, bf16[512,512]{1,0:T(8,128)(2,1)} %k_hbm.5, bf16[3,2,2,256,256]{4,3,2,1,0:T(8,128)(2,1)} %get-tuple-element.54.refs_0_, ...), custom_call_target="tpu_custom_call" | custom-call | flops 3000000000 | bytes 1048576 | tf_op jit(solution)/shard_map/third_part/pallas_call | solution.py:292
  44.3 4.3 %whole_part.1 = (bf16[128,1024]{1,0:T(8,128)(2,1)S(1)}, bf16[128,1024]{1,0:T(8,128)(2,1)S(1)}, f32[128,2048]{1,0:T(8,128)S(1)}) custom-call(s32[3]{0:T(128)S(1)} %add_add_fusion.place_ref, bf16[512,1024]{1,0:T(8,128)(2,1)} %z_hbm.3, bf16[1024,2048]{1,0:T(8,128)(2,1)} %w_hbm.3, f32[1,128]{1,0:T(1,128)} %bitcast.9, ...), custom_call_target="tpu_custom_call" | custom-call | flops 1073741824 | bytes 1048576 | tf_op jit(solution)/shard_map/whole_part/pallas_call | solution.py:292
  48.7 0.1 collective-permute-start.8
  48.8 0.5 collective-permute-start.9
  49.3 1.0 %collective-permute-done.8 = bf16[128,1024]{1,0:T(8,128)(2,1)S(1)} collective-permute-done((bf16[128,1024]{1,0:T(8,128)(2,1)S(1)}, bf16[128,1024]{1,0:T(8,128)(2,1)S(1)}, u32[]{:S(2)}, u32[]{:S(2)}) %collective-permute-start.8) | collective-permute-done | bytes 262176 | tf_op jit(solution)/shard_map/ppermute | solution.py:664
  50.3 0.4 collective-permute-done.9
  50.7 2.6 %collective-permute-done.10 = bf16[128,2048]{1,0:T(8,128)(2,1)S(1)} collective-permute-done((bf16[128,2048]{1,0:T(8,128)(2,1)S(1)}, bf16[128,2048]{1,0:T(8,128)(2,1)S(1)}, u32[]{:S(2)}, u32[]{:S(2)}) %collective-permute-start.10) | collective-permute-done | bytes 524320 | tf_op jit(solution)/shard_map/ppermute | solution.py:657
  53.2 1.0 %add_convert_fusion = bf16[128,2048]{1,0:T(8,128)(2,1)} fusion(bf16[128,2048]{1,0:T(8,128)(2,1)S(1)} %collective-permute-done.10, f32[128,2048]{1,0:T(8,128)S(1)} %get-tuple-element.82, bf16[128,1024]{1,0:T(8,128)(2,1)S(1)} %collective-permute-done.9, bf16[128,1024]{1,0:T(8,128)(2,1)S(1)} %collective-permute-done.8), kind=kLoop, calls=%fused_computation | loop fusion | flops 2097152 | bytes 2621440 | tf_op jit(solution)/shard_map/convert_element_type | solution.py:667
Async XLA Ops:
  8.1 9.6 %collective-permute-start = (bf16[2,128,256]{2,1,0:T(8,128)(2,1)S(1)}, bf16[2,128,256]{2,1,0:T(8,128)(2,1)S(1)}, u32[]{:S(2)}, u32[]{:S(2)}) collective-permute-start(bf16[2,128,256]{2,1,0:T(8,128)(2,1)S(1)} %get-tuple-element.63), channel_id=1, source_target_pairs={{0,12},{4,8},{8,4},{12,0},{16,28},{20,24},{24,20},{28,16},{1,13},{... | collective-permute-start | bytes 393224 | tf_op jit(solution)/shard_map/ppermute | solution.py:625
  12.1 6.3 %collective-permute-start.1 = (bf16[2,128,256]{2,1,0:T(8,128)(2,1)S(1)}, bf16[2,128,256]{2,1,0:T(8,128)(2,1)S(1)}, u32[]{:S(2)}, u32[]{:S(2)}) collective-permute-start(bf16[2,128,256]{2,1,0:T(8,128)(2,1)S(1)} %get-tuple-element.64), channel_id=1, source_target_pairs={{0,4},{4,0},{8,12},{12,8},{16,20},{20,16},{24,28},{28,24},{1,5},{5... | collective-permute-start | bytes 393224 | tf_op jit(solution)/shard_map/ppermute | solution.py:625
  12.6 6.0 %collective-permute-start.2 = (bf16[2,128,256]{2,1,0:T(8,128)(2,1)S(1)}, bf16[2,128,256]{2,1,0:T(8,128)(2,1)S(1)}, u32[]{:S(2)}, u32[]{:S(2)}) collective-permute-start(bf16[2,128,256]{2,1,0:T(8,128)(2,1)S(1)} %get-tuple-element.65), channel_id=1, source_target_pairs={{0,8},{4,12},{8,0},{12,4},{16,24},{20,28},{24,16},{28,20},{1,9},{5... | collective-permute-start | bytes 393224 | tf_op jit(solution)/shard_map/ppermute | solution.py:625
  19.1 4.7 %copy-start = (bf16[2,128,128]{2,1,0:T(8,128)(2,1)}, bf16[2,128,128]{2,1,0:T(8,128)(2,1)S(1)}, u32[]{:S(2)}) copy-start(bf16[2,128,128]{2,1,0:T(8,128)(2,1)S(1)} %get-tuple-element.66.refs_8_) | copy-start | bytes 196612
  19.1 8.3 %collective-permute-start.3 = (bf16[2,128,128]{2,1,0:T(8,128)(2,1)S(1)}, bf16[2,128,128]{2,1,0:T(8,128)(2,1)S(1)}, u32[]{:S(2)}, u32[]{:S(2)}) collective-permute-start(bf16[2,128,128]{2,1,0:T(8,128)(2,1)S(1)} %get-tuple-element.66.refs_8_), channel_id=1, source_target_pairs={{0,16},{4,20},{8,24},{12,28},{1,17},{5,21},{9,25},{13,29},{2,18},{... | collective-permute-start | bytes 196616 | tf_op jit(solution)/shard_map/ppermute | solution.py:645
  27.8 6.6 %collective-permute-start.4 = (bf16[2,128,128]{2,1,0:T(8,128)(2,1)S(1)}, bf16[2,128,128]{2,1,0:T(8,128)(2,1)S(1)}, u32[]{:S(2)}, u32[]{:S(2)}) collective-permute-start(bf16[2,128,128]{2,1,0:T(8,128)(2,1)S(1)} %get-tuple-element.74), channel_id=1, source_target_pairs={{0,12},{4,8},{8,4},{12,0},{16,28},{20,24},{24,20},{28,16},{1,13},{... | collective-permute-start | bytes 196616 | tf_op jit(solution)/shard_map/ppermute | solution.py:649
  29.9 4.5 %collective-permute-start.5 = (bf16[2,128,128]{2,1,0:T(8,128)(2,1)S(1)}, bf16[2,128,128]{2,1,0:T(8,128)(2,1)S(1)}, u32[]{:S(2)}, u32[]{:S(2)}) collective-permute-start(bf16[2,128,128]{2,1,0:T(8,128)(2,1)S(1)} %get-tuple-element.75), channel_id=1, source_target_pairs={{0,4},{4,0},{8,12},{12,8},{16,20},{20,16},{24,28},{28,24},{1,5},{5... | collective-permute-start | bytes 196616 | tf_op jit(solution)/shard_map/ppermute | solution.py:649
  31.0 4.3 %collective-permute-start.6 = (bf16[2,128,128]{2,1,0:T(8,128)(2,1)S(1)}, bf16[2,128,128]{2,1,0:T(8,128)(2,1)S(1)}, u32[]{:S(2)}, u32[]{:S(2)}) collective-permute-start(bf16[2,128,128]{2,1,0:T(8,128)(2,1)S(1)} %get-tuple-element.76), channel_id=1, source_target_pairs={{0,8},{4,12},{8,0},{12,4},{16,24},{20,28},{24,16},{28,20},{1,9},{5... | collective-permute-start | bytes 196616 | tf_op jit(solution)/shard_map/ppermute | solution.py:649
  37.1 2.0 %collective-permute-start.7 = (bf16[128,2048]{1,0:T(8,128)(2,1)S(1)}, bf16[128,2048]{1,0:T(8,128)(2,1)S(1)}, u32[]{:S(2)}, u32[]{:S(2)}) collective-permute-start(bf16[128,2048]{1,0:T(8,128)(2,1)S(1)} %get-tuple-element.78), channel_id=1, source_target_pairs={{0,1},{1,0},{2,3},{3,2},{4,5},{5,4},{6,7},{7,6},{8,9},{9,8},{10,11... | collective-permute-start | bytes 1572872 | tf_op jit(solution)/shard_map/ppermute | solution.py:656
  39.2 14.0 %collective-permute-start.10 = (bf16[128,2048]{1,0:T(8,128)(2,1)S(1)}, bf16[128,2048]{1,0:T(8,128)(2,1)S(1)}, u32[]{:S(2)}, u32[]{:S(2)}) collective-permute-start(bf16[128,2048]{1,0:T(8,128)(2,1)S(1)} %add_convert_fusion.1), channel_id=1, source_target_pairs={{0,2},{1,3},{2,0},{3,1},{4,6},{5,7},{6,4},{7,5},{8,10},{9,11},{10,... | collective-permute-start | bytes 1572872 | tf_op jit(solution)/shard_map/ppermute | solution.py:657
  48.7 1.6 %collective-permute-start.8 = (bf16[128,1024]{1,0:T(8,128)(2,1)S(1)}, bf16[128,1024]{1,0:T(8,128)(2,1)S(1)}, u32[]{:S(2)}, u32[]{:S(2)}) collective-permute-start(bf16[128,1024]{1,0:T(8,128)(2,1)S(1)} %get-tuple-element.83), channel_id=1, source_target_pairs={{0,1},{1,0},{2,3},{3,2},{4,5},{5,4},{6,7},{7,6},{8,9},{9,8},{10,11... | collective-permute-start | bytes 786440 | tf_op jit(solution)/shard_map/ppermute | solution.py:664
  48.8 1.9 %collective-permute-start.9 = (bf16[128,1024]{1,0:T(8,128)(2,1)S(1)}, bf16[128,1024]{1,0:T(8,128)(2,1)S(1)}, u32[]{:S(2)}, u32[]{:S(2)}) collective-permute-start(bf16[128,1024]{1,0:T(8,128)(2,1)S(1)} %get-tuple-element.84), channel_id=1, source_target_pairs={{0,1},{1,0},{2,3},{3,2},{4,5},{5,4},{6,7},{7,6},{8,9},{9,8},{10,11... | collective-permute-start | bytes 786440 | tf_op jit(solution)/shard_map/ppermute | solution.py:664

commit v6 on v5

--- a/solution.py
+++ b/solution.py
@@ -145,7 +145,7 @@
     return total
 
 
-def delta_kernel(waits, rate, gate, beta, quarters, first, k_refs, v_refs, ends_refs, resid_ref, held_ref, cumul_ref, log_ref):
+def delta_kernel(waits, rate, gate, beta, quarters, first, k_refs, v_refs, ends_refs, work_ref, marks_ref):
     waited(waits[0])
     tokens = k_refs[0].shape[0]
     heads = gate.shape[0]
@@ -175,8 +175,8 @@
         lb, lk = log_beta[:, here], log_k[:, here]
         col_log = cumul - lk
         row_lower = cumul + lb + lk
-        cumul_ref[:, here] = cumul
-        log_ref[:, here] = col_log
+        marks_ref[:heads, here] = cumul
+        marks_ref[heads:, here] = col_log
         key_end = jnp.exp(end - cumul + lk)
         ends = jnp.exp(end)
         columns = jnp.concatenate([row_lower, jnp.exp(lb), jnp.exp(row_lower), key_end], axis=0).T
@@ -209,11 +209,11 @@
             before = iota((DK, DV + DK), 1) == iota((DK, DV + DK), 0) + DV
             before = {a: jnp.where(before, 1.0, 0.0) for a in all_heads}
             for a in all_heads:
-                held_ref[a // 2, c, a % 2] = before[a].astype(BF16)
+                work_ref[a // 2, c, a % 2, CHUNK:, :] = before[a].astype(BF16)
         else:
             held = {a: state[a].astype(BF16) for a in all_heads}
             for a in all_heads:
-                held_ref[a // 2, c, a % 2] = held[a]
+                work_ref[a // 2, c, a % 2, CHUNK:, :] = held[a]
             moved = {a: mm(solved[c, a][:, DV:].astype(BF16), held[a]) for a in all_heads}
             resid = {
                 a: jnp.concatenate([solved[c, a][:, :DV] - moved[a][:, :DV], -moved[a][:, DV:]], axis=1)
@@ -221,7 +221,7 @@
             }
             before = state
         for a in all_heads:
-            resid_ref[a // 2, c, a % 2] = resid[a].astype(BF16)
+            work_ref[a // 2, c, a % 2, :CHUNK, :] = resid[a].astype(BF16)
         state = {
             a: decays[c, a] * before[a] + mm(ended[c, a][0], (ended[c, a][1] * resid[a]).astype(BF16))
             for a in all_heads
@@ -257,11 +257,6 @@
         gain_ref[here, a * DK : (a + 1) * DK] = result[:, DV:].astype(BF16)
 
 
-def lanes(source, which, target):
-    width = target.shape[1]
-    return source.at[:, pl.ds(pl.multiple_of(which * width, 128), width)], target
-
-
 def started(moves, sems, first=0):
     copies = [pltpu.make_async_copy(a, b, sems.at[first + i]) for i, (a, b) in enumerate(moves)]
     for copy in copies:
@@ -303,105 +298,121 @@
 
 def local_shapes(count, tokens, heads):
     chunks = tokens // CHUNK
-    return [
-        ((count, chunks, 2, CHUNK, DV + DK), BF16),
-        ((count, chunks, 2, DK, DV + DK), BF16),
-        ((heads, tokens), F32),
-        ((heads, tokens), F32),
-    ]
-
-
-def first_part(member, turns, rate, keys, values, gate_logit, beta_logit):
+    return [((count, chunks, 2, CHUNK + DK, DV + DK), BF16), ((2 * heads, tokens), F32)]
+
+
+def pair_lanes(ref, quarter, width):
+    return ref.at[:, pl.ds(pl.multiple_of(quarter * width, width), width)]
+
+
+def first_part(code, turns, rate, keys, values, gate_logit, beta_logit):
     heads, tokens = gate_logit.shape
     count = len(turns)
-    key_part, value_part = (tokens, DK), (tokens, 2 * DV)
-
-    def kernel(member_ref, rate_hbm, k_hbm, v_hbm, gate_hbm, beta_hbm, *refs):
-        ends, (resid, held, cumul, logs, rate, gate, beta, k_own, v_own), refs = (
-            refs[:count], refs[count : count + 9], refs[count + 9 :]
-        )
+
+    def kernel(code_ref, rate_hbm, gate_hbm, beta_hbm, k_hbm, v_hbm, *refs):
+        ends, (work, marks, rate, gate, beta, k_own, v_own), refs = refs[:count], refs[count : count + 7], refs[count + 7 :]
         k_refs, v_refs, sems = refs[:count], refs[count : 2 * count], refs[-1]
-        quarters = [jnp.bitwise_xor(member_ref[0], turn) for turn in turns]
+        pair = jnp.bitwise_and(code_ref[0], count)
+        quarters = [jnp.bitwise_xor(pair, turn) for turn in turns]
         moves = [(rate_hbm, rate), (gate_hbm, gate), (beta_hbm, beta)]
-        moves += [lanes(k_hbm, q, ref) for q, ref in zip(quarters, k_refs)]
-        moves += [lanes(v_hbm, q, ref) for q, ref in zip(quarters, v_refs)]
-        moves += [lanes(k_hbm, member_ref[0], k_own), lanes(v_hbm, member_ref[0], v_own)]
+        moves += [(pair_lanes(k_hbm, q, DK), ref) for q, ref in zip(quarters, k_refs)]
+        moves += [(pair_lanes(v_hbm, q, 2 * DV), ref) for q, ref in zip(quarters, v_refs)]
+        moves += [(pair_lanes(k_hbm, pair, DK), k_own), (pair_lanes(v_hbm, pair, 2 * DV), v_own)]
         copies = started(moves, sems)
         waits = copies[:3], copies[3 : 3 + count], copies[3 + count : -2]
-        delta_kernel(waits, rate, gate, beta, quarters, 0, k_refs, v_refs, ends, resid, held, cumul, logs)
+        delta_kernel(waits, rate, gate, beta, quarters, 0, k_refs, v_refs, ends, work, marks)
         waited(copies[-2:])
 
-    vmem = pltpu.VMEM
+    vmem = pltpu.MemorySpace.VMEM
     outs = [(vmem, (2, DK, DV + DK), BF16)] * count
     outs += [(vmem, *shape) for shape in local_shapes(count, tokens, heads)]
-    outs += [(vmem, (1, heads), F32), (vmem, (heads, tokens), F32), (vmem, (heads, tokens), F32)]
-    outs += [(vmem, key_part, BF16), (vmem, value_part, BF16)]
-    outs = [(pltpu.MemorySpace.VMEM, *rest) for _, *rest in outs]
-    scratch = [vmem(key_part, BF16)] * count + [vmem(value_part, BF16)] * count
+    outs += [(vmem, a.shape, a.dtype) for a in (rate, gate_logit, beta_logit)]
+    outs += [(vmem, (tokens, DK), BF16), (vmem, (tokens, 2 * DV), BF16)]
+    groups = [(pltpu.SMEM, [code]), (pltpu.HBM, [rate, gate_logit, beta_logit, keys, values])]
+    scratch = [pltpu.VMEM((tokens, DK), BF16)] * count + [pltpu.VMEM((tokens, 2 * DV), BF16)] * count
     scratch += [pltpu.SemaphoreType.DMA((5 + 2 * count,))]
-    groups = [(pltpu.SMEM, [member]), (pltpu.HBM, [rate, keys, values, gate_logit, beta_logit])]
     result = call(kernel, "first_part", groups, outs, scratch, DELTA_VMEM, 6 * 10**9)
-    return result[:count], result[count : count + 4], result[count + 4 :]
-
-
-def second_part(member, operands, earlier):
+    return result[:count], result[count : count + 2], result[count + 2 :]
+
+
+def chunk_moves(first, chunks, sources, targets):
+    (q_hbm, k_hbm, work, marks), (q, k, work_to, marks_to) = sources, targets
+    rows = pl.ds(pl.multiple_of(first * CHUNK, CHUNK), chunks * CHUNK)
+    return [
+        (q_hbm.at[rows, :], q),
+        (k_hbm.at[rows, :], k),
+        (marks.at[:, rows], marks_to),
+        (work.at[:, pl.ds(first, chunks)], work_to),
+    ]
+
+
+def chunk_shapes(chunks, pairs, width):
+    tokens = chunks * CHUNK
+    return [((tokens, width), BF16)] * 2 + local_shapes(pairs - 1, tokens, 2 * pairs)
+
+
+def second_part(code, chunks, operands, earlier, query, keys):
     heads, tokens = operands[1].shape
-
-    def kernel(member_ref, rate, gate, beta, k_own, v_own, *refs):
-        earlier_refs, (ends,), out_hbm, local, sems = refs[:4], refs[4:5], refs[5:13], refs[13:17], refs[17]
-        copies = started(zip(earlier_refs, out_hbm[:4]), sems)
-        delta_kernel(
-            [[]] * 3, rate, gate, beta, [member_ref[0]], heads // 2 - 1, [k_own], [v_own], [ends], *local
-        )
-        copies += started(zip(local, out_hbm[4:]), sems, 4)
+    near = chunk_shapes(chunks, heads // 2, query.shape[1])
+
+    def kernel(code_ref, q_hbm, k_hbm, rate, gate, beta, k_own, v_own, *refs):
+        earlier_refs, (ends, *local), out_hbm, targets, sems = refs[:2], refs[2:5], refs[5:7], refs[7:11], refs[11]
+        moves = chunk_moves(code_ref[0] // (heads // 2), chunks, (q_hbm, k_hbm, *earlier_refs), targets)
+        copies = started([*moves, *zip(earlier_refs, out_hbm)], sems)
+        pair = jnp.bitwise_and(code_ref[0], heads // 2 - 1)
+        delta_kernel([[]] * 3, rate, gate, beta, [pair], heads // 2 - 1, [k_own], [v_own], [ends], *local)
         waited(copies)
 
-    shapes = local_shapes(1, tokens, heads)
-    outs = [(pltpu.MemorySpace.VMEM, (2, DK, DV + DK), BF16)]
+    vmem = pltpu.MemorySpace.VMEM
+    outs = [(vmem, (2, DK, DV + DK), BF16)] + [(vmem, *shape) for shape in local_shapes(1, tokens, heads)]
     outs += [(pltpu.MemorySpace.HBM, a.shape, a.dtype) for a in earlier]
-    outs += [(pltpu.MemorySpace.HBM, *shape) for shape in shapes]
-    scratch = [pltpu.VMEM(*shape) for shape in shapes] + [pltpu.SemaphoreType.DMA((8,))]
-    groups = [(pltpu.SMEM, [member]), (pltpu.VMEM, [*operands, *earlier])]
-    ends, *rest = call(kernel, "second_part", groups, outs, scratch, DELTA_VMEM, 2 * 10**9)
-    return ends, rest[:4], rest[4:]
-
-
-def third_part(place, turns, chunks, query, keys, earlier, own, after):
+    outs += [(vmem, *shape) for shape in near]
+    scratch = [pltpu.SemaphoreType.DMA((6,))]
+    groups = [(pltpu.SMEM, [code]), (pltpu.HBM, [query, keys]), (pltpu.VMEM, [*operands, *earlier])]
+    ends, work, marks, *rest = call(kernel, "second_part", groups, outs, scratch, DELTA_VMEM, 2 * 10**9)
+    return ends, [work, marks], rest[:2], rest[2:]
+
+
+def third_part(place, turns, chunks, sources, near, own, after):
     count = len(turns) + 1
     tokens = chunks * CHUNK
     heads = 2 * count
 
-    def kernel(place_ref, q_hbm, k_hbm, *refs):
-        sources, (_, out, gain), refs = refs[:8], refs[8:11], refs[11:]
-        q_refs, k_refs, local, sems = refs[:count], refs[count : 2 * count], refs[2 * count : -1], refs[-1]
+    def kernel(place_ref, *refs):
+        sources, (own_work, own_marks), (out, gain), scratch = refs[:4], refs[4:6], refs[7:9], refs[9:]
         first = place_ref[0] * chunks
-        rows = pl.ds(pl.multiple_of(first * CHUNK, CHUNK), tokens)
+        local, copies = sources, []
+        if not near:
+            local = scratch[:4]
+            copies = started(chunk_moves(first, chunks, sources, local), scratch[4])
+            waited(copies[:3])
+        q, k, work, marks = local
         quarters = [jnp.bitwise_xor(place_ref[2], turn) for turn in (*turns, 0)]
-        moves = []
-        for hbm, targets in ((q_hbm, q_refs), (k_hbm, k_refs)):
-            for quarter, ref in zip(quarters, targets):
-                moves.append((hbm.at[rows, pl.ds(pl.multiple_of(quarter * DK, DK), DK)], ref))
-        for i in (2, 3, 6, 7):
-            moves.append((sources[i].at[:, rows], local[i]))
-        for i in (0, 1, 4, 5):
-            moves.append((sources[i].at[:, pl.ds(first, chunks)], local[i]))
-        copies = started(moves, sems)
-        waited(copies[:-4])
+        q_refs = [pair_lanes(q, quarter, DK) for quarter in quarters]
+        k_refs = [pair_lanes(k, quarter, DK) for quarter in quarters]
+        own_here = own_marks[:, pl.ds(pl.multiple_of(first * CHUNK, CHUNK), tokens)]
         theirs = iota((heads, tokens), 0) < heads - 2
-        cumul = jnp.where(theirs, local[2][...], local[6][...])
-        logs = jnp.where(theirs, local[3][...], local[7][...])
-
-        def read(which):
-            return lambda c, a: local[which][a // 2, c, a % 2] if a < heads - 2 else local[which + 4][0, c, a % 2]
-
-        local_outputs(q_refs, k_refs, cumul, logs, copies[-4:], read(0), read(1), out, gain)
+        cumul = jnp.where(theirs, marks[:heads, :], own_here[:heads])
+        logs = jnp.where(theirs, marks[heads:, :], own_here[heads:])
+
+        def read(rows):
+            def block(c, a):
+                if a < heads - 2:
+                    return work[a // 2, c, a % 2, rows, :]
+                return own_work[0, first + c, a % 2, rows, :]
+
+            return block
+
+        resid, held = read(slice(0, CHUNK)), read(slice(CHUNK, CHUNK + DK))
+        local_outputs(q_refs, k_refs, cumul, logs, copies[3:], resid, held, out, gain)
 
     outs = [(pltpu.MemorySpace.VMEM, (tokens, heads * DV), BF16)] * 2
-    scratch = [pltpu.VMEM((tokens, DK), BF16)] * (2 * count)
-    for pairs in (count - 1, 1):
-        scratch += [pltpu.VMEM(*shape) for shape in local_shapes(pairs, tokens, heads)]
-    scratch += [pltpu.SemaphoreType.DMA((2 * count + 8,))]
-    groups = [(pltpu.SMEM, [place]), (pltpu.HBM, [query, keys, *earlier, *own, after])]
+    scratch = []
+    if not near:
+        scratch = [pltpu.VMEM(*shape) for shape in chunk_shapes(chunks, count, sources[0].shape[1])]
+        scratch += [pltpu.SemaphoreType.DMA((4,))]
+    groups = [(pltpu.SMEM, [place]), (pltpu.VMEM if near else pltpu.HBM, sources), (pltpu.VMEM, own)]
+    groups += [(pltpu.HBM, [after])]
     return call(kernel, "third_part", groups, outs, scratch, OUTPUT_VMEM, 3 * 10**9)
 
 
@@ -621,20 +632,20 @@
     member = member_at.reshape(1)
     rate, norm_gain = decay_rate.reshape(1, -1), norm_gain.reshape(1, -1)
 
-    away, earlier, operands = first_part(member, turns, rate, keys, values, gate_logit.T, beta_logit.T)
-    others = [lax.ppermute(a, "seq", pairs[turn]) for a, turn in zip(away, turns)]
-    own, earlier, mine = second_part(member, operands, earlier)
     groups = shards // members
-    order, ending, *total = group_part(member, turns, own, others, groups > 2)
-
     chips = cores // 2
     chip, core = head // 2, lax.rem(head, 2)
     rows = query.shape[0] // chips
     spots = [jnp.stack([lax.rem(chip + by, chips), core, member_at]) for by in range(chips)]
     apart = rows == CHUNK and chips == 2
     chunks = 1 if apart else query.shape[0] // CHUNK
-    spot = spots[1] if apart else jnp.zeros_like(spots[0]).at[2].set(member_at)
-    out, gain = third_part(spot, turns, chunks, query, keys, earlier, mine, ending)
+    code = (member_at + members * lax.rem(chip + 1, chips)).reshape(1) if apart else member
+    spot = spots[1] if apart else jnp.stack([jnp.zeros_like(core), core, member_at])
+    away, earlier, operands = first_part(code, turns, rate, keys, values, gate_logit.T, beta_logit.T)
+    others = [lax.ppermute(a, "seq", pairs[turn]) for a, turn in zip(away, turns)]
+    own, mine, locals_, near = second_part(code, chunks, operands, earlier, query, keys)
+    order, ending, *total = group_part(member, turns, own, others, groups > 2)
+    out, gain = third_part(spot, turns, chunks, near, True, mine, ending)
 
     came = []
     for step in range(groups - 1):
@@ -659,7 +670,7 @@
     if arrived:
         spot, both = lax.optimization_barrier((spot, both))
     if apart:
-        out, gain = third_part(spot, turns, chunks, query, keys, earlier, mine, ending)
+        out, gain = third_part(spot, turns, chunks, [query, keys, *locals_], False, mine, ending)
     *gives, stay = whole_part(spot, turns, rows, gate_z, out_weight, norm_gain, out, gain, [*back, keep])
     total = stay + jnp.concatenate([lax.ppermute(g, "head", swap) for g in gives], axis=1).astype(F32)
     for part in arrived:

time: 54.4 us -> 53.4 us (0.982)
  Pallas kernels: 30.2 us -> 27.7 us
  waiting for transfers between devices: 7.5 us -> 8.72 us
    pallas_call x9, Pallas kernels: 30.2 us -> 27.7 us  [call(): pl.pallas_call(kernel, in_specs=specs, out_specs=[pl.BlockSpec(memory_spa...]
    ppermute x3, waiting for transfers between devices: 0.88 us -> 1.53 us  [on_device(): lax.ppermute(a, 'seq', pairs[turn])]
  transfers between devices with their start and end apart: 11 -> 11, of which waited for: 7 -> 8; matrix products, arithmetic and copies ran while one was open for 0% -> 0% of each run, Pallas kernels for 36% -> 32%
where the time goes in v6:
time: 53.4 us; the launch traced here: 53.2 us
  Pallas kernels  27.7 us (52%)
  starting transfers between devices  15.3 us (29%)
  waiting for transfers between devices  8.72 us (16%)
  other arithmetic  1.25 us (2%)
    pallas_call x9, Pallas kernels, call(): pl.pallas_call(kernel, in_specs=specs, out_specs=[pl.BlockSpec(memory_spa...  27.7 us
    ppermute x3, starting transfers between devices, on_device(): lax.ppermute(a, 'seq', pairs[turn])  4.69 us
    ppermute x1, starting transfers between devices, on_device(): came.append(lax.ppermute(ending, 'seq', along))  4.69 us
    ppermute x3, starting transfers between devices, on_device(): lax.ppermute(g, 'seq', pairs[turn])  3.78 us
    ppermute x1, waiting for transfers between devices, on_device(): lax.ppermute(both, 'head', [(i, (i + 2 * by) % cores) for i in range(core...  2.74 us
    ppermute x1, waiting for transfers between devices, on_device(): both = (stay + lax.ppermute(give, 'head', swap).astype(F32)).astype(BF16)  1.81 us
    ppermute x1, starting transfers between devices, on_device(): lax.ppermute(both, 'head', [(i, (i + 2 * by) % cores) for i in range(core...  1.55 us
    ppermute x3, waiting for transfers between devices, on_device(): lax.ppermute(a, 'seq', pairs[turn])  1.53 us
  transfers between devices with their start and end apart: 11, of which 8 were waited for; matrix products, arithmetic and copies ran while one was open for 0% of the time, Pallas kernels for 32%

profile of v6, /device:TPU:0, one launch (start us, length us, event | category | flops | bytes accessed | tf_op | source)
XLA Modules:
  0.0 53.2 jit_solution(7127228920430396043)
XLA Ops:
  0.0 8.0 %first_part.1 = (bf16[2,128,256]{2,1,0:T(8,128)(2,1)S(1)}, bf16[2,128,256]{2,1,0:T(8,128)(2,1)S(1)}, bf16[2,128,256]{2,1,0:T(8,128)(2,1)S(1)}, bf16[3,2,2,384,25...) custom-call(s32[1]{0:T(128)} %bitcast.5.code_ref, ...), custom_call_target="tpu_custom_call" | custom-call | flops 6000000000 | bytes 1048576 | tf_op jit(solution)/shard_map/first_part/pallas_call | solution.py:287
  8.1 4.0 %collective-permute-start = (bf16[2,128,256]{2,1,0:T(8,128)(2,1)S(1)}, bf16[2,128,256]{2,1,0:T(8,128)(2,1)S(1)}, u32[]{:S(2)}, u32[]{:S(2)}) collective-permute-start(bf16[2,128,256]{2,1,0:T(8,128)(2,1)S(1)} %get-tuple-element.57), channel_id=1, source_target_pairs={{0,12},{4,8},{8,4},{12,0},{16,28},{20,24},{24,20},{28,16},{1,13},{... | collective-permute-start | bytes 393224 | tf_op jit(solution)/shard_map/ppermute | solution.py:645
  12.1 0.5 collective-permute-start.1
  12.6 0.1 collective-permute-start.2
  12.7 4.2 %second_part.1 = (bf16[2,128,256]{2,1,0:T(8,128)(2,1)S(1)}, bf16[1,2,2,384,256]{4,3,2,1,0:T(8,128)(2,1)S(1)}, f32[16,512]{1,0:T(8,128)S(1)}, bf16[3,2,2,384,256]...) custom-call(s32[1]{0:T(128)} %bitcast.5.code_ref, ...), custom_call_target="tpu_custom_call" | custom-call | flops 2000000000 | bytes 1048576 | tf_op jit(solution)/shard_map/second_part/pallas_call | solution.py:287
  17.0 0.1 add_add_fusion.1.place_ref
  17.1 0.0 collective-permute-done.refs_0_
  17.1 1.4 %collective-permute-done.1.refs_1_ = bf16[2,128,256]{2,1,0:T(8,128)(2,1)S(1)} collective-permute-done((bf16[2,128,256]{2,1,0:T(8,128)(2,1)S(1)}, bf16[2,128,256]{2,1,0:T(8,128)(2,1)S(1)}, u32[]{:S(2)}, u32[]{:S(2)}) %collective-permute-start.1) | collective-permute-done | bytes 131104 | tf_op jit(solution)/shard_map/ppermute | solution.py:645
  18.4 0.2 collective-permute-done.2.refs_2_
  18.6 0.5 group_part.1
  19.1 0.0 copy-start
  19.1 4.7 %collective-permute-start.3 = (bf16[2,128,128]{2,1,0:T(8,128)(2,1)S(1)}, bf16[2,128,128]{2,1,0:T(8,128)(2,1)S(1)}, u32[]{:S(2)}, u32[]{:S(2)}) collective-permute-start(bf16[2,128,128]{2,1,0:T(8,128)(2,1)S(1)} %get-tuple-element.60.refs_6_), channel_id=1, source_target_pairs={{0,16},{4,20},{8,24},{12,28},{1,17},{5,21},{9,25},{13,29},{2,18},{... | collective-permute-start | bytes 196616 | tf_op jit(solution)/shard_map/ppermute | solution.py:656
  23.8 0.0 copy-done
  23.8 1.9 %third_part.2 = (bf16[256,1024]{1,0:T(8,128)(2,1)S(1)}, bf16[256,1024]{1,0:T(8,128)(2,1)S(1)}) custom-call(s32[3]{0:T(128)S(1)} %add_add_fusion.1.place_ref, bf16[256,512]{1,0:T(8,128)(2,1)S(1)} %get-tuple-element.50.refs_0_, bf16[256,512]{1,0:T(8,128)(2,1)S(1)} %get-tuple-element.51.refs_1_, bf16[3,1,2,384,256]{4,3,2,1,0:T(8,128)(2,1)S(1)} %get-tuple-element.52.refs_2_, ...), custom_call_target="tpu_custom_call" | custom-call | flops 3000000000 | bytes 1048576 | tf_op jit(solution)/shard_map/third_part/pallas_call | solution.py:287
  25.6 0.0 collective-permute-done.3.refs_0_
  25.6 0.5 starts_part.1
  26.1 2.6 %collective-permute-start.4 = (bf16[2,128,128]{2,1,0:T(8,128)(2,1)S(1)}, bf16[2,128,128]{2,1,0:T(8,128)(2,1)S(1)}, u32[]{:S(2)}, u32[]{:S(2)}) collective-permute-start(bf16[2,128,128]{2,1,0:T(8,128)(2,1)S(1)} %get-tuple-element.68), channel_id=1, source_target_pairs={{0,12},{4,8},{8,4},{12,0},{16,28},{20,24},{24,20},{28,16},{1,13},{... | collective-permute-start | bytes 196616 | tf_op jit(solution)/shard_map/ppermute | solution.py:660
  28.7 1.2 %collective-permute-start.5 = (bf16[2,128,128]{2,1,0:T(8,128)(2,1)S(1)}, bf16[2,128,128]{2,1,0:T(8,128)(2,1)S(1)}, u32[]{:S(2)}, u32[]{:S(2)}) collective-permute-start(bf16[2,128,128]{2,1,0:T(8,128)(2,1)S(1)} %get-tuple-element.69), channel_id=1, source_target_pairs={{0,4},{4,0},{8,12},{12,8},{16,20},{20,16},{24,28},{28,24},{1,5},{5... | collective-permute-start | bytes 196616 | tf_op jit(solution)/shard_map/ppermute | solution.py:660
  29.9 0.0 collective-permute-start.6
  29.9 3.0 %keep_part.1 = (f32[256,2048]{1,0:T(8,128)S(1)}, f32[256,768]{1,0:T(8,128)S(1)}, bf16[768,2048]{1,0:T(8,128)(2,1)S(1)}) custom-call(s32[3]{0:T(128)S(1)} %add_add_fusion.1.place_ref, bf16[512,1024]{1,0:T(8,128)(2,1)} %z_hbm.3, bf16[1024,2048]{1,0:T(8,128)(2,1)} %w_hbm.3, f32[1,128]{1,0:T(1,128)} %bitcast.9, ...), custom_call_target="tpu_custom_call" | custom-call | flops 268435456 | bytes 1048576 | tf_op jit(solution)/shard_map/keep_part/pallas_call | solution.py:287
  32.9 0.0 collective-permute-done.4.refs_0_
  32.9 0.1 collective-permute-done.5.refs_1_
  33.0 1.2 %collective-permute-done.6.refs_2_ = bf16[2,128,128]{2,1,0:T(8,128)(2,1)S(1)} collective-permute-done((bf16[2,128,128]{2,1,0:T(8,128)(2,1)S(1)}, bf16[2,128,128]{2,1,0:T(8,128)(2,1)S(1)}, u32[]{:S(2)}, u32[]{:S(2)}) %collective-permute-start.6) | collective-permute-done | bytes 65568 | tf_op jit(solution)/shard_map/ppermute | solution.py:660
  34.2 1.9 %away_part.1 = (bf16[128,2048]{1,0:T(8,128)(2,1)S(1)}, f32[128,2048]{1,0:T(8,128)S(1)}) custom-call(s32[3]{0:T(128)S(1)} %add_add_fusion.1.place_ref, f32[256,2048]{1,0:T(8,128)S(1)} %get-tuple-element.65.sum_ref, f32[256,768]{1,0:T(8,128)S(1)} %get-tuple-element.66.gate, bf16[768,2048]{1,0:T(8,128)(2,1)S(1)} %get-tuple-element.67.w, ...), custom_call_target="tpu_custom_call" | custom-call | flops 805306368 | bytes 1048576 | tf_op jit(solution)/shard_map/away_part/pallas_call | solution.py:287
  36.1 0.1 collective-permute-start.7
  36.2 0.1 add_add_fusion.place_ref
  36.2 1.8 %collective-permute-done.7 = bf16[128,2048]{1,0:T(8,128)(2,1)S(1)} collective-permute-done((bf16[128,2048]{1,0:T(8,128)(2,1)S(1)}, bf16[128,2048]{1,0:T(8,128)(2,1)S(1)}, u32[]{:S(2)}, u32[]{:S(2)}) %collective-permute-start.7) | collective-permute-done | bytes 524320 | tf_op jit(solution)/shard_map/ppermute | solution.py:667
  38.0 0.1 add_convert_fusion.1
  38.2 1.6 %collective-permute-start.10 = (bf16[128,2048]{1,0:T(8,128)(2,1)S(1)}, bf16[128,2048]{1,0:T(8,128)(2,1)S(1)}, u32[]{:S(2)}, u32[]{:S(2)}) collective-permute-start(bf16[128,2048]{1,0:T(8,128)(2,1)S(1)} %add_convert_fusion.1), channel_id=1, source_target_pairs={{0,2},{1,3},{2,0},{3,1},{4,6},{5,7},{6,4},{7,5},{8,10},{9,11},{10,... | collective-permute-start | bytes 1572872 | tf_op jit(solution)/shard_map/ppermute | solution.py:668
  39.7 3.4 %third_part.3 = (bf16[256,1024]{1,0:T(8,128)(2,1)S(1)}, bf16[256,1024]{1,0:T(8,128)(2,1)S(1)}) custom-call(s32[3]{0:T(128)S(1)} %add_add_fusion.place_ref, bf16[512,512]{1,0:T(8,128)(2,1)} %refs_0_.1, bf16[512,512]{1,0:T(8,128)(2,1)} %refs_1_.1, bf16[3,2,2,384,256]{4,3,2,1,0:T(8,128)(2,1)} %get-tuple-element.74.refs_2_, ...), custom_call_target="tpu_custom_call" | custom-call | flops 3000000000 | bytes 1048576 | tf_op jit(solution)/shard_map/third_part/pallas_call | solution.py:287
  43.1 4.3 %whole_part.1 = (bf16[128,1024]{1,0:T(8,128)(2,1)S(1)}, bf16[128,1024]{1,0:T(8,128)(2,1)S(1)}, f32[128,2048]{1,0:T(8,128)S(1)}) custom-call(s32[3]{0:T(128)S(1)} %add_add_fusion.place_ref, bf16[512,1024]{1,0:T(8,128)(2,1)} %z_hbm.3, bf16[1024,2048]{1,0:T(8,128)(2,1)} %w_hbm.3, f32[1,128]{1,0:T(1,128)} %bitcast.10, ...), custom_call_target="tpu_custom_call" | custom-call | flops 1073741824 | bytes 1048576 | tf_op jit(solution)/shard_map/whole_part/pallas_call | solution.py:287
  47.5 0.1 collective-permute-start.8
  47.5 0.5 collective-permute-start.9
  48.0 1.0 %collective-permute-done.8 = bf16[128,1024]{1,0:T(8,128)(2,1)S(1)} collective-permute-done((bf16[128,1024]{1,0:T(8,128)(2,1)S(1)}, bf16[128,1024]{1,0:T(8,128)(2,1)S(1)}, u32[]{:S(2)}, u32[]{:S(2)}) %collective-permute-start.8) | collective-permute-done | bytes 262176 | tf_op jit(solution)/shard_map/ppermute | solution.py:675
  49.1 0.4 collective-permute-done.9
  49.4 2.7 %collective-permute-done.10 = bf16[128,2048]{1,0:T(8,128)(2,1)S(1)} collective-permute-done((bf16[128,2048]{1,0:T(8,128)(2,1)S(1)}, bf16[128,2048]{1,0:T(8,128)(2,1)S(1)}, u32[]{:S(2)}, u32[]{:S(2)}) %collective-permute-start.10) | collective-permute-done | bytes 524320 | tf_op jit(solution)/shard_map/ppermute | solution.py:668
  52.2 1.0 %add_convert_fusion = bf16[128,2048]{1,0:T(8,128)(2,1)} fusion(bf16[128,2048]{1,0:T(8,128)(2,1)S(1)} %collective-permute-done.10, f32[128,2048]{1,0:T(8,128)S(1)} %get-tuple-element.78, bf16[128,1024]{1,0:T(8,128)(2,1)S(1)} %collective-permute-done.9, bf16[128,1024]{1,0:T(8,128)(2,1)S(1)} %collective-permute-done.8), kind=kLoop, calls=%fused_computation | loop fusion | flops 2097152 | bytes 2621440 | tf_op jit(solution)/shard_map/convert_element_type | solution.py:678
Async XLA Ops:
  8.1 9.0 %collective-permute-start = (bf16[2,128,256]{2,1,0:T(8,128)(2,1)S(1)}, bf16[2,128,256]{2,1,0:T(8,128)(2,1)S(1)}, u32[]{:S(2)}, u32[]{:S(2)}) collective-permute-start(bf16[2,128,256]{2,1,0:T(8,128)(2,1)S(1)} %get-tuple-element.57), channel_id=1, source_target_pairs={{0,12},{4,8},{8,4},{12,0},{16,28},{20,24},{24,20},{28,16},{1,13},{... | collective-permute-start | bytes 393224 | tf_op jit(solution)/shard_map/ppermute | solution.py:645
  12.1 6.3 %collective-permute-start.1 = (bf16[2,128,256]{2,1,0:T(8,128)(2,1)S(1)}, bf16[2,128,256]{2,1,0:T(8,128)(2,1)S(1)}, u32[]{:S(2)}, u32[]{:S(2)}) collective-permute-start(bf16[2,128,256]{2,1,0:T(8,128)(2,1)S(1)} %get-tuple-element.58), channel_id=1, source_target_pairs={{0,4},{4,0},{8,12},{12,8},{16,20},{20,16},{24,28},{28,24},{1,5},{5... | collective-permute-start | bytes 393224 | tf_op jit(solution)/shard_map/ppermute | solution.py:645
  12.6 6.0 %collective-permute-start.2 = (bf16[2,128,256]{2,1,0:T(8,128)(2,1)S(1)}, bf16[2,128,256]{2,1,0:T(8,128)(2,1)S(1)}, u32[]{:S(2)}, u32[]{:S(2)}) collective-permute-start(bf16[2,128,256]{2,1,0:T(8,128)(2,1)S(1)} %get-tuple-element.59), channel_id=1, source_target_pairs={{0,8},{4,12},{8,0},{12,4},{16,24},{20,28},{24,16},{28,20},{1,9},{5... | collective-permute-start | bytes 393224 | tf_op jit(solution)/shard_map/ppermute | solution.py:645
  19.1 4.7 %copy-start = (bf16[2,128,128]{2,1,0:T(8,128)(2,1)}, bf16[2,128,128]{2,1,0:T(8,128)(2,1)S(1)}, u32[]{:S(2)}) copy-start(bf16[2,128,128]{2,1,0:T(8,128)(2,1)S(1)} %get-tuple-element.60.refs_6_) | copy-start | bytes 196612
  19.1 6.6 %collective-permute-start.3 = (bf16[2,128,128]{2,1,0:T(8,128)(2,1)S(1)}, bf16[2,128,128]{2,1,0:T(8,128)(2,1)S(1)}, u32[]{:S(2)}, u32[]{:S(2)}) collective-permute-start(bf16[2,128,128]{2,1,0:T(8,128)(2,1)S(1)} %get-tuple-element.60.refs_6_), channel_id=1, source_target_pairs={{0,16},{4,20},{8,24},{12,28},{1,17},{5,21},{9,25},{13,29},{2,18},{... | collective-permute-start | bytes 196616 | tf_op jit(solution)/shard_map/ppermute | solution.py:656
  26.1 6.8 %collective-permute-start.4 = (bf16[2,128,128]{2,1,0:T(8,128)(2,1)S(1)}, bf16[2,128,128]{2,1,0:T(8,128)(2,1)S(1)}, u32[]{:S(2)}, u32[]{:S(2)}) collective-permute-start(bf16[2,128,128]{2,1,0:T(8,128)(2,1)S(1)} %get-tuple-element.68), channel_id=1, source_target_pairs={{0,12},{4,8},{8,4},{12,0},{16,28},{20,24},{24,20},{28,16},{1,13},{... | collective-permute-start | bytes 196616 | tf_op jit(solution)/shard_map/ppermute | solution.py:660
  28.7 4.3 %collective-permute-start.5 = (bf16[2,128,128]{2,1,0:T(8,128)(2,1)S(1)}, bf16[2,128,128]{2,1,0:T(8,128)(2,1)S(1)}, u32[]{:S(2)}, u32[]{:S(2)}) collective-permute-start(bf16[2,128,128]{2,1,0:T(8,128)(2,1)S(1)} %get-tuple-element.69), channel_id=1, source_target_pairs={{0,4},{4,0},{8,12},{12,8},{16,20},{20,16},{24,28},{28,24},{1,5},{5... | collective-permute-start | bytes 196616 | tf_op jit(solution)/shard_map/ppermute | solution.py:660
  29.9 4.3 %collective-permute-start.6 = (bf16[2,128,128]{2,1,0:T(8,128)(2,1)S(1)}, bf16[2,128,128]{2,1,0:T(8,128)(2,1)S(1)}, u32[]{:S(2)}, u32[]{:S(2)}) collective-permute-start(bf16[2,128,128]{2,1,0:T(8,128)(2,1)S(1)} %get-tuple-element.70), channel_id=1, source_target_pairs={{0,8},{4,12},{8,0},{12,4},{16,24},{20,28},{24,16},{28,20},{1,9},{5... | collective-permute-start | bytes 196616 | tf_op jit(solution)/shard_map/ppermute | solution.py:660
  36.1 2.0 %collective-permute-start.7 = (bf16[128,2048]{1,0:T(8,128)(2,1)S(1)}, bf16[128,2048]{1,0:T(8,128)(2,1)S(1)}, u32[]{:S(2)}, u32[]{:S(2)}) collective-permute-start(bf16[128,2048]{1,0:T(8,128)(2,1)S(1)} %get-tuple-element.72), channel_id=1, source_target_pairs={{0,1},{1,0},{2,3},{3,2},{4,5},{5,4},{6,7},{7,6},{8,9},{9,8},{10,11... | collective-permute-start | bytes 1572872 | tf_op jit(solution)/shard_map/ppermute | solution.py:667
  38.2 14.0 %collective-permute-start.10 = (bf16[128,2048]{1,0:T(8,128)(2,1)S(1)}, bf16[128,2048]{1,0:T(8,128)(2,1)S(1)}, u32[]{:S(2)}, u32[]{:S(2)}) collective-permute-start(bf16[128,2048]{1,0:T(8,128)(2,1)S(1)} %add_convert_fusion.1), channel_id=1, source_target_pairs={{0,2},{1,3},{2,0},{3,1},{4,6},{5,7},{6,4},{7,5},{8,10},{9,11},{10,... | collective-permute-start | bytes 1572872 | tf_op jit(solution)/shard_map/ppermute | solution.py:668
  47.5 1.6 %collective-permute-start.8 = (bf16[128,1024]{1,0:T(8,128)(2,1)S(1)}, bf16[128,1024]{1,0:T(8,128)(2,1)S(1)}, u32[]{:S(2)}, u32[]{:S(2)}) collective-permute-start(bf16[128,1024]{1,0:T(8,128)(2,1)S(1)} %get-tuple-element.79), channel_id=1, source_target_pairs={{0,1},{1,0},{2,3},{3,2},{4,5},{5,4},{6,7},{7,6},{8,9},{9,8},{10,11... | collective-permute-start | bytes 786440 | tf_op jit(solution)/shard_map/ppermute | solution.py:675
  47.5 1.9 %collective-permute-start.9 = (bf16[128,1024]{1,0:T(8,128)(2,1)S(1)}, bf16[128,1024]{1,0:T(8,128)(2,1)S(1)}, u32[]{:S(2)}, u32[]{:S(2)}) collective-permute-start(bf16[128,1024]{1,0:T(8,128)(2,1)S(1)} %get-tuple-element.80), channel_id=1, source_target_pairs={{0,1},{1,0},{2,3},{3,2},{4,5},{5,4},{6,7},{7,6},{8,9},{9,8},{10,11... | collective-permute-start | bytes 786440 | tf_op jit(solution)/shard_map/ppermute | solution.py:675

commit v7 on v6

--- a/solution.py
+++ b/solution.py
@@ -335,6 +335,15 @@
     return result[:count], result[count : count + 2], result[count + 2 :]
 
 
+def place_code(chip, core, member, members):
+    return ((chip * 2 + core) * members + member).reshape(1)
+
+
+def place_of(code_ref, members):
+    code = code_ref[0]
+    return code // (2 * members), jnp.bitwise_and(code // members, 1), jnp.bitwise_and(code, members - 1)
+
+
 def chunk_moves(first, chunks, sources, targets):
     (q_hbm, k_hbm, work, marks), (q, k, work_to, marks_to) = sources, targets
     rows = pl.ds(pl.multiple_of(first * CHUNK, CHUNK), chunks * CHUNK)
@@ -378,7 +387,8 @@
     tokens = chunks * CHUNK
     heads = 2 * count
 
-    def kernel(place_ref, *refs):
+    def kernel(code_ref, *refs):
+        place_ref = place_of(code_ref, count)
         sources, (own_work, own_marks), (out, gain), scratch = refs[:4], refs[4:6], refs[7:9], refs[9:]
         first = place_ref[0] * chunks
         local, copies = sources, []
@@ -549,7 +559,8 @@
     wide = weight.shape[1]
     count = len(turns)
 
-    def kernel(place_ref, z_hbm, w_hbm, norm_hbm, out, gain, start_ref, sum_ref, gate_ref, w_away, *refs):
+    def kernel(code_ref, z_hbm, w_hbm, norm_hbm, out, gain, start_ref, sum_ref, gate_ref, w_away, *refs):
+        place_ref = place_of(code_ref, count + 1)
         norm, own_gate, z_away, z_own, w_own, sems = refs
         moves = [(norm_hbm, norm)] + pair_moves(place_ref, [0], z_hbm, w_hbm, z_own, w_own)
         copies = started(moves + pair_moves(place_ref, turns, z_hbm, w_hbm, z_away, w_away), sems)
@@ -578,7 +589,8 @@
 def away_part(place, kept, out, gain, starts):
     rows, wide = kept[0].shape
 
-    def kernel(place_ref, sum_ref, gate, w, out, gain, *refs):
+    def kernel(code_ref, sum_ref, gate, w, out, gain, *refs):
+        place_ref = place_of(code_ref, len(starts) + 1)
         start_refs, (send_ref, stay_ref) = refs[:-2], refs[-2:]
         pairs = gated_pairs(out, gain, gate, core_rows(place_ref, rows, out), 0, start_refs)
         partial = projected(pairs, w) + sum_ref[...]
@@ -595,7 +607,8 @@
     wide = weight.shape[1]
     count = len(turns) + 1
 
-    def kernel(place_ref, z_hbm, w_hbm, norm_hbm, out, gain, *refs):
+    def kernel(code_ref, z_hbm, w_hbm, norm_hbm, out, gain, *refs):
+        place_ref = place_of(code_ref, count)
         start_refs, sends, (stay_ref, norm, gate, z, w, sems) = refs[:count], refs[count : count + 2], refs[count + 2 :]
         moves = [(norm_hbm, norm)] + pair_moves(place_ref, (*turns, 0), z_hbm, w_hbm, z, w)
         copies = started(moves, sems)
@@ -636,11 +649,12 @@
     chips = cores // 2
     chip, core = head // 2, lax.rem(head, 2)
     rows = query.shape[0] // chips
-    spots = [jnp.stack([lax.rem(chip + by, chips), core, member_at]) for by in range(chips)]
+    spots = [place_code(lax.rem(chip + by, chips), core, member_at, members) for by in range(chips)]
     apart = rows == CHUNK and chips == 2
     chunks = 1 if apart else query.shape[0] // CHUNK
     code = (member_at + members * lax.rem(chip + 1, chips)).reshape(1) if apart else member
-    spot = spots[1] if apart else jnp.stack([jnp.zeros_like(core), core, member_at])
+    spot = spots[1] if apart else place_code(0, core, member_at, members)
+    code, member, spot, *spots = lax.optimization_barrier((code, member, spot, *spots))
     away, earlier, operands = first_part(code, turns, rate, keys, values, gate_logit.T, beta_logit.T)
     others = [lax.ppermute(a, "seq", pairs[turn]) for a, turn in zip(away, turns)]
     own, mine, locals_, near = second_part(code, chunks, operands, earlier, query, keys)

time: 53.4 us -> 52.8 us (0.989)
  Pallas kernels: 27.7 us -> 25 us
  waiting for transfers between devices: 8.72 us -> 10.9 us
    pallas_call x9, Pallas kernels: 27.7 us -> 25 us  [call(): pl.pallas_call(kernel, in_specs=specs, out_specs=[pl.BlockSpec(memory_spa...]
    ppermute x1, waiting for transfers between devices: 2.74 us -> 3.84 us  [on_device(): lax.ppermute(both, 'head', [(i, (i + 2 * by) % cores) for i in range(core...]
    ppermute x3, waiting for transfers between devices: 1.24 us -> 1.78 us  [on_device(): lax.ppermute(g, 'seq', pairs[turn])]
  transfers between devices with their start and end apart: 11 -> 11, of which waited for: 8 -> 9; matrix products, arithmetic and copies ran while one was open for 0% -> 0% of each run, Pallas kernels for 32% -> 28%
where the time goes in v7:
time: 52.8 us; the launch traced here: 52.6 us
  Pallas kernels  25 us (47%)
  starting transfers between devices  15.5 us (29%)
  waiting for transfers between devices  10.9 us (21%)
  other arithmetic  1.09 us (2%)
    pallas_call x9, Pallas kernels, call(): pl.pallas_call(kernel, in_specs=specs, out_specs=[pl.BlockSpec(memory_spa...  25 us
    ppermute x3, starting transfers between devices, on_device(): lax.ppermute(a, 'seq', pairs[turn])  4.69 us
    ppermute x1, starting transfers between devices, on_device(): came.append(lax.ppermute(ending, 'seq', along))  4.69 us
    ppermute x3, starting transfers between devices, on_device(): lax.ppermute(g, 'seq', pairs[turn])  3.97 us
    ppermute x1, waiting for transfers between devices, on_device(): lax.ppermute(both, 'head', [(i, (i + 2 * by) % cores) for i in range(core...  3.84 us
    ppermute x1, waiting for transfers between devices, on_device(): both = (stay + lax.ppermute(give, 'head', swap).astype(F32)).astype(BF16)  1.9 us
    ppermute x3, waiting for transfers between devices, on_device(): lax.ppermute(g, 'seq', pairs[turn])  1.78 us
    ppermute x3, waiting for transfers between devices, on_device(): lax.ppermute(a, 'seq', pairs[turn])  1.6 us
  transfers between devices with their start and end apart: 11, of which 9 were waited for; matrix products, arithmetic and copies ran while one was open for 0% of the time, Pallas kernels for 28%

profile of v7, /device:TPU:0, one launch (start us, length us, event | category | flops | bytes accessed | tf_op | source)
XLA Modules:
  0.0 52.6 jit_solution(13246977913080522520)
XLA Ops:
  0.0 8.0 %first_part.1 = (bf16[2,128,256]{2,1,0:T(8,128)(2,1)S(1)}, bf16[2,128,256]{2,1,0:T(8,128)(2,1)S(1)}, bf16[2,128,256]{2,1,0:T(8,128)(2,1)S(1)}, bf16[3,2,2,384,25...) custom-call(s32[1]{0:T(128)} %bitcast.code_ref, ...), custom_call_target="tpu_custom_call" | custom-call | flops 6000000000 | bytes 1048576 | tf_op jit(solution)/shard_map/first_part/pallas_call | solution.py:287
  8.1 4.0 %collective-permute-start = (bf16[2,128,256]{2,1,0:T(8,128)(2,1)S(1)}, bf16[2,128,256]{2,1,0:T(8,128)(2,1)S(1)}, u32[]{:S(2)}, u32[]{:S(2)}) collective-permute-start(bf16[2,128,256]{2,1,0:T(8,128)(2,1)S(1)} %get-tuple-element.67), channel_id=1, source_target_pairs={{0,12},{4,8},{8,4},{12,0},{16,28},{20,24},{24,20},{28,16},{1,13},{... | collective-permute-start | bytes 393224 | tf_op jit(solution)/shard_map/ppermute | solution.py:659
  12.1 0.5 collective-permute-start.1
  12.6 0.1 collective-permute-start.2
  12.7 4.2 %second_part.1 = (bf16[2,128,256]{2,1,0:T(8,128)(2,1)S(1)}, bf16[1,2,2,384,256]{4,3,2,1,0:T(8,128)(2,1)S(1)}, f32[16,512]{1,0:T(8,128)S(1)}, bf16[3,2,2,384,256]...) custom-call(s32[1]{0:T(128)} %bitcast.code_ref, ...), custom_call_target="tpu_custom_call" | custom-call | flops 2000000000 | bytes 1048576 | tf_op jit(solution)/shard_map/second_part/pallas_call | solution.py:287
  17.0 0.0 collective-permute-done.refs_0_
  17.0 1.4 %collective-permute-done.1.refs_1_ = bf16[2,128,256]{2,1,0:T(8,128)(2,1)S(1)} collective-permute-done((bf16[2,128,256]{2,1,0:T(8,128)(2,1)S(1)}, bf16[2,128,256]{2,1,0:T(8,128)(2,1)S(1)}, u32[]{:S(2)}, u32[]{:S(2)}) %collective-permute-start.1) | collective-permute-done | bytes 131104 | tf_op jit(solution)/shard_map/ppermute | solution.py:659
  18.4 0.2 collective-permute-done.2.refs_2_
  18.6 0.5 group_part.1
  19.1 0.0 copy-start
  19.1 4.7 %collective-permute-start.3 = (bf16[2,128,128]{2,1,0:T(8,128)(2,1)S(1)}, bf16[2,128,128]{2,1,0:T(8,128)(2,1)S(1)}, u32[]{:S(2)}, u32[]{:S(2)}) collective-permute-start(bf16[2,128,128]{2,1,0:T(8,128)(2,1)S(1)} %get-tuple-element.70.refs_6_), channel_id=1, source_target_pairs={{0,16},{4,20},{8,24},{12,28},{1,17},{5,21},{9,25},{13,29},{2,18},{... | collective-permute-start | bytes 196616 | tf_op jit(solution)/shard_map/ppermute | solution.py:670
  23.8 0.0 copy-done
  23.8 1.3 %third_part.2 = (bf16[256,1024]{1,0:T(8,128)(2,1)S(1)}, bf16[256,1024]{1,0:T(8,128)(2,1)S(1)}) custom-call(s32[1]{0:T(128)} %bitcast.2.code_ref, bf16[256,512]{1,0:T(8,128)(2,1)S(1)} %get-tuple-element.59.refs_0_, bf16[256,512]{1,0:T(8,128)(2,1)S(1)} %get-tuple-element.60.refs_1_, bf16[3,1,2,384,256]{4,3,2,1,0:T(8,128)(2,1)S(1)} %get-tuple-element.61.refs_2_, ...), custom_call_target="tpu_custom_call" | custom-call | flops 3000000000 | bytes 1048576 | tf_op jit(solution)/shard_map/third_part/pallas_call | solution.py:287
  25.1 0.4 collective-permute-done.3.refs_0_
  25.5 0.5 starts_part.1
  25.9 2.8 %collective-permute-start.4 = (bf16[2,128,128]{2,1,0:T(8,128)(2,1)S(1)}, bf16[2,128,128]{2,1,0:T(8,128)(2,1)S(1)}, u32[]{:S(2)}, u32[]{:S(2)}) collective-permute-start(bf16[2,128,128]{2,1,0:T(8,128)(2,1)S(1)} %get-tuple-element.78), channel_id=1, source_target_pairs={{0,12},{4,8},{8,4},{12,0},{16,28},{20,24},{24,20},{28,16},{1,13},{... | collective-permute-start | bytes 196616 | tf_op jit(solution)/shard_map/ppermute | solution.py:674
  28.7 1.2 %collective-permute-start.5 = (bf16[2,128,128]{2,1,0:T(8,128)(2,1)S(1)}, bf16[2,128,128]{2,1,0:T(8,128)(2,1)S(1)}, u32[]{:S(2)}, u32[]{:S(2)}) collective-permute-start(bf16[2,128,128]{2,1,0:T(8,128)(2,1)S(1)} %get-tuple-element.79), channel_id=1, source_target_pairs={{0,4},{4,0},{8,12},{12,8},{16,20},{20,16},{24,28},{28,24},{1,5},{5... | collective-permute-start | bytes 196616 | tf_op jit(solution)/shard_map/ppermute | solution.py:674
  29.9 0.0 collective-permute-start.6
  29.9 2.5 %keep_part.1 = (f32[256,2048]{1,0:T(8,128)S(1)}, f32[256,768]{1,0:T(8,128)S(1)}, bf16[768,2048]{1,0:T(8,128)(2,1)S(1)}) custom-call(s32[1]{0:T(128)} %bitcast.2.code_ref, bf16[512,1024]{1,0:T(8,128)(2,1)} %z_hbm.3, bf16[1024,2048]{1,0:T(8,128)(2,1)} %w_hbm.3, f32[1,128]{1,0:T(1,128)} %bitcast.8, bf16[256,1024]{1,0:T(8,128)(2,1)S(1)} %get-tuple-element.71.refs_1_.out, ...), custom_call_target="tpu_custom_call" | custom-call | flops 268435456 | bytes 1048576 | tf_op jit(solution)/shard_map/keep_part/pallas_call | solution.py:287
  32.4 0.0 collective-permute-done.4.refs_0_
  32.4 0.6 %collective-permute-done.5.refs_1_ = bf16[2,128,128]{2,1,0:T(8,128)(2,1)S(1)} collective-permute-done((bf16[2,128,128]{2,1,0:T(8,128)(2,1)S(1)}, bf16[2,128,128]{2,1,0:T(8,128)(2,1)S(1)}, u32[]{:S(2)}, u32[]{:S(2)}) %collective-permute-start.5) | collective-permute-done | bytes 65568 | tf_op jit(solution)/shard_map/ppermute | solution.py:674
  33.0 1.2 %collective-permute-done.6.refs_2_ = bf16[2,128,128]{2,1,0:T(8,128)(2,1)S(1)} collective-permute-done((bf16[2,128,128]{2,1,0:T(8,128)(2,1)S(1)}, bf16[2,128,128]{2,1,0:T(8,128)(2,1)S(1)}, u32[]{:S(2)}, u32[]{:S(2)}) %collective-permute-start.6) | collective-permute-done | bytes 65568 | tf_op jit(solution)/shard_map/ppermute | solution.py:674
  34.2 1.4 %away_part.1 = (bf16[128,2048]{1,0:T(8,128)(2,1)S(1)}, f32[128,2048]{1,0:T(8,128)S(1)}) custom-call(s32[1]{0:T(128)} %bitcast.2.code_ref, f32[256,2048]{1,0:T(8,128)S(1)} %get-tuple-element.75.sum_ref, f32[256,768]{1,0:T(8,128)S(1)} %get-tuple-element.76.gate, bf16[768,2048]{1,0:T(8,128)(2,1)S(1)} %get-tuple-element.77.w, ...), custom_call_target="tpu_custom_call" | custom-call | flops 805306368 | bytes 1048576 | tf_op jit(solution)/shard_map/away_part/pallas_call | solution.py:287
  35.5 0.1 collective-permute-start.7
  35.6 1.9 %collective-permute-done.7 = bf16[128,2048]{1,0:T(8,128)(2,1)S(1)} collective-permute-done((bf16[128,2048]{1,0:T(8,128)(2,1)S(1)}, bf16[128,2048]{1,0:T(8,128)(2,1)S(1)}, u32[]{:S(2)}, u32[]{:S(2)}) %collective-permute-start.7) | collective-permute-done | bytes 524320 | tf_op jit(solution)/shard_map/ppermute | solution.py:681
  37.5 0.1 add_convert_fusion.1
  37.6 1.6 %collective-permute-start.10 = (bf16[128,2048]{1,0:T(8,128)(2,1)S(1)}, bf16[128,2048]{1,0:T(8,128)(2,1)S(1)}, u32[]{:S(2)}, u32[]{:S(2)}) collective-permute-start(bf16[128,2048]{1,0:T(8,128)(2,1)S(1)} %add_convert_fusion.1), channel_id=1, source_target_pairs={{0,2},{1,3},{2,0},{3,1},{4,6},{5,7},{6,4},{7,5},{8,10},{9,11},{10,... | collective-permute-start | bytes 1572872 | tf_op jit(solution)/shard_map/ppermute | solution.py:682
  39.2 2.8 %third_part.3 = (bf16[256,1024]{1,0:T(8,128)(2,1)S(1)}, bf16[256,1024]{1,0:T(8,128)(2,1)S(1)}) custom-call(s32[1]{0:T(128)} %bitcast.3.code_ref, bf16[512,512]{1,0:T(8,128)(2,1)} %refs_0_.1, bf16[512,512]{1,0:T(8,128)(2,1)} %refs_1_.1, bf16[3,2,2,384,256]{4,3,2,1,0:T(8,128)(2,1)} %get-tuple-element.84.refs_2_, f32[16,512]{1,0:T(8,128)} %get-tuple-element.85.refs_3_, ...), custom_call_target="tpu_custom_call" | custom-call | flops 3000000000 | bytes 1048576 | tf_op jit(solution)/shard_map/third_part/pallas_call | solution.py:287
  42.0 3.8 %whole_part.1 = (bf16[128,1024]{1,0:T(8,128)(2,1)S(1)}, bf16[128,1024]{1,0:T(8,128)(2,1)S(1)}, f32[128,2048]{1,0:T(8,128)S(1)}) custom-call(s32[1]{0:T(128)} %bitcast.3.code_ref, bf16[512,1024]{1,0:T(8,128)(2,1)} %z_hbm.3, bf16[1024,2048]{1,0:T(8,128)(2,1)} %w_hbm.3, f32[1,128]{1,0:T(1,128)} %bitcast.9, bf16[256,1024]{1,0:T(8,128)(2,1)S(1)} %get-tuple-element.86.out, ...), custom_call_target="tpu_custom_call" | custom-call | flops 1073741824 | bytes 1048576 | tf_op jit(solution)/shard_map/whole_part/pallas_call | solution.py:287
  45.8 0.1 collective-permute-start.8
  45.9 0.5 collective-permute-start.9
  46.4 1.0 %collective-permute-done.8 = bf16[128,1024]{1,0:T(8,128)(2,1)S(1)} collective-permute-done((bf16[128,1024]{1,0:T(8,128)(2,1)S(1)}, bf16[128,1024]{1,0:T(8,128)(2,1)S(1)}, u32[]{:S(2)}, u32[]{:S(2)}) %collective-permute-start.8) | collective-permute-done | bytes 262176 | tf_op jit(solution)/shard_map/ppermute | solution.py:689
  47.4 0.4 collective-permute-done.9
  47.8 3.8 %collective-permute-done.10 = bf16[128,2048]{1,0:T(8,128)(2,1)S(1)} collective-permute-done((bf16[128,2048]{1,0:T(8,128)(2,1)S(1)}, bf16[128,2048]{1,0:T(8,128)(2,1)S(1)}, u32[]{:S(2)}, u32[]{:S(2)}) %collective-permute-start.10) | collective-permute-done | bytes 524320 | tf_op jit(solution)/shard_map/ppermute | solution.py:682
  51.6 1.0 %add_convert_fusion = bf16[128,2048]{1,0:T(8,128)(2,1)} fusion(bf16[128,2048]{1,0:T(8,128)(2,1)S(1)} %collective-permute-done.10, f32[128,2048]{1,0:T(8,128)S(1)} %get-tuple-element.88, bf16[128,1024]{1,0:T(8,128)(2,1)S(1)} %collective-permute-done.9, bf16[128,1024]{1,0:T(8,128)(2,1)S(1)} %collective-permute-done.8), kind=kLoop, calls=%fused_computation | loop fusion | flops 2097152 | bytes 2621440 | tf_op jit(solution)/shard_map/convert_element_type | solution.py:692
Async XLA Ops:
  8.1 8.9 %collective-permute-start = (bf16[2,128,256]{2,1,0:T(8,128)(2,1)S(1)}, bf16[2,128,256]{2,1,0:T(8,128)(2,1)S(1)}, u32[]{:S(2)}, u32[]{:S(2)}) collective-permute-start(bf16[2,128,256]{2,1,0:T(8,128)(2,1)S(1)} %get-tuple-element.67), channel_id=1, source_target_pairs={{0,12},{4,8},{8,4},{12,0},{16,28},{20,24},{24,20},{28,16},{1,13},{... | collective-permute-start | bytes 393224 | tf_op jit(solution)/shard_map/ppermute | solution.py:659
  12.1 6.3 %collective-permute-start.1 = (bf16[2,128,256]{2,1,0:T(8,128)(2,1)S(1)}, bf16[2,128,256]{2,1,0:T(8,128)(2,1)S(1)}, u32[]{:S(2)}, u32[]{:S(2)}) collective-permute-start(bf16[2,128,256]{2,1,0:T(8,128)(2,1)S(1)} %get-tuple-element.68), channel_id=1, source_target_pairs={{0,4},{4,0},{8,12},{12,8},{16,20},{20,16},{24,28},{28,24},{1,5},{5... | collective-permute-start | bytes 393224 | tf_op jit(solution)/shard_map/ppermute | solution.py:659
  12.6 6.0 %collective-permute-start.2 = (bf16[2,128,256]{2,1,0:T(8,128)(2,1)S(1)}, bf16[2,128,256]{2,1,0:T(8,128)(2,1)S(1)}, u32[]{:S(2)}, u32[]{:S(2)}) collective-permute-start(bf16[2,128,256]{2,1,0:T(8,128)(2,1)S(1)} %get-tuple-element.69), channel_id=1, source_target_pairs={{0,8},{4,12},{8,0},{12,4},{16,24},{20,28},{24,16},{28,20},{1,9},{5... | collective-permute-start | bytes 393224 | tf_op jit(solution)/shard_map/ppermute | solution.py:659
  19.1 4.7 %copy-start = (bf16[2,128,128]{2,1,0:T(8,128)(2,1)}, bf16[2,128,128]{2,1,0:T(8,128)(2,1)S(1)}, u32[]{:S(2)}) copy-start(bf16[2,128,128]{2,1,0:T(8,128)(2,1)S(1)} %get-tuple-element.70.refs_6_) | copy-start | bytes 196612
  19.1 6.4 %collective-permute-start.3 = (bf16[2,128,128]{2,1,0:T(8,128)(2,1)S(1)}, bf16[2,128,128]{2,1,0:T(8,128)(2,1)S(1)}, u32[]{:S(2)}, u32[]{:S(2)}) collective-permute-start(bf16[2,128,128]{2,1,0:T(8,128)(2,1)S(1)} %get-tuple-element.70.refs_6_), channel_id=1, source_target_pairs={{0,16},{4,20},{8,24},{12,28},{1,17},{5,21},{9,25},{13,29},{2,18},{... | collective-permute-start | bytes 196616 | tf_op jit(solution)/shard_map/ppermute | solution.py:670
  25.9 6.4 %collective-permute-start.4 = (bf16[2,128,128]{2,1,0:T(8,128)(2,1)S(1)}, bf16[2,128,128]{2,1,0:T(8,128)(2,1)S(1)}, u32[]{:S(2)}, u32[]{:S(2)}) collective-permute-start(bf16[2,128,128]{2,1,0:T(8,128)(2,1)S(1)} %get-tuple-element.78), channel_id=1, source_target_pairs={{0,12},{4,8},{8,4},{12,0},{16,28},{20,24},{24,20},{28,16},{1,13},{... | collective-permute-start | bytes 196616 | tf_op jit(solution)/shard_map/ppermute | solution.py:674
  28.7 4.3 %collective-permute-start.5 = (bf16[2,128,128]{2,1,0:T(8,128)(2,1)S(1)}, bf16[2,128,128]{2,1,0:T(8,128)(2,1)S(1)}, u32[]{:S(2)}, u32[]{:S(2)}) collective-permute-start(bf16[2,128,128]{2,1,0:T(8,128)(2,1)S(1)} %get-tuple-element.79), channel_id=1, source_target_pairs={{0,4},{4,0},{8,12},{12,8},{16,20},{20,16},{24,28},{28,24},{1,5},{5... | collective-permute-start | bytes 196616 | tf_op jit(solution)/shard_map/ppermute | solution.py:674
  29.9 4.3 %collective-permute-start.6 = (bf16[2,128,128]{2,1,0:T(8,128)(2,1)S(1)}, bf16[2,128,128]{2,1,0:T(8,128)(2,1)S(1)}, u32[]{:S(2)}, u32[]{:S(2)}) collective-permute-start(bf16[2,128,128]{2,1,0:T(8,128)(2,1)S(1)} %get-tuple-element.80), channel_id=1, source_target_pairs={{0,8},{4,12},{8,0},{12,4},{16,24},{20,28},{24,16},{28,20},{1,9},{5... | collective-permute-start | bytes 196616 | tf_op jit(solution)/shard_map/ppermute | solution.py:674
  35.5 2.0 %collective-permute-start.7 = (bf16[128,2048]{1,0:T(8,128)(2,1)S(1)}, bf16[128,2048]{1,0:T(8,128)(2,1)S(1)}, u32[]{:S(2)}, u32[]{:S(2)}) collective-permute-start(bf16[128,2048]{1,0:T(8,128)(2,1)S(1)} %get-tuple-element.82), channel_id=1, source_target_pairs={{0,1},{1,0},{2,3},{3,2},{4,5},{5,4},{6,7},{7,6},{8,9},{9,8},{10,11... | collective-permute-start | bytes 1572872 | tf_op jit(solution)/shard_map/ppermute | solution.py:681
  37.6 14.0 %collective-permute-start.10 = (bf16[128,2048]{1,0:T(8,128)(2,1)S(1)}, bf16[128,2048]{1,0:T(8,128)(2,1)S(1)}, u32[]{:S(2)}, u32[]{:S(2)}) collective-permute-start(bf16[128,2048]{1,0:T(8,128)(2,1)S(1)} %add_convert_fusion.1), channel_id=1, source_target_pairs={{0,2},{1,3},{2,0},{3,1},{4,6},{5,7},{6,4},{7,5},{8,10},{9,11},{10,... | collective-permute-start | bytes 1572872 | tf_op jit(solution)/shard_map/ppermute | solution.py:682
  45.8 1.6 %collective-permute-start.8 = (bf16[128,1024]{1,0:T(8,128)(2,1)S(1)}, bf16[128,1024]{1,0:T(8,128)(2,1)S(1)}, u32[]{:S(2)}, u32[]{:S(2)}) collective-permute-start(bf16[128,1024]{1,0:T(8,128)(2,1)S(1)} %get-tuple-element.89), channel_id=1, source_target_pairs={{0,1},{1,0},{2,3},{3,2},{4,5},{5,4},{6,7},{7,6},{8,9},{9,8},{10,11... | collective-permute-start | bytes 786440 | tf_op jit(solution)/shard_map/ppermute | solution.py:689
  45.9 1.9 %collective-permute-start.9 = (bf16[128,1024]{1,0:T(8,128)(2,1)S(1)}, bf16[128,1024]{1,0:T(8,128)(2,1)S(1)}, u32[]{:S(2)}, u32[]{:S(2)}) collective-permute-start(bf16[128,1024]{1,0:T(8,128)(2,1)S(1)} %get-tuple-element.90), channel_id=1, source_target_pairs={{0,1},{1,0},{2,3},{3,2},{4,5},{5,4},{6,7},{7,6},{8,9},{9,8},{10,11... | collective-permute-start | bytes 786440 | tf_op jit(solution)/shard_map/ppermute | solution.py:689

commit v8 on v7

--- a/solution.py
+++ b/solution.py
@@ -426,39 +426,48 @@
     return call(kernel, "third_part", groups, outs, scratch, OUTPUT_VMEM, 3 * 10**9)
 
 
-def in_order(member_ref, turns, own_ref, other_refs, order_ref):
-    order_ref[member_ref[0]] = own_ref[...]
+def in_order(member, turns, own_ref, other_refs, order_ref):
+    order_ref[member] = own_ref[...]
     for turn, ref in zip(turns, other_refs):
-        order_ref[jnp.bitwise_xor(member_ref[0], turn)] = ref[...]
+        order_ref[jnp.bitwise_xor(member, turn)] = ref[...]
 
 
 def after_shard(ends, state):
     return mm(ends[:, DV:], state.astype(BF16)) + ends[:, :DV].astype(F32)
 
 
-def group_part(member, turns, own, others, chained):
+def group_part(code, turns, own, others, chained):
     count = len(turns) + 1
 
-    def kernel(member_ref, own_ref, *refs):
+    def kernel(code_ref, own_ref, *refs):
         other_refs, (order, ending_ref, *total_refs) = refs[: count - 1], refs[count - 1 :]
-        in_order(member_ref, turns, own_ref, other_refs, order)
-        states = [order[0, h][:, :DV].astype(F32) for h in range(2)]
-        for i in range(1, count):
-            states = [after_shard(order[i, h], states[h]) for h in range(2)]
-        for h in range(2):
-            ending_ref[h] = states[h].astype(BF16)
-        for total_ref in total_refs:
+        in_order(jnp.bitwise_and(code_ref[0], count - 1), turns, own_ref, other_refs, order)
+
+        @pl.when(code_ref[0] < count)
+        def _():
+            states = [order[0, h][:, :DV].astype(F32) for h in range(2)]
+            for i in range(1, count):
+                states = [after_shard(order[i, h], states[h]) for h in range(2)]
             for h in range(2):
-                transit = order[0, h][:, DV:]
-                for i in range(1, count):
-                    transit = mm(order[i, h][:, DV:], transit).astype(BF16)
-                total_ref[h] = jnp.concatenate([states[h].astype(BF16), transit], axis=1)
+                ending_ref[h] = states[h].astype(BF16)
+            for total_ref in total_refs:
+                for h in range(2):
+                    transit = order[0, h][:, DV:]
+                    for i in range(1, count):
+                        transit = mm(order[i, h][:, DV:], transit).astype(BF16)
+                    total_ref[h] = jnp.concatenate([states[h].astype(BF16), transit], axis=1)
+
+        @pl.when(code_ref[0] >= count)
+        def _():
+            ending_ref[...] = jnp.zeros_like(ending_ref)
+            for total_ref in total_refs:
+                total_ref[...] = jnp.zeros_like(total_ref)
 
     vmem = pltpu.MemorySpace.VMEM
     outs = [(vmem, (count, *own.shape), BF16), (vmem, (2, DK, DV), BF16)]
     if chained:
         outs.append((vmem, own.shape, BF16))
-    groups = [(pltpu.SMEM, [member]), (pltpu.VMEM, [own, *others])]
+    groups = [(pltpu.SMEM, [code]), (pltpu.VMEM, [own, *others])]
     return call(kernel, "group_part", groups, outs, [], SMALL_VMEM, 10**8)
 
 
@@ -654,11 +663,12 @@
     chunks = 1 if apart else query.shape[0] // CHUNK
     code = (member_at + members * lax.rem(chip + 1, chips)).reshape(1) if apart else member
     spot = spots[1] if apart else place_code(0, core, member_at, members)
-    code, member, spot, *spots = lax.optimization_barrier((code, member, spot, *spots))
+    last = (member_at + members * (seq >= shards - members).astype(jnp.int32)).reshape(1)
+    code, member, last, spot, *spots = lax.optimization_barrier((code, member, last, spot, *spots))
     away, earlier, operands = first_part(code, turns, rate, keys, values, gate_logit.T, beta_logit.T)
     others = [lax.ppermute(a, "seq", pairs[turn]) for a, turn in zip(away, turns)]
     own, mine, locals_, near = second_part(code, chunks, operands, earlier, query, keys)
-    order, ending, *total = group_part(member, turns, own, others, groups > 2)
+    order, ending, *total = group_part(last, turns, own, others, groups > 2)
     out, gain = third_part(spot, turns, chunks, near, True, mine, ending)
 
     came = []

time: 52.8 us -> 52.4 us (level)
  no operation moved by 1% of the time
where the time goes in v8:
time: 52.4 us; the launch traced here: 52.2 us
  Pallas kernels  25 us (48%)
  starting transfers between devices  15.1 us (29%)
  waiting for transfers between devices  10.9 us (21%)
  other arithmetic  1.09 us (2%)
    pallas_call x9, Pallas kernels, call(): pl.pallas_call(kernel, in_specs=specs, out_specs=[pl.BlockSpec(memory_spa...  25 us
    ppermute x3, starting transfers between devices, on_device(): lax.ppermute(a, 'seq', pairs[turn])  4.69 us
    ppermute x1, starting transfers between devices, on_device(): came.append(lax.ppermute(ending, 'seq', along))  4.26 us
    ppermute x3, starting transfers between devices, on_device(): lax.ppermute(g, 'seq', pairs[turn])  3.97 us
    ppermute x1, waiting for transfers between devices, on_device(): lax.ppermute(both, 'head', [(i, (i + 2 * by) % cores) for i in range(core...  3.84 us
    ppermute x1, waiting for transfers between devices, on_device(): both = (stay + lax.ppermute(give, 'head', swap).astype(F32)).astype(BF16)  1.9 us
    ppermute x3, waiting for transfers between devices, on_device(): lax.ppermute(g, 'seq', pairs[turn])  1.78 us
    ppermute x3, waiting for transfers between devices, on_device(): lax.ppermute(a, 'seq', pairs[turn])  1.6 us
  transfers between devices with their start and end apart: 11, of which 9 were waited for; matrix products, arithmetic and copies ran while one was open for 0% of the time, Pallas kernels for 28%

profile of v8, /device:TPU:0, one launch (start us, length us, event | category | flops | bytes accessed | tf_op | source)
XLA Modules:
  0.0 52.2 jit_solution(2964535782816026953)
XLA Ops:
  0.0 8.0 %first_part.1 = (bf16[2,128,256]{2,1,0:T(8,128)(2,1)S(1)}, bf16[2,128,256]{2,1,0:T(8,128)(2,1)S(1)}, bf16[2,128,256]{2,1,0:T(8,128)(2,1)S(1)}, bf16[3,2,2,384,25...) custom-call(s32[1]{0:T(128)} %bitcast.code_ref, ...), custom_call_target="tpu_custom_call" | custom-call | flops 6000000000 | bytes 1048576 | tf_op jit(solution)/shard_map/first_part/pallas_call | solution.py:287
  8.1 4.0 %collective-permute-start = (bf16[2,128,256]{2,1,0:T(8,128)(2,1)S(1)}, bf16[2,128,256]{2,1,0:T(8,128)(2,1)S(1)}, u32[]{:S(2)}, u32[]{:S(2)}) collective-permute-start(bf16[2,128,256]{2,1,0:T(8,128)(2,1)S(1)} %get-tuple-element.68), channel_id=1, source_target_pairs={{0,12},{4,8},{8,4},{12,0},{16,28},{20,24},{24,20},{28,16},{1,13},{... | collective-permute-start | bytes 393224 | tf_op jit(solution)/shard_map/ppermute | solution.py:669
  12.1 0.5 collective-permute-start.1
  12.6 0.1 collective-permute-start.2
  12.7 4.2 %second_part.1 = (bf16[2,128,256]{2,1,0:T(8,128)(2,1)S(1)}, bf16[1,2,2,384,256]{4,3,2,1,0:T(8,128)(2,1)S(1)}, f32[16,512]{1,0:T(8,128)S(1)}, bf16[3,2,2,384,256]...) custom-call(s32[1]{0:T(128)} %bitcast.code_ref, ...), custom_call_target="tpu_custom_call" | custom-call | flops 2000000000 | bytes 1048576 | tf_op jit(solution)/shard_map/second_part/pallas_call | solution.py:287
  17.0 0.0 collective-permute-done.refs_0_
  17.0 1.4 %collective-permute-done.1.refs_1_ = bf16[2,128,256]{2,1,0:T(8,128)(2,1)S(1)} collective-permute-done((bf16[2,128,256]{2,1,0:T(8,128)(2,1)S(1)}, bf16[2,128,256]{2,1,0:T(8,128)(2,1)S(1)}, u32[]{:S(2)}, u32[]{:S(2)}) %collective-permute-start.1) | collective-permute-done | bytes 131104 | tf_op jit(solution)/shard_map/ppermute | solution.py:669
  18.4 0.2 collective-permute-done.2.refs_2_
  18.6 0.5 group_part.1
  19.1 0.0 copy-start
  19.1 4.3 %collective-permute-start.3 = (bf16[2,128,128]{2,1,0:T(8,128)(2,1)S(1)}, bf16[2,128,128]{2,1,0:T(8,128)(2,1)S(1)}, u32[]{:S(2)}, u32[]{:S(2)}) collective-permute-start(bf16[2,128,128]{2,1,0:T(8,128)(2,1)S(1)} %get-tuple-element.71.refs_6_), channel_id=1, source_target_pairs={{0,16},{4,20},{8,24},{12,28},{1,17},{5,21},{9,25},{13,29},{2,18},{... | collective-permute-start | bytes 196616 | tf_op jit(solution)/shard_map/ppermute | solution.py:680
  23.3 0.0 copy-done
  23.3 1.3 %third_part.2 = (bf16[256,1024]{1,0:T(8,128)(2,1)S(1)}, bf16[256,1024]{1,0:T(8,128)(2,1)S(1)}) custom-call(s32[1]{0:T(128)} %bitcast.3.code_ref, bf16[256,512]{1,0:T(8,128)(2,1)S(1)} %get-tuple-element.60.refs_0_, bf16[256,512]{1,0:T(8,128)(2,1)S(1)} %get-tuple-element.61.refs_1_, bf16[3,1,2,384,256]{4,3,2,1,0:T(8,128)(2,1)S(1)} %get-tuple-element.62.refs_2_, ...), custom_call_target="tpu_custom_call" | custom-call | flops 3000000000 | bytes 1048576 | tf_op jit(solution)/shard_map/third_part/pallas_call | solution.py:287
  24.7 0.4 collective-permute-done.3.refs_0_
  25.0 0.5 starts_part.1
  25.5 2.8 %collective-permute-start.4 = (bf16[2,128,128]{2,1,0:T(8,128)(2,1)S(1)}, bf16[2,128,128]{2,1,0:T(8,128)(2,1)S(1)}, u32[]{:S(2)}, u32[]{:S(2)}) collective-permute-start(bf16[2,128,128]{2,1,0:T(8,128)(2,1)S(1)} %get-tuple-element.80), channel_id=1, source_target_pairs={{0,12},{4,8},{8,4},{12,0},{16,28},{20,24},{24,20},{28,16},{1,13},{... | collective-permute-start | bytes 196616 | tf_op jit(solution)/shard_map/ppermute | solution.py:684
  28.3 1.2 %collective-permute-start.5 = (bf16[2,128,128]{2,1,0:T(8,128)(2,1)S(1)}, bf16[2,128,128]{2,1,0:T(8,128)(2,1)S(1)}, u32[]{:S(2)}, u32[]{:S(2)}) collective-permute-start(bf16[2,128,128]{2,1,0:T(8,128)(2,1)S(1)} %get-tuple-element.81), channel_id=1, source_target_pairs={{0,4},{4,0},{8,12},{12,8},{16,20},{20,16},{24,28},{28,24},{1,5},{5... | collective-permute-start | bytes 196616 | tf_op jit(solution)/shard_map/ppermute | solution.py:684
  29.5 0.0 collective-permute-start.6
  29.5 2.5 %keep_part.1 = (f32[256,2048]{1,0:T(8,128)S(1)}, f32[256,768]{1,0:T(8,128)S(1)}, bf16[768,2048]{1,0:T(8,128)(2,1)S(1)}) custom-call(s32[1]{0:T(128)} %bitcast.3.code_ref, bf16[512,1024]{1,0:T(8,128)(2,1)} %z_hbm.3, bf16[1024,2048]{1,0:T(8,128)(2,1)} %w_hbm.3, f32[1,128]{1,0:T(1,128)} %bitcast.9, bf16[256,1024]{1,0:T(8,128)(2,1)S(1)} %get-tuple-element.72.refs_1_.out, ...), custom_call_target="tpu_custom_call" | custom-call | flops 268435456 | bytes 1048576 | tf_op jit(solution)/shard_map/keep_part/pallas_call | solution.py:287
  32.0 0.0 collective-permute-done.4.refs_0_
  32.0 0.6 %collective-permute-done.5.refs_1_ = bf16[2,128,128]{2,1,0:T(8,128)(2,1)S(1)} collective-permute-done((bf16[2,128,128]{2,1,0:T(8,128)(2,1)S(1)}, bf16[2,128,128]{2,1,0:T(8,128)(2,1)S(1)}, u32[]{:S(2)}, u32[]{:S(2)}) %collective-permute-start.5) | collective-permute-done | bytes 65568 | tf_op jit(solution)/shard_map/ppermute | solution.py:684
  32.6 1.2 %collective-permute-done.6.refs_2_ = bf16[2,128,128]{2,1,0:T(8,128)(2,1)S(1)} collective-permute-done((bf16[2,128,128]{2,1,0:T(8,128)(2,1)S(1)}, bf16[2,128,128]{2,1,0:T(8,128)(2,1)S(1)}, u32[]{:S(2)}, u32[]{:S(2)}) %collective-permute-start.6) | collective-permute-done | bytes 65568 | tf_op jit(solution)/shard_map/ppermute | solution.py:684
  33.7 1.4 %away_part.1 = (bf16[128,2048]{1,0:T(8,128)(2,1)S(1)}, f32[128,2048]{1,0:T(8,128)S(1)}) custom-call(s32[1]{0:T(128)} %bitcast.3.code_ref, f32[256,2048]{1,0:T(8,128)S(1)} %get-tuple-element.77.sum_ref, f32[256,768]{1,0:T(8,128)S(1)} %get-tuple-element.78.gate, bf16[768,2048]{1,0:T(8,128)(2,1)S(1)} %get-tuple-element.79.w, ...), custom_call_target="tpu_custom_call" | custom-call | flops 805306368 | bytes 1048576 | tf_op jit(solution)/shard_map/away_part/pallas_call | solution.py:287
  35.1 0.1 collective-permute-start.7
  35.2 1.9 %collective-permute-done.7 = bf16[128,2048]{1,0:T(8,128)(2,1)S(1)} collective-permute-done((bf16[128,2048]{1,0:T(8,128)(2,1)S(1)}, bf16[128,2048]{1,0:T(8,128)(2,1)S(1)}, u32[]{:S(2)}, u32[]{:S(2)}) %collective-permute-start.7) | collective-permute-done | bytes 524320 | tf_op jit(solution)/shard_map/ppermute | solution.py:691
  37.1 0.1 add_convert_fusion.1
  37.2 1.6 %collective-permute-start.10 = (bf16[128,2048]{1,0:T(8,128)(2,1)S(1)}, bf16[128,2048]{1,0:T(8,128)(2,1)S(1)}, u32[]{:S(2)}, u32[]{:S(2)}) collective-permute-start(bf16[128,2048]{1,0:T(8,128)(2,1)S(1)} %add_convert_fusion.1), channel_id=1, source_target_pairs={{0,2},{1,3},{2,0},{3,1},{4,6},{5,7},{6,4},{7,5},{8,10},{9,11},{10,... | collective-permute-start | bytes 1572872 | tf_op jit(solution)/shard_map/ppermute | solution.py:692
  38.7 2.8 %third_part.3 = (bf16[256,1024]{1,0:T(8,128)(2,1)S(1)}, bf16[256,1024]{1,0:T(8,128)(2,1)S(1)}) custom-call(s32[1]{0:T(128)} %bitcast.4.code_ref, bf16[512,512]{1,0:T(8,128)(2,1)} %refs_0_.1, bf16[512,512]{1,0:T(8,128)(2,1)} %refs_1_.1, bf16[3,2,2,384,256]{4,3,2,1,0:T(8,128)(2,1)} %get-tuple-element.86.refs_2_, f32[16,512]{1,0:T(8,128)} %get-tuple-element.87.refs_3_, ...), custom_call_target="tpu_custom_call" | custom-call | flops 3000000000 | bytes 1048576 | tf_op jit(solution)/shard_map/third_part/pallas_call | solution.py:287
  41.6 3.8 %whole_part.1 = (bf16[128,1024]{1,0:T(8,128)(2,1)S(1)}, bf16[128,1024]{1,0:T(8,128)(2,1)S(1)}, f32[128,2048]{1,0:T(8,128)S(1)}) custom-call(s32[1]{0:T(128)} %bitcast.4.code_ref, bf16[512,1024]{1,0:T(8,128)(2,1)} %z_hbm.3, bf16[1024,2048]{1,0:T(8,128)(2,1)} %w_hbm.3, f32[1,128]{1,0:T(1,128)} %bitcast.10, bf16[256,1024]{1,0:T(8,128)(2,1)S(1)} %get-tuple-element.88.out, ...), custom_call_target="tpu_custom_call" | custom-call | flops 1073741824 | bytes 1048576 | tf_op jit(solution)/shard_map/whole_part/pallas_call | solution.py:287
  45.4 0.1 collective-permute-start.8
  45.5 0.5 collective-permute-start.9
  46.0 1.0 %collective-permute-done.8 = bf16[128,1024]{1,0:T(8,128)(2,1)S(1)} collective-permute-done((bf16[128,1024]{1,0:T(8,128)(2,1)S(1)}, bf16[128,1024]{1,0:T(8,128)(2,1)S(1)}, u32[]{:S(2)}, u32[]{:S(2)}) %collective-permute-start.8) | collective-permute-done | bytes 262176 | tf_op jit(solution)/shard_map/ppermute | solution.py:699
  47.0 0.4 collective-permute-done.9
  47.4 3.8 %collective-permute-done.10 = bf16[128,2048]{1,0:T(8,128)(2,1)S(1)} collective-permute-done((bf16[128,2048]{1,0:T(8,128)(2,1)S(1)}, bf16[128,2048]{1,0:T(8,128)(2,1)S(1)}, u32[]{:S(2)}, u32[]{:S(2)}) %collective-permute-start.10) | collective-permute-done | bytes 524320 | tf_op jit(solution)/shard_map/ppermute | solution.py:692
  51.2 1.0 %add_convert_fusion = bf16[128,2048]{1,0:T(8,128)(2,1)} fusion(bf16[128,2048]{1,0:T(8,128)(2,1)S(1)} %collective-permute-done.10, f32[128,2048]{1,0:T(8,128)S(1)} %get-tuple-element.90, bf16[128,1024]{1,0:T(8,128)(2,1)S(1)} %collective-permute-done.9, bf16[128,1024]{1,0:T(8,128)(2,1)S(1)} %collective-permute-done.8), kind=kLoop, calls=%fused_computation | loop fusion | flops 2097152 | bytes 2621440 | tf_op jit(solution)/shard_map/convert_element_type | solution.py:702
Async XLA Ops:
  8.1 8.9 %collective-permute-start = (bf16[2,128,256]{2,1,0:T(8,128)(2,1)S(1)}, bf16[2,128,256]{2,1,0:T(8,128)(2,1)S(1)}, u32[]{:S(2)}, u32[]{:S(2)}) collective-permute-start(bf16[2,128,256]{2,1,0:T(8,128)(2,1)S(1)} %get-tuple-element.68), channel_id=1, source_target_pairs={{0,12},{4,8},{8,4},{12,0},{16,28},{20,24},{24,20},{28,16},{1,13},{... | collective-permute-start | bytes 393224 | tf_op jit(solution)/shard_map/ppermute | solution.py:669
  12.1 6.3 %collective-permute-start.1 = (bf16[2,128,256]{2,1,0:T(8,128)(2,1)S(1)}, bf16[2,128,256]{2,1,0:T(8,128)(2,1)S(1)}, u32[]{:S(2)}, u32[]{:S(2)}) collective-permute-start(bf16[2,128,256]{2,1,0:T(8,128)(2,1)S(1)} %get-tuple-element.69), channel_id=1, source_target_pairs={{0,4},{4,0},{8,12},{12,8},{16,20},{20,16},{24,28},{28,24},{1,5},{5... | collective-permute-start | bytes 393224 | tf_op jit(solution)/shard_map/ppermute | solution.py:669
  12.6 6.0 %collective-permute-start.2 = (bf16[2,128,256]{2,1,0:T(8,128)(2,1)S(1)}, bf16[2,128,256]{2,1,0:T(8,128)(2,1)S(1)}, u32[]{:S(2)}, u32[]{:S(2)}) collective-permute-start(bf16[2,128,256]{2,1,0:T(8,128)(2,1)S(1)} %get-tuple-element.70), channel_id=1, source_target_pairs={{0,8},{4,12},{8,0},{12,4},{16,24},{20,28},{24,16},{28,20},{1,9},{5... | collective-permute-start | bytes 393224 | tf_op jit(solution)/shard_map/ppermute | solution.py:669
  19.1 4.3 %copy-start = (bf16[2,128,128]{2,1,0:T(8,128)(2,1)}, bf16[2,128,128]{2,1,0:T(8,128)(2,1)S(1)}, u32[]{:S(2)}) copy-start(bf16[2,128,128]{2,1,0:T(8,128)(2,1)S(1)} %get-tuple-element.71.refs_6_) | copy-start | bytes 196612
  19.1 6.0 %collective-permute-start.3 = (bf16[2,128,128]{2,1,0:T(8,128)(2,1)S(1)}, bf16[2,128,128]{2,1,0:T(8,128)(2,1)S(1)}, u32[]{:S(2)}, u32[]{:S(2)}) collective-permute-start(bf16[2,128,128]{2,1,0:T(8,128)(2,1)S(1)} %get-tuple-element.71.refs_6_), channel_id=1, source_target_pairs={{0,16},{4,20},{8,24},{12,28},{1,17},{5,21},{9,25},{13,29},{2,18},{... | collective-permute-start | bytes 196616 | tf_op jit(solution)/shard_map/ppermute | solution.py:680
  25.5 6.4 %collective-permute-start.4 = (bf16[2,128,128]{2,1,0:T(8,128)(2,1)S(1)}, bf16[2,128,128]{2,1,0:T(8,128)(2,1)S(1)}, u32[]{:S(2)}, u32[]{:S(2)}) collective-permute-start(bf16[2,128,128]{2,1,0:T(8,128)(2,1)S(1)} %get-tuple-element.80), channel_id=1, source_target_pairs={{0,12},{4,8},{8,4},{12,0},{16,28},{20,24},{24,20},{28,16},{1,13},{... | collective-permute-start | bytes 196616 | tf_op jit(solution)/shard_map/ppermute | solution.py:684
  28.3 4.3 %collective-permute-start.5 = (bf16[2,128,128]{2,1,0:T(8,128)(2,1)S(1)}, bf16[2,128,128]{2,1,0:T(8,128)(2,1)S(1)}, u32[]{:S(2)}, u32[]{:S(2)}) collective-permute-start(bf16[2,128,128]{2,1,0:T(8,128)(2,1)S(1)} %get-tuple-element.81), channel_id=1, source_target_pairs={{0,4},{4,0},{8,12},{12,8},{16,20},{20,16},{24,28},{28,24},{1,5},{5... | collective-permute-start | bytes 196616 | tf_op jit(solution)/shard_map/ppermute | solution.py:684
  29.5 4.3 %collective-permute-start.6 = (bf16[2,128,128]{2,1,0:T(8,128)(2,1)S(1)}, bf16[2,128,128]{2,1,0:T(8,128)(2,1)S(1)}, u32[]{:S(2)}, u32[]{:S(2)}) collective-permute-start(bf16[2,128,128]{2,1,0:T(8,128)(2,1)S(1)} %get-tuple-element.82), channel_id=1, source_target_pairs={{0,8},{4,12},{8,0},{12,4},{16,24},{20,28},{24,16},{28,20},{1,9},{5... | collective-permute-start | bytes 196616 | tf_op jit(solution)/shard_map/ppermute | solution.py:684
  35.1 2.0 %collective-permute-start.7 = (bf16[128,2048]{1,0:T(8,128)(2,1)S(1)}, bf16[128,2048]{1,0:T(8,128)(2,1)S(1)}, u32[]{:S(2)}, u32[]{:S(2)}) collective-permute-start(bf16[128,2048]{1,0:T(8,128)(2,1)S(1)} %get-tuple-element.84), channel_id=1, source_target_pairs={{0,1},{1,0},{2,3},{3,2},{4,5},{5,4},{6,7},{7,6},{8,9},{9,8},{10,11... | collective-permute-start | bytes 1572872 | tf_op jit(solution)/shard_map/ppermute | solution.py:691
  37.2 14.0 %collective-permute-start.10 = (bf16[128,2048]{1,0:T(8,128)(2,1)S(1)}, bf16[128,2048]{1,0:T(8,128)(2,1)S(1)}, u32[]{:S(2)}, u32[]{:S(2)}) collective-permute-start(bf16[128,2048]{1,0:T(8,128)(2,1)S(1)} %add_convert_fusion.1), channel_id=1, source_target_pairs={{0,2},{1,3},{2,0},{3,1},{4,6},{5,7},{6,4},{7,5},{8,10},{9,11},{10,... | collective-permute-start | bytes 1572872 | tf_op jit(solution)/shard_map/ppermute | solution.py:692
  45.4 1.6 %collective-permute-start.8 = (bf16[128,1024]{1,0:T(8,128)(2,1)S(1)}, bf16[128,1024]{1,0:T(8,128)(2,1)S(1)}, u32[]{:S(2)}, u32[]{:S(2)}) collective-permute-start(bf16[128,1024]{1,0:T(8,128)(2,1)S(1)} %get-tuple-element.91), channel_id=1, source_target_pairs={{0,1},{1,0},{2,3},{3,2},{4,5},{5,4},{6,7},{7,6},{8,9},{9,8},{10,11... | collective-permute-start | bytes 786440 | tf_op jit(solution)/shard_map/ppermute | solution.py:699
  45.5 1.9 %collective-permute-start.9 = (bf16[128,1024]{1,0:T(8,128)(2,1)S(1)}, bf16[128,1024]{1,0:T(8,128)(2,1)S(1)}, u32[]{:S(2)}, u32[]{:S(2)}) collective-permute-start(bf16[128,1024]{1,0:T(8,128)(2,1)S(1)} %get-tuple-element.92), channel_id=1, source_target_pairs={{0,1},{1,0},{2,3},{3,2},{4,5},{5,4},{6,7},{7,6},{8,9},{9,8},{10,11... | collective-permute-start | bytes 786440 | tf_op jit(solution)/shard_map/ppermute | solution.py:699
